TPU v7x, 128 devices: a whole 4x4x4 slice. The times are simulated.
128 devices in a mesh: section: 4 (over z), dp: 4 (over x), seq: 8 (over y, core).
Axes of the slice: x: 4, y: 4, z: 4, core: 2. Of those that a mesh axis runs over, the one named last changes fastest.
Arguments:
- block_input: bfloat16 [8, 1024, 1280], P('dp', 'seq', 'section'), may hold values from -6 to 6
- cotangent: bfloat16 [8, 1024, 1280], P('dp', 'seq', 'section'), may hold values from -6 to 6
- cell_lengths: int32 [8, 5], replicated, may hold values from 1 to 1020, as said below
- norm_attn_gain: bfloat16 [4, 1280], P('section', ('dp', 'seq')), may hold values from 0.5 to 1.5
- norm_attn_bias: bfloat16 [4, 1280], P('section', ('dp', 'seq')), may hold values from -1 to 1
- w_qkv: bfloat16 [4, 1280, 3840], P('section', ('dp', 'seq')), may hold values from -0.15625 to 0.15625
- w_out: bfloat16 [4, 1280, 1280], P('section', ('dp', 'seq')), may hold values from -1.25 to 1.25
- norm_ffn_gain: bfloat16 [4, 1280], P('section', ('dp', 'seq')), may hold values from 0.5 to 1.5
- norm_ffn_bias: bfloat16 [4, 1280], P('section', ('dp', 'seq')), may hold values from -1 to 1
- w_up: bfloat16 [4, 1280, 5120], P('section', ('dp', 'seq')), may hold values from -0.15625 to 0.15625
- w_down: bfloat16 [4, 5120, 1280], P('section', ('dp', 'seq')), may hold values from -0.078125 to 0.078125
Outputs:
- block_output: bfloat16 [8, 1024, 1280], P('dp', 'seq', 'section')
- input_grad: float32 [8, 1024, 1280], P('dp', 'seq', 'section')
- grad_norm_attn_gain: float32 [4, 1280], P('section', ('dp', 'seq'))
- grad_norm_attn_bias: float32 [4, 1280], P('section', ('dp', 'seq'))
- grad_w_qkv: float32 [4, 1280, 3840], P('section', ('dp', 'seq'))
- grad_w_out: float32 [4, 1280, 1280], P('section', ('dp', 'seq'))
- grad_norm_ffn_gain: float32 [4, 1280], P('section', ('dp', 'seq'))
- grad_norm_ffn_bias: float32 [4, 1280], P('section', ('dp', 'seq'))
- grad_w_up: float32 [4, 1280, 5120], P('section', ('dp', 'seq'))
- grad_w_down: float32 [4, 5120, 1280], P('section', ('dp', 'seq'))
Inputs may be any that keep to these rules, and one draw needn't show every extreme that they name: `cell_lengths`: each micro-batch's 5 cell lengths, in packed order, sum to 1024. Among the 2 micro-batches of each index of dp, one holds a cell of 1020 rows.
All inputs are finite; a program needn't handle non-finite values.
Results may differ from a plain program's by a relative error of at most 0.025.
Values may be sent and summed in bfloat16 or wider, within the bound.
No kernel may reach another device: no remote copies, remote signals or barrier semaphores. Data moves between devices by JAX's collectives and lax.ppermute only.
A program may use at most 448 MiB of HBM per device.

v0:
```python
import jax
import jax.numpy as jnp
from jax import lax
from jax.sharding import PartitionSpec as P

HEAD_DIM = 64


EPSILON = 1e-05
MASKED = -1e30


def passed_along(value, axis, steps):
    count = lax.axis_size(axis)
    leading, last = (max(0, -steps), min(count, count - steps))
    return lax.ppermute(value, axis, [(source, source + steps) for source in range(leading, last)])


def for_sending(shard):

    def short(part):
        return part.astype(jnp.bfloat16) if part.dtype == jnp.float32 else part

    return jax.tree.map(short, shard)


def layer_norm(values, gain_row, bias_row):
    centered = values - jnp.mean(values, axis=-1, keepdims=True)
    spread = jnp.mean(centered * centered, axis=-1, keepdims=True)
    return centered * lax.rsqrt(spread + EPSILON) * gain_row + bias_row


def gelu_exact(values):
    return jax.nn.gelu(values, approximate=False)


def guarded(active, compute, shape):
    return lax.cond(active, compute, lambda: jnp.zeros(shape, jnp.float32))


def segment_ids(lengths, length_total):
    bounds = jnp.cumsum(lengths)
    places = jnp.arange(length_total, dtype=jnp.int32)
    return jnp.sum((places[:, None] >= bounds[None, :]).astype(jnp.int32), axis=1)


def split_heads(matrix):
    return matrix.reshape(matrix.shape[:-1] + (matrix.shape[-1] // HEAD_DIM, HEAD_DIM))


def summed_product(left, right, active):
    return guarded(
        active,
        lambda: jnp.dot(left, right, preferred_element_type=jnp.float32),
        (left.shape[0], right.shape[1]),
    )


def soft_weights(queries_low, keys_all, query_segments, key_segments, active):
    scaling = HEAD_DIM ** (-0.5)
    query_heads = split_heads(queries_low)
    key_heads = split_heads(keys_all)
    shape = (query_heads.shape[0], query_heads.shape[2], query_heads.shape[1], key_heads.shape[1])
    scores = (
        guarded(
            active,
            lambda: jnp.einsum(
                "gqhd,gkhd->ghqk", query_heads, key_heads, preferred_element_type=jnp.float32
            ),
            shape,
        )
        * scaling
    )
    allowed = query_segments[:, :, None] == key_segments[:, None, :]
    scores = jnp.where(allowed[:, None], scores, MASKED)
    return jax.nn.softmax(scores, axis=-1)


def forward_layer(hidden_in, weights, query_segments, key_segments, active):
    gain_attn, bias_attn, mat_qkv, mat_out, gain_ffn, bias_ffn, mat_up, mat_down = weights
    rows_here = hidden_in.shape[0]
    local_width = mat_out.shape[0]
    normed_low = layer_norm(hidden_in, gain_attn, bias_attn).astype(jnp.bfloat16)
    group = normed_low.shape[0] // rows_here
    qkv_low = guarded(
        active,
        lambda: jnp.dot(normed_low, mat_qkv, preferred_element_type=jnp.float32),
        (normed_low.shape[0], mat_qkv.shape[1]),
    ).astype(jnp.bfloat16)
    qkv_groups = qkv_low.reshape(group, rows_here, 3 * local_width)
    keys_all, values_all = (
        lax.all_gather(qkv_groups[:, :, local_width : 2 * local_width], "seq", axis=1, tiled=True),
        lax.all_gather(qkv_groups[:, :, 2 * local_width :], "seq", axis=1, tiled=True),
    )
    soft_probs = soft_weights(
        qkv_groups[:, :, :local_width], keys_all, query_segments, key_segments, active
    )
    probs_low = soft_probs.astype(jnp.bfloat16)
    value_heads = split_heads(values_all)
    attended = guarded(
        active,
        lambda: jnp.einsum(
            "ghqk,gkhd->gqhd", probs_low, value_heads, preferred_element_type=jnp.float32
        ),
        (group, rows_here, local_width // HEAD_DIM, HEAD_DIM),
    )
    attended_low = attended.reshape(group * rows_here, local_width).astype(jnp.bfloat16)
    hidden_mid = hidden_in + summed_product(attended_low, mat_out, active)
    normed_ffn_low = layer_norm(hidden_mid, gain_ffn, bias_ffn).astype(jnp.bfloat16)
    upward = guarded(
        active,
        lambda: jnp.dot(normed_ffn_low, mat_up, preferred_element_type=jnp.float32),
        (normed_ffn_low.shape[0], mat_up.shape[1]),
    )
    active_low = gelu_exact(upward).astype(jnp.bfloat16)
    hidden_out = hidden_mid + summed_product(active_low, mat_down, active)
    kept_values = (
        normed_low,
        qkv_groups,
        keys_all,
        values_all,
        soft_probs,
        probs_low,
        attended_low,
        hidden_mid,
        normed_ffn_low,
        upward,
        active_low,
    )
    return (hidden_out.astype(jnp.bfloat16), kept_values)


def backward_layer(hidden_in, weights, kept_values, grad_out, active):
    gain_attn, bias_attn, mat_qkv, mat_out, gain_ffn, bias_ffn, mat_up, mat_down = weights
    (
        normed_wide,
        qkv_groups,
        keys_all,
        values_all,
        soft_probs,
        probs_low,
        attended_low,
        hidden_mid,
        normed_ffn_wide,
        upward,
        active_low,
    ) = kept_values
    rows_here = hidden_in.shape[0]
    local_width = mat_out.shape[0]
    group = qkv_groups.shape[0]
    heads_here = local_width // HEAD_DIM
    grad_out_wide = grad_out.astype(jnp.bfloat16)
    grad_down = guarded(
        active,
        lambda: jnp.dot(active_low.T, grad_out_wide, preferred_element_type=jnp.float32),
        (active_low.shape[1], grad_out_wide.shape[1]),
    )
    grad_active = guarded(
        active,
        lambda: jnp.dot(grad_out_wide, mat_down.T, preferred_element_type=jnp.float32),
        (grad_out_wide.shape[0], mat_down.shape[0]),
    )
    grad_upward_low = jax.vjp(gelu_exact, upward)[1](grad_active)[0].astype(jnp.bfloat16)
    grad_up = guarded(
        active,
        lambda: jnp.dot(normed_ffn_wide.T, grad_upward_low, preferred_element_type=jnp.float32),
        (normed_ffn_wide.shape[1], grad_upward_low.shape[1]),
    )
    grad_normed_ffn = summed_product(grad_upward_low, mat_up.T, active)
    grad_mid_part, grad_gain_ffn, grad_bias_ffn = jax.vjp(
        layer_norm, hidden_mid, gain_ffn, bias_ffn
    )[1](grad_normed_ffn)
    grad_mid = grad_out + grad_mid_part
    grad_mid_wide = grad_mid.astype(jnp.bfloat16)
    grad_outproj = guarded(
        active,
        lambda: jnp.dot(attended_low.T, grad_mid_wide, preferred_element_type=jnp.float32),
        (attended_low.shape[1], grad_mid_wide.shape[1]),
    )
    grad_attended_low = guarded(
        active,
        lambda: jnp.dot(grad_mid_wide, mat_out.T, preferred_element_type=jnp.float32),
        (grad_mid_wide.shape[0], mat_out.shape[0]),
    ).astype(jnp.bfloat16)
    grad_heads = split_heads(grad_attended_low.reshape(group, rows_here, local_width))
    query_heads = split_heads(qkv_groups[:, :, :local_width])
    key_heads = split_heads(keys_all)
    value_heads = split_heads(values_all)
    scaling = HEAD_DIM ** (-0.5)
    grad_probs = guarded(
        active,
        lambda: jnp.einsum(
            "gqhd,gkhd->ghqk", grad_heads, value_heads, preferred_element_type=jnp.float32
        ),
        soft_probs.shape,
    )
    row_terms = jnp.sum(grad_probs * soft_probs, axis=-1, keepdims=True)
    grad_scores_low = (soft_probs * (grad_probs - row_terms)).astype(jnp.bfloat16)
    grad_queries = (
        guarded(
            active,
            lambda: jnp.einsum(
                "ghqk,gkhd->gqhd", grad_scores_low, key_heads, preferred_element_type=jnp.float32
            ),
            (group, rows_here, heads_here, HEAD_DIM),
        )
        * scaling
    )
    shape = (rows_here * lax.axis_size("seq"), group, heads_here, HEAD_DIM)
    grad_keys = (
        guarded(
            active,
            lambda: jnp.einsum(
                "ghqk,gqhd->kghd", grad_scores_low, query_heads, preferred_element_type=jnp.float32
            ),
            shape,
        )
        * scaling
    )
    grad_values = guarded(
        active,
        lambda: jnp.einsum(
            "ghqk,gqhd->kghd", probs_low, grad_heads, preferred_element_type=jnp.float32
        ),
        shape,
    )
    grad_pairs = jnp.swapaxes(
        lax.psum_scatter(
            jnp.concatenate(
                [
                    grad_keys.reshape(rows_here * lax.axis_size("seq"), group, local_width),
                    grad_values.reshape(rows_here * lax.axis_size("seq"), group, local_width),
                ],
                axis=2,
            ).astype(jnp.bfloat16),
            "seq",
            scatter_dimension=0,
            tiled=True,
        ).astype(jnp.float32),
        0,
        1,
    )
    grad_qkv_groups = jnp.concatenate(
        [grad_queries.reshape(group, rows_here, local_width), grad_pairs], axis=2
    ).astype(jnp.bfloat16)
    grad_qkv_low = grad_qkv_groups.reshape(group * rows_here, 3 * local_width)
    grad_qkv = guarded(
        active,
        lambda: jnp.dot(normed_wide.T, grad_qkv_low, preferred_element_type=jnp.float32),
        (normed_wide.shape[1], grad_qkv_low.shape[1]),
    )
    grad_normed_attn = summed_product(grad_qkv_low, mat_qkv.T, active)
    grad_in_part, grad_gain_attn, grad_bias_attn = jax.vjp(
        layer_norm, hidden_in, gain_attn, bias_attn
    )[1](grad_normed_attn)
    grad_in = grad_mid + grad_in_part
    return (
        grad_in,
        (
            grad_gain_attn,
            grad_bias_attn,
            grad_qkv,
            grad_outproj,
            grad_gain_ffn,
            grad_bias_ffn,
            grad_up,
            grad_down,
        ),
    )


def unpack(gathered):
    return tuple(
        (member[0].astype(jnp.float32) if member.ndim == 2 else member[0] for member in gathered)
    )


def local(
    block_input,
    cotangent,
    cell_lengths,
    norm_attn_gain,
    norm_attn_bias,
    w_qkv,
    w_out,
    norm_ffn_gain,
    norm_ffn_bias,
    w_up,
    w_down,
):
    sections = lax.axis_size("section")
    section_index = lax.axis_index("section")
    seq_index = lax.axis_index("seq")
    dp_count = lax.axis_size("dp")
    seq_count = lax.axis_size("seq")
    micro_count = block_input.shape[0]
    rows_here = block_input.shape[1]
    rows_total = rows_here * seq_count
    whole_input, whole_cot = (
        lax.all_gather(block_input, "section", axis=2, tiled=True),
        lax.all_gather(cotangent, "section", axis=2, tiled=True),
    )
    model_width = whole_input.shape[2]
    packed = (
        norm_attn_gain,
        norm_attn_bias,
        w_qkv,
        w_out,
        norm_ffn_gain,
        norm_ffn_bias,
        w_up,
        w_down,
    )
    all_segments = jax.vmap(lambda lengths: segment_ids(lengths, rows_total))(cell_lengths).reshape(
        dp_count, micro_count, rows_total
    )
    weights = unpack(
        (
            lax.all_gather(packed[0], ("dp", "seq"), axis=1, tiled=True),
            lax.all_gather(packed[1], ("dp", "seq"), axis=1, tiled=True),
            lax.all_gather(packed[2], ("dp", "seq"), axis=1, tiled=True),
            lax.all_gather(packed[3], ("dp", "seq"), axis=1, tiled=True),
            lax.all_gather(packed[4], ("dp", "seq"), axis=1, tiled=True),
            lax.all_gather(packed[5], ("dp", "seq"), axis=1, tiled=True),
            lax.all_gather(packed[6], ("dp", "seq"), axis=1, tiled=True),
            lax.all_gather(packed[7], ("dp", "seq"), axis=1, tiled=True),
        )
    )
    own_segments = lax.dynamic_index_in_dim(all_segments, lax.axis_index("dp"), 0, keepdims=False)
    group_segments = own_segments[:, None, :]
    tick_total = micro_count + sections - 1

    def group_rows(micro_slot):
        key_segments = group_segments[micro_slot]
        query_segments = lax.dynamic_slice_in_dim(key_segments, seq_index * rows_here, rows_here, 1)
        return (query_segments, key_segments)

    def forward_tick(step_index, loop_state):
        received, kept_inputs, finished = loop_state
        micro_index = step_index - section_index
        active = (micro_index >= 0) & (micro_index < micro_count)
        micro_slot = jnp.clip(micro_index, 0, micro_count - 1)
        incoming = jnp.where(section_index == 0, whole_input[micro_slot], received)
        query_segments, key_segments = group_rows(micro_slot)
        computed = forward_layer(
            incoming.astype(jnp.float32), weights, query_segments, key_segments, active
        )[0]
        hidden_out = jnp.where(active, computed, jnp.zeros_like(computed))
        kept_inputs = kept_inputs.at[micro_slot].set(
            jnp.where(active, incoming, kept_inputs[micro_slot])
        )
        last_active = active & (section_index == sections - 1)
        finished = finished.at[micro_slot].set(
            jnp.where(last_active, hidden_out, finished[micro_slot])
        )
        received = passed_along(hidden_out, "section", 1)
        return (received, kept_inputs, finished)

    empty_rows = jnp.zeros((rows_here, model_width), jnp.bfloat16)
    empty_batch = jnp.zeros((micro_count, rows_here, model_width), jnp.bfloat16)
    forward_state = lax.fori_loop(
        0, tick_total, forward_tick, (empty_rows, empty_batch, empty_batch)
    )
    kept_inputs, finished = (forward_state[1], forward_state[2])

    def backward_tick(step_index, loop_state):
        received_grad, totals, input_grads = loop_state
        micro_index = step_index - (sections - 1 - section_index)
        active = (micro_index >= 0) & (micro_index < micro_count)
        micro_slot = jnp.clip(micro_index, 0, micro_count - 1)
        arriving = jnp.where(
            section_index == sections - 1, whole_cot[micro_slot], received_grad
        ).astype(jnp.float32)
        query_segments, key_segments = group_rows(micro_slot)
        hidden_in = kept_inputs[micro_slot].astype(jnp.float32)
        kept_values = forward_layer(hidden_in, weights, query_segments, key_segments, active)[1]
        computed_grad, computed_layer = backward_layer(
            hidden_in, weights, kept_values, arriving, active
        )
        grad_in = jnp.where(active, computed_grad, jnp.zeros_like(computed_grad))
        totals = tuple(
            (
                running + jnp.where(active, addend, jnp.zeros_like(addend))
                for running, addend in zip(totals, computed_layer)
            )
        )
        first_active = active & (section_index == 0)
        input_grads = input_grads.at[micro_slot].set(
            jnp.where(first_active, grad_in, input_grads[micro_slot])
        )
        received_grad = passed_along(grad_in.astype(jnp.bfloat16), "section", -1)
        return (received_grad, totals, input_grads)

    grad_start = tuple((jnp.zeros(member.shape, jnp.float32) for member in weights))
    backward_state = lax.fori_loop(
        0,
        tick_total,
        backward_tick,
        (empty_rows, grad_start, jnp.zeros((micro_count, rows_here, model_width), jnp.float32)),
    )
    totals, input_grads = (backward_state[1], backward_state[2])
    output_part, input_part = (
        lax.psum_scatter(
            finished.astype(jnp.float32).astype(jnp.bfloat16),
            "section",
            scatter_dimension=2,
            tiled=True,
        ).astype(jnp.float32),
        lax.psum_scatter(
            input_grads.astype(jnp.bfloat16), "section", scatter_dimension=2, tiled=True
        ).astype(jnp.float32),
    )
    reduced = jax.tree.map(
        lambda part: part.astype(jnp.float32),
        lax.psum_scatter(
            for_sending(tuple((running[None] for running in totals))),
            ("dp", "seq"),
            scatter_dimension=1,
            tiled=True,
        ),
    )
    return (
        output_part.astype(jnp.bfloat16),
        input_part,
        reduced[0],
        reduced[1],
        reduced[2],
        reduced[3],
        reduced[4],
        reduced[5],
        reduced[6],
        reduced[7],
    )


def solution(mesh):
    return jax.shard_map(
        local,
        mesh=mesh,
        in_specs=(
            P("dp", "seq", "section"),
            P("dp", "seq", "section"),
            P(),
            P("section", ("dp", "seq")),
            P("section", ("dp", "seq")),
            P("section", ("dp", "seq"), None),
            P("section", ("dp", "seq"), None),
            P("section", ("dp", "seq")),
            P("section", ("dp", "seq")),
            P("section", ("dp", "seq"), None),
            P("section", ("dp", "seq"), None),
        ),
        out_specs=(
            P("dp", "seq", "section"),
            P("dp", "seq", "section"),
            P("section", ("dp", "seq")),
            P("section", ("dp", "seq")),
            P("section", ("dp", "seq"), None),
            P("section", ("dp", "seq"), None),
            P("section", ("dp", "seq")),
            P("section", ("dp", "seq")),
            P("section", ("dp", "seq"), None),
            P("section", ("dp", "seq"), None),
        ),
        check_vma=False,
    )
```

profile of v0, /device:TPU:23, one launch (start us, length us, event | category | flops | bytes accessed | tf_op | source)
XLA Modules:
  0.0 2865.7 jit_solution(4420735299422028929)
XLA Ops:
  16.4 120.4 %all-reduce.9 = (bf16[1280]{0:T(1024)(128)(2,1)S(1)}, bf16[1280]{0:T(1024)(128)(2,1)S(1)}, bf16[1280]{0:T(1024)(128)(2,1)S(1)}, bf16[1280]{0:T(1024)(128)(2,1)S(1)}) all-reduce(bf16[1280]{0:T(1024)(128)(2,1)S(1)} %dynamic-update-slice.33, ...), channel_id=1, replica_groups=mesh['section'=4,'dp'=4,'seq'=8] {'dp','seq'}, use_global_device_ids=true, to_apply=%add | all-reduce | flops 5120 | bytes 20480
  181.1 17.8 copy.102
  198.9 47.5 %all-gather.15.cloned.1.call-done = bf16[1,5120,1280]{2,1,0:T(8,128)(2,1)} async-done(((bf16[1,160,1280]{2,1,0:T(8,128)(2,1)}), bf16[1,5120,1280]{2,1,0:T(8,128)(2,1)}) %all-gather.15.cloned.1.call-update) | async-done | bytes 13107216 | tf_op jit(solution)/shard_map/all_gather | solution.py:326
  248.1 580.3 %while.58 = (s32[]{:T(128)}, bf16[128,1280]{1,0:T(8,128)(2,1)}, bf16[2,128,1280]{2,1,0:T(8,128)(2,1)}, bf16[2,128,1280]{1,2,0:T(8,128)(2,1)S(1)}, s32[]{:T(128)}...) while((s32[]{:T(128)}, bf16[128,1280]{1,0:T(8,128)(2,1)}, ...), condition=%wide.region_22.23_spmd, body=%wide.region_2.22_spmd.sunk | while | flops 5784660992 | bytes 208698192 | solution.py:361
  263.8 24.9 all-gather.19.cloned.1.call-done
  379.3 27.3 all-gather.19.cloned.1.call-done
  493.7 33.3 %all-gather.19.cloned.1.call-done = bf16[1,1024,1280]{1,2,0:T(8,128)(2,1)} async-done(((bf16[1,128,1280]{1,2,0:T(8,128)(2,1)}), bf16[1,1024,1280]{1,2,0:T(8,128)(2,1)}) %all-gather.19.cloned.1.call-update) | async-done | bytes 2621456 | tf_op jit(solution)/shard_map/while/body/eval_jaxpr/all_gather | solution.py:92
  575.6 21.9 collective-permute-start
  613.9 34.6 %all-gather.19.cloned.1.call-done = bf16[1,1024,1280]{1,2,0:T(8,128)(2,1)} async-done(((bf16[1,128,1280]{1,2,0:T(8,128)(2,1)}), bf16[1,1024,1280]{1,2,0:T(8,128)(2,1)}) %all-gather.19.cloned.1.call-update) | async-done | bytes 2621456 | tf_op jit(solution)/shard_map/while/body/eval_jaxpr/all_gather | solution.py:92
  717.4 52.4 %all-gather.19.cloned.1.call-done = bf16[1,1024,1280]{1,2,0:T(8,128)(2,1)} async-done(((bf16[1,128,1280]{1,2,0:T(8,128)(2,1)}), bf16[1,1024,1280]{1,2,0:T(8,128)(2,1)}) %all-gather.19.cloned.1.call-update) | async-done | bytes 2621456 | tf_op jit(solution)/shard_map/while/body/eval_jaxpr/all_gather | solution.py:92
  829.2 1581.9 %while.59 = (s32[]{:T(128)}, bf16[128,1280]{1,0:T(8,128)(2,1)S(1)}, f32[1280]{0:T(1024)}, f32[1280]{0:T(1024)}, f32[1280,3840]{1,0:T(8,128)}, /*index=5*/f32[128...) while((s32[]{:T(128)}, bf16[128,1280]{1,0:T(8,128)(2,1)S(1)}, ...), condition=%wide.region_76.77_spmd.clone, body=%wide.region_24.76_spmd.clone.sunk | while | flops 15639482368 | bytes 876230528 | solution.py:395
  840.6 48.2 %all-gather.23.cloned.1.call-done = bf16[1,1024,1280]{2,1,0:T(8,128)(2,1)} async-done(((bf16[1,128,1280]{2,1,0:T(8,128)(2,1)}), bf16[1,1024,1280]{2,1,0:T(8,128)(2,1)}) %all-gather.23.cloned.1.call-update) | async-done | bytes 2621456 | tf_op jit(solution)/shard_map/while/body/eval_jaxpr/all_gather | solution.py:92
  1044.7 22.1 reduce-scatter.28.cloned.1.call-done
  1103.5 80.5 %all-gather.23.cloned.1.call-done = bf16[1,1024,1280]{2,1,0:T(8,128)(2,1)} async-done(((bf16[1,128,1280]{2,1,0:T(8,128)(2,1)}), bf16[1,1024,1280]{2,1,0:T(8,128)(2,1)}) %all-gather.23.cloned.1.call-update) | async-done | bytes 2621456 | tf_op jit(solution)/shard_map/while/body/eval_jaxpr/all_gather | solution.py:92
  1323.1 21.2 select_add_fusion.18
  1344.3 18.5 select_add_fusion.19
  1407.8 93.9 %all-gather.23.cloned.1.call-done = bf16[1,1024,1280]{2,1,0:T(8,128)(2,1)} async-done(((bf16[1,128,1280]{2,1,0:T(8,128)(2,1)}), bf16[1,1024,1280]{2,1,0:T(8,128)(2,1)}) %all-gather.23.cloned.1.call-update) | async-done | bytes 2621456 | tf_op jit(solution)/shard_map/while/body/eval_jaxpr/all_gather | solution.py:92
  1640.9 21.2 select_add_fusion.18
  1662.1 18.5 select_add_fusion.19
  1713.8 42.8 %collective-permute-done.1 = bf16[128,1280]{1,0:T(8,128)(2,1)S(1)} collective-permute-done((bf16[128,1280]{1,0:T(8,128)(2,1)}, bf16[128,1280]{1,0:T(8,128)(2,1)S(1)}, u32[]{:S(2)}, u32[]{:S(2)}) %collective-permute-start.1) | collective-permute-done | bytes 327712 | tf_op jit(solution)/shard_map/while/body/eval_jaxpr/ppermute | solution.py:16
  1784.1 33.5 %all-gather.23.cloned.1.call-done = bf16[1,1024,1280]{2,1,0:T(8,128)(2,1)} async-done(((bf16[1,128,1280]{2,1,0:T(8,128)(2,1)}), bf16[1,1024,1280]{2,1,0:T(8,128)(2,1)}) %all-gather.23.cloned.1.call-update) | async-done | bytes 2621456 | tf_op jit(solution)/shard_map/while/body/eval_jaxpr/all_gather | solution.py:92
  1995.3 26.8 select_add_fusion.18
  2022.1 26.6 select_add_fusion.19
  2073.1 20.7 select_add_fusion.15
  2309.3 26.8 select_add_fusion.18
  2336.0 26.6 select_add_fusion.19
  2387.3 20.7 select_add_fusion.15
  2459.1 119.5 %all-reduce.8 = (bf16[1,1280]{1,0:T(2,128)(2,1)S(1)}, bf16[1,1280]{1,0:T(2,128)(2,1)S(1)}, bf16[1,1280]{1,0:T(2,128)(2,1)S(1)}, bf16[1,1280]{1,0:T(2,128)(2,1)S(1)}) all-reduce(bf16[1,1280]{1,0:T(2,128)(2,1)S(1)} %convert_element_type.457, ...), channel_id=5, replica_groups=mesh['section'=4,'dp'=4,'seq'=8] {'dp','seq'}, use_global_device_ids=true, to_apply=%region_78.79.clone | all-reduce | flops 5120 | bytes 20480
  2583.0 31.3 %reduce-scatter.20.cloned.1.call-done = bf16[1,40,3840]{2,1,0:T(8,128)(2,1)} async-done(((bf16[1,1280,3840]{2,1,0:T(8,128)(2,1)}), bf16[1,40,3840]{2,1,0:T(8,128)(2,1)}) %reduce-scatter.20.cloned.1.call-update) | async-done | bytes 307216 | tf_op jit(solution)/shard_map/reduce_scatter | solution.py:415
  2616.2 107.1 %reduce-scatter.26.cloned.1.call-done = bf16[1,160,1280]{2,1,0:T(8,128)(2,1)} async-done(((bf16[1,5120,1280]{2,1,0:T(8,128)(2,1)}), bf16[1,160,1280]{2,1,0:T(8,128)(2,1)}) %reduce-scatter.26.cloned.1.call-update) | async-done | bytes 409616 | tf_op jit(solution)/shard_map/reduce_scatter | solution.py:415
  2725.2 107.4 %reduce-scatter.24.cloned.1.call-done = bf16[1,40,5120]{2,1,0:T(8,128)(2,1)} async-done(((bf16[1,1280,5120]{2,1,0:T(8,128)(2,1)}), bf16[1,40,5120]{2,1,0:T(8,128)(2,1)}) %reduce-scatter.24.cloned.1.call-update) | async-done | bytes 409616 | tf_op jit(solution)/shard_map/reduce_scatter | solution.py:415
  2834.6 24.4 reduce-scatter.16.cloned.1.call-done
  (1305 shorter events, 1997.0 us)
Async XLA Ops:
  7.2 160.2 %all-gather.9.cloned.1.call-start = ((), (), s32[]{:S(2)}) async-start(), calls=%async_computation.7 | async-start | bytes 10137600 | tf_op jit(solution)/shard_map/all_gather | solution.py:321
  7.9 173.2 %all-gather.13.cloned.1.call-start = ((), (), s32[]{:S(2)}) async-start(), calls=%async_computation.9 | async-start | bytes 13516800 | tf_op jit(solution)/shard_map/all_gather | solution.py:325
  8.7 190.2 %all-gather.11.cloned.1.call-start = ((), (), s32[]{:S(2)}) async-start(), calls=%async_computation.8 | async-start | bytes 3379200 | tf_op jit(solution)/shard_map/all_gather | solution.py:322
  9.4 237.0 %all-gather.15.cloned.1.call-start = ((), (), s32[]{:S(2)}) async-start(), calls=%async_computation.10 | async-start | bytes 13516800 | tf_op jit(solution)/shard_map/all_gather | solution.py:326
  260.6 60.0 %all-gather.17.cloned.1.call-start = ((), (), s32[]{:S(2)}) async-start(), calls=%async_computation.17 | async-start | bytes 2949120 | tf_op jit(solution)/shard_map/while/body/eval_jaxpr/all_gather | solution.py:93
  376.0 62.7 %all-gather.17.cloned.1.call-start = ((), (), s32[]{:S(2)}) async-start(), calls=%async_computation.17 | async-start | bytes 2949120 | tf_op jit(solution)/shard_map/while/body/eval_jaxpr/all_gather | solution.py:93
  490.5 68.5 %all-gather.17.cloned.1.call-start = ((), (), s32[]{:S(2)}) async-start(), calls=%async_computation.17 | async-start | bytes 2949120 | tf_op jit(solution)/shard_map/while/body/eval_jaxpr/all_gather | solution.py:93
  603.6 44.8 %all-gather.19.cloned.1.call-start = ((), (), s32[]{:S(2)}) async-start(), calls=%async_computation.18 | async-start | bytes 2949120 | tf_op jit(solution)/shard_map/while/body/eval_jaxpr/all_gather | solution.py:92
  610.7 69.7 %all-gather.17.cloned.1.call-start = ((), (), s32[]{:S(2)}) async-start(), calls=%async_computation.17 | async-start | bytes 2949120 | tf_op jit(solution)/shard_map/while/body/eval_jaxpr/all_gather | solution.py:93
  707.1 62.6 %all-gather.19.cloned.1.call-start = ((), (), s32[]{:S(2)}) async-start(), calls=%async_computation.18 | async-start | bytes 2949120 | tf_op jit(solution)/shard_map/while/body/eval_jaxpr/all_gather | solution.py:92
  714.2 87.5 %all-gather.17.cloned.1.call-start = ((), (), s32[]{:S(2)}) async-start(), calls=%async_computation.17 | async-start | bytes 2949120 | tf_op jit(solution)/shard_map/while/body/eval_jaxpr/all_gather | solution.py:93
  829.7 59.2 %all-gather.23.cloned.1.call-start = ((), (), s32[]{:S(2)}) async-start(), calls=%async_computation.20 | async-start | bytes 2949120 | tf_op jit(solution)/shard_map/while/body/eval_jaxpr/all_gather | solution.py:92
  835.3 81.8 %all-gather.21.cloned.1.call-start = ((), (), s32[]{:S(2)}) async-start(), calls=%async_computation.19 | async-start | bytes 2949120 | tf_op jit(solution)/shard_map/while/body/eval_jaxpr/all_gather | solution.py:93
  835.9 230.9 %reduce-scatter.28.cloned.1.call-start = ((), (), s32[]{:S(2)}) async-start(), calls=%async_computation.21 | async-start | bytes 5898240 | tf_op jit(solution)/shard_map/while
  1092.4 91.6 %all-gather.23.cloned.1.call-start = ((), (), s32[]{:S(2)}) async-start(), calls=%async_computation.20 | async-start | bytes 2949120 | tf_op jit(solution)/shard_map/while/body/eval_jaxpr/all_gather | solution.py:92
  1098.0 114.4 %all-gather.21.cloned.1.call-start = ((), (), s32[]{:S(2)}) async-start(), calls=%async_computation.19 | async-start | bytes 2949120 | tf_op jit(solution)/shard_map/while/body/eval_jaxpr/all_gather | solution.py:93
  1098.8 264.0 %reduce-scatter.28.cloned.1.call-start = ((), (), s32[]{:S(2)}) async-start(), calls=%async_computation.21 | async-start | bytes 5898240 | tf_op jit(solution)/shard_map/while
  1396.7 105.0 %all-gather.23.cloned.1.call-start = ((), (), s32[]{:S(2)}) async-start(), calls=%async_computation.20 | async-start | bytes 2949120 | tf_op jit(solution)/shard_map/while/body/eval_jaxpr/all_gather | solution.py:92
  1402.3 127.7 %all-gather.21.cloned.1.call-start = ((), (), s32[]{:S(2)}) async-start(), calls=%async_computation.19 | async-start | bytes 2949120 | tf_op jit(solution)/shard_map/while/body/eval_jaxpr/all_gather | solution.py:93
  1403.1 277.5 %reduce-scatter.28.cloned.1.call-start = ((), (), s32[]{:S(2)}) async-start(), calls=%async_computation.21 | async-start | bytes 5898240 | tf_op jit(solution)/shard_map/while
  1688.3 68.3 %collective-permute-start.1 = (bf16[128,1280]{1,0:T(8,128)(2,1)}, bf16[128,1280]{1,0:T(8,128)(2,1)S(1)}, u32[]{:S(2)}, u32[]{:S(2)}) collective-permute-start(bf16[128,1280]{1,0:T(8,128)(2,1)} %get-tuple-element.2299), channel_id=1, source_target_pairs={{32,0},{64,32},{96,64},{33,1},{65,33},{97,65},{34,2},{66,34},{98,6... | collective-permute-start | bytes 983048 | tf_op jit(solution)/shard_map/while/body/eval_jaxpr/ppermute | solution.py:16
  1757.1 60.6 %all-gather.23.cloned.1.call-start = ((), (), s32[]{:S(2)}) async-start(), calls=%async_computation.20 | async-start | bytes 2949120 | tf_op jit(solution)/shard_map/while/body/eval_jaxpr/all_gather | solution.py:92
  1769.8 76.3 %all-gather.21.cloned.1.call-start = ((), (), s32[]{:S(2)}) async-start(), calls=%async_computation.19 | async-start | bytes 2949120 | tf_op jit(solution)/shard_map/while/body/eval_jaxpr/all_gather | solution.py:93
  1770.5 278.2 %reduce-scatter.28.cloned.1.call-start = ((), (), s32[]{:S(2)}) async-start(), calls=%async_computation.21 | async-start | bytes 5898240 | tf_op jit(solution)/shard_map/while
  2107.5 52.6 %all-gather.21.cloned.1.call-start = ((), (), s32[]{:S(2)}) async-start(), calls=%async_computation.19 | async-start | bytes 2949120 | tf_op jit(solution)/shard_map/while/body/eval_jaxpr/all_gather | solution.py:93
  2108.2 254.4 %reduce-scatter.28.cloned.1.call-start = ((), (), s32[]{:S(2)}) async-start(), calls=%async_computation.21 | async-start | bytes 5898240 | tf_op jit(solution)/shard_map/while
  2411.2 168.6 %reduce-scatter.18.cloned.1.call-start = ((), (), s32[]{:S(2)}) async-start(), calls=%async_computation.12 | async-start | bytes 819200 | tf_op jit(solution)/shard_map/reduce_scatter | solution.py:409
  2412.0 169.4 %reduce-scatter.22.cloned.1.call-start = ((), (), s32[]{:S(2)}) async-start(), calls=%async_computation.14 | async-start | bytes 3379200 | tf_op jit(solution)/shard_map/reduce_scatter | solution.py:415
  2417.0 197.3 %reduce-scatter.20.cloned.1.call-start = ((), (), s32[]{:S(2)}) async-start(), calls=%async_computation.13 | async-start | bytes 10137600 | tf_op jit(solution)/shard_map/reduce_scatter | solution.py:415
  2428.7 294.6 %reduce-scatter.26.cloned.1.call-start = ((), (), s32[]{:S(2)}) async-start(), calls=%async_computation.16 | async-start | bytes 13516800 | tf_op jit(solution)/shard_map/reduce_scatter | solution.py:415
  2442.3 390.4 %reduce-scatter.24.cloned.1.call-start = ((), (), s32[]{:S(2)}) async-start(), calls=%async_computation.15 | async-start | bytes 13516800 | tf_op jit(solution)/shard_map/reduce_scatter | solution.py:415
  2457.6 401.3 %reduce-scatter.16.cloned.1.call-start = ((), (), s32[]{:S(2)}) async-start(), calls=%async_computation.11 | async-start | bytes 819200 | tf_op jit(solution)/shard_map/reduce_scatter | solution.py:403
  (270 other events, 3871.5 us)
Sparse Core Ops, SparseCore 0:
  10.3 57.2 all-gather.8
  69.9 63.9 all-gather.12
  136.2 44.3 all-gather.10
  182.7 63.6 all-gather.14
  260.7 27.8 all-gather.18
  290.1 30.4 all-gather.16
  376.1 30.4 all-gather.18
  408.3 30.4 all-gather.16
  490.6 36.3 all-gather.18
  528.5 30.4 all-gather.16
  610.9 37.5 all-gather.18
  650.0 30.4 all-gather.16
  714.3 55.3 all-gather.18
  771.3 30.4 all-gather.16
  835.4 53.3 all-gather.22
  890.4 26.6 all-gather.20
  995.9 70.8 reduce-scatter.27
  1098.1 85.8 all-gather.22
  1185.7 26.6 all-gather.20
  1291.2 71.3 reduce-scatter.27
  1402.4 99.1 all-gather.22
  1503.4 26.6 all-gather.20
  1609.1 71.0 reduce-scatter.27
  1769.9 47.7 all-gather.22
  1819.3 26.6 all-gather.20
  1958.7 35.6 reduce-scatter.27
  2133.4 26.6 all-gather.20
  2273.0 34.6 reduce-scatter.27
  2437.8 77.3 reduce-scatter.21
  2519.0 95.2 reduce-scatter.19
  2618.1 105.1 reduce-scatter.25
  2727.6 104.9 reduce-scatter.23
  (3 shorter events, 66.5 us)
where the time goes:
time: 2880 us; the launch traced here: 2870 us
  waiting for transfers between devices  936 us (32%)
  other arithmetic  889 us (31%)
  local copies, waits for them, and re-layouts  409 us (14%)
  matrix products  294 us (10%)
  blocking collectives  264 us (9%)
  starting transfers between devices  43.3 us (2%)
    all_gather x10, waiting for transfers between devices, forward_layer(): lax.all_gather(qkv_groups[:, :, local_width:2 * local_width], 'seq', axis...  438 us
    add x30, other arithmetic, backward_tick(): running + jnp.where(active, addend, jnp.zeros_like(addend))  319 us
    reduce_scatter x4, waiting for transfers between devices, local(): lax.psum_scatter(for_sending(tuple((running[None] for running in totals))...  246 us
    unnamed x2, blocking collectives  240 us
    another operation x59, local copies, waits for them, and re-layouts  173 us
    while x505, local copies, waits for them, and re-layouts  92.3 us
    all_gather x10, waiting for transfers between devices, forward_layer(): lax.all_gather(qkv_groups[:, :, 2 * local_width:], 'seq', axis=1, tiled=T...  75.9 us
    ppermute x10, waiting for transfers between devices, passed_along(): lax.ppermute(value, axis, [(source, source + steps) for source in range(l...  72.4 us
  transfers between devices with their start and end apart: 45, of which 32 were waited for; matrix products, arithmetic and copies ran while one was open for 30% of the time, Pallas kernels for 0%

commit v1 on v0

v1 whole, which is shorter than its diff:
```python
import functools
import math

import jax
import jax.numpy as jnp
from jax import lax
from jax.experimental import pallas as pl
from jax.experimental.pallas import tpu as pltpu
from jax.sharding import Mesh, PartitionSpec as P

HEAD_DIM = 64
EPSILON = 1e-05
MASKED = -1e30
BF = jnp.bfloat16
F32 = jnp.float32
VMEM_LIMIT = 20 * 1024 * 1024


def moved(value, axis, steps):
    count = lax.axis_size(axis)
    return lax.ppermute(value, axis, [(i, (i + steps) % count) for i in range(count)])


def fetched(value, axis, steps):
    return moved(value, axis, -steps)


def swapped(value):
    return moved(value, "core", 1)


def transposed(value):
    rows, columns = lax.axis_size("dp"), lax.axis_size("y")
    pairs = [(x * columns + y, y * columns + x) for x in range(rows) for y in range(columns)]
    return lax.ppermute(value, ("dp", "y"), pairs)


def place_kernel(first, second, group, *refs):
    own, plus, two_a, two_b, minus = refs[:5]
    outs = refs[5 : 5 + group]
    sems = refs[5 + group]
    count = 4
    f = lax.axis_index(first)
    s = lax.axis_index(second)
    copies = []
    for e in range(count):
        for d in range(count):
            if e == 0:
                source = own.at[d]
            elif e == 1:
                source = plus.at[d]
            elif e == 3:
                source = minus.at[d]
            elif d < 2:
                source = two_a.at[d]
            else:
                source = two_b.at[d - 2]
            f_at = lax.rem(f + d, count)
            s_at = lax.rem(s + e, count)
            chip = f_at * count + s_at if first == "dp" else s_at * count + f_at
            for g in range(group):
                copies.append(
                    pltpu.make_async_copy(source.at[g], outs[g].at[chip], sems.at[len(copies)])
                )
    for copy in copies:
        copy.start()
    for copy in copies:
        copy.wait()


def split_at(columns):
    return columns // 256 * 128


class Gather:
    def __init__(self, shards, first, second):
        self.first, self.second, self.group = first, second, len(shards)
        self.shard = jnp.stack(shards)

    def neighbours(self, earlier=None):
        shard = after(self.shard, earlier)
        self.near = fetched(shard, self.first, 1), fetched(shard, self.first, 3)
        return self.near

    def along_first(self):
        plus, minus = self.near
        half = split_at(plus.shape[-1])
        two_a = fetched(plus[..., :half], self.first, 1)
        two_b = fetched(minus[..., half:], self.first, 3)
        two = jnp.concatenate([two_a, two_b], axis=-1)
        self.bundle = jnp.stack([self.shard, plus, two, minus])
        return self.bundle

    def along_second(self, earlier=None):
        bundle = after(self.bundle, earlier)
        self.plus = fetched(bundle, self.second, 1)
        self.minus = fetched(bundle, self.second, 3)
        return self.plus, self.minus

    def placed(self):
        two_a = fetched(self.plus[:2], self.second, 1)
        two_b = fetched(self.minus[2:], self.second, 3)
        rows, columns = self.shard.shape[1:]
        wholes = pl.pallas_call(
            functools.partial(place_kernel, self.first, self.second, self.group),
            out_shape=[jax.ShapeDtypeStruct((16, rows, columns), self.shard.dtype)] * self.group,
            in_specs=[pl.BlockSpec(memory_space=pltpu.VMEM)] * 5,
            out_specs=[pl.BlockSpec(memory_space=pl.ANY)] * self.group,
            scratch_shapes=[pltpu.SemaphoreType.DMA((16 * self.group,))],
            compiler_params=pltpu.CompilerParams(vmem_limit_bytes=VMEM_LIMIT),
            name="place_" + self.first,
        )(self.bundle, self.plus, two_a, two_b, self.minus)
        return [whole.reshape(16 * rows, columns) for whole in wholes]


def gathered_vectors(vectors):
    count, width = vectors.shape
    own = jnp.pad(vectors, ((0, 8 - count), (0, 128 - width)))
    other = swapped(own)
    core_zero = lax.axis_index("core") == 0
    block = jnp.stack([picked(core_zero, own, other), picked(core_zero, other, own)])
    rows = jnp.stack([block] + [fetched(block, "y", d) for d in (1, 2, 3)])
    plane = jnp.stack([rows] + [fetched(rows, "dp", d) for d in (1, 2, 3)])
    plane = jnp.roll(plane, (lax.axis_index("dp"), lax.axis_index("y")), (0, 1))
    plane = plane[:, :, :, :count, :width].transpose(3, 0, 1, 2, 4)
    return plane.reshape(count, -1).astype(F32)


class Scatter:
    def __init__(self, wholes, big, small):
        self.big, self.small = big, small
        self.grids = [whole.reshape((4, 4, whole.shape[0] // 16, whole.shape[1])) for whole in wholes]
        self.along = 0 if big == "dp" else 1
        self.at_big = lax.axis_index(big)
        self.at_small = lax.axis_index(small)

    def chunk(self, steps, lower=0, upper=4):
        at = lax.rem(self.at_big + steps, 4)
        parts = []
        for grid in self.grids:
            part = lax.dynamic_index_in_dim(grid, at, self.along, keepdims=False)
            parts.append(part[lower:upper])
        return parts[0] if len(parts) == 1 else jnp.concatenate(parts, axis=-1)

    def far(self):
        self.far_right, self.far_left = self.chunk(2, 0, 2), self.chunk(2, 2, 4)
        return self.far_right, self.far_left

    def near(self, earlier=None):
        far_right, far_left = after((self.far_right, self.far_left), earlier)
        from_left = moved(far_right, self.big, 1)
        from_right = moved(far_left, self.big, -1)
        self.right = jnp.concatenate([added(self.chunk(1, 0, 2), from_left), self.chunk(1, 2, 4)])
        self.left = jnp.concatenate([self.chunk(3, 0, 2), added(self.chunk(3, 2, 4), from_right)])
        return self.right, self.left

    def bundle(self, earlier=None):
        right, left = after((self.right, self.left), earlier)
        got_left = moved(right, self.big, 1)
        got_right = moved(left, self.big, -1)
        mine = self.chunk(0).astype(F32) + got_left.astype(F32) + got_right.astype(F32)
        self.mine = mine.astype(BF)
        return self.mine

    def piece(self, steps):
        return lax.dynamic_index_in_dim(self.mine, lax.rem(self.at_small + steps, 4), 0, keepdims=False)

    def small_far(self):
        far = self.piece(2)
        half = split_at(far.shape[-1])
        from_left = moved(far[:, :half], self.small, 1)
        from_right = moved(far[:, half:], self.small, -1)
        right, left = self.piece(1), self.piece(3)
        self.right = jnp.concatenate([added(right[:, :half], from_left), right[:, half:]], axis=1)
        self.left = jnp.concatenate([left[:, :half], added(left[:, half:], from_right)], axis=1)
        return self.right, self.left

    def total(self, earlier=None):
        right, left = after((self.right, self.left), earlier)
        got_left = moved(right, self.small, 1)
        got_right = moved(left, self.small, -1)
        return self.piece(0).astype(F32) + got_left.astype(F32) + got_right.astype(F32)


def added(left, right):
    return (left.astype(F32) + right.astype(F32)).astype(BF)


def after(value, earlier):
    return value if earlier is None else lax.optimization_barrier((value, earlier))[0]


def picked(first, value_zero, value_one):
    return jnp.where(first, value_zero, value_one)


def norm_parts(values):
    centered = values - jnp.mean(values, axis=-1, keepdims=True)
    spread = jnp.mean(centered * centered, axis=-1, keepdims=True)
    scale = lax.rsqrt(spread + EPSILON)
    return centered * scale, scale


def layer_norm(values, gain, bias):
    return norm_parts(values)[0] * gain + bias


def layer_norm_back(values, gain, grad):
    unit, scale = norm_parts(values)
    inner = grad * gain
    mean_inner = jnp.mean(inner, axis=-1, keepdims=True)
    mean_cross = jnp.mean(inner * unit, axis=-1, keepdims=True)
    grad_in = scale * (inner - mean_inner - unit * mean_cross)
    return grad_in, unit


NT = (((1,), (1,)), ((), ()))
NN = (((1,), (0,)), ((), ()))


def mxu(left, right, dims=NN):
    return lax.dot_general(left, right, dims, preferred_element_type=F32)


def half_mask(shape, half, axis):
    places = lax.broadcasted_iota(jnp.int32, shape, axis)
    return (places < HEAD_DIM) if half == 0 else (places >= HEAD_DIM)


def whole():
    return pl.BlockSpec(memory_space=pltpu.VMEM)


def called(kernel, name, out_shape, operands, flops, transcendentals):
    shapes = [(o.shape, o.dtype) for o in (*operands, *out_shape)]
    return pl.pallas_call(
        kernel,
        out_shape=out_shape,
        in_specs=[whole()] * len(operands),
        out_specs=[whole()] * len(out_shape),
        compiler_params=pltpu.CompilerParams(vmem_limit_bytes=VMEM_LIMIT),
        cost_estimate=pl.CostEstimate(
            flops=flops,
            bytes_accessed=sum(math.prod(shape) * dtype.itemsize for shape, dtype in shapes),
            transcendentals=transcendentals,
        ),
        name=name,
    )(*operands)


def by_head(block):
    zero = jnp.zeros_like(block)
    return jnp.concatenate([jnp.where(half_mask(block.shape, h, 1), block, zero) for h in range(2)])


def of_heads(rows):
    half = rows.shape[0] // 2
    return jnp.where(half_mask((half, rows.shape[1]), 0, 1), rows[:half], rows[half:])


def attend_kernel(save, q_ref, kv_ref, mark_q_ref, mark_k_ref, out_ref, *kept):
    scaling = jnp.asarray(HEAD_DIM ** (-0.5), BF)
    mark_k = mark_k_ref[...]
    mark_q = jnp.concatenate([mark_q_ref[...]] * 2)
    queries = q_ref.shape[0]
    for pair in range(q_ref.shape[1] // 128):
        q = by_head(q_ref[:, 128 * pair : 128 * pair + 128] * scaling)
        k = kv_ref[:, 256 * pair : 256 * pair + 128]
        v = kv_ref[:, 256 * pair + 128 : 256 * pair + 256]
        q_marked = jnp.concatenate([q, mark_q], axis=1)
        k_marked = jnp.concatenate([k, mark_k], axis=1)
        scores = mxu(q_marked, k_marked, NT)
        top = jnp.max(scores, axis=1, keepdims=True)
        probs = jnp.exp(scores - top).astype(BF)
        out = mxu(probs, jnp.concatenate([v, jnp.ones_like(v)], axis=1))
        total = out[:, 128:]
        out_ref[:, 128 * pair : 128 * pair + 128] = of_heads(out[:, :128] / total).astype(BF)
        if save:
            lse = top + jnp.log(total[:, :1])
            kept[0][:, 2 * pair : 2 * pair + 1] = lse[:queries]
            kept[0][:, 2 * pair + 1 : 2 * pair + 2] = lse[queries:]


def attend(q, kv, mark_q, mark_k, save):
    queries, width = q.shape
    keys = kv.shape[0]
    out_shape = [jax.ShapeDtypeStruct((queries, width), BF)]
    if save:
        out_shape.append(jax.ShapeDtypeStruct((queries, width // HEAD_DIM), F32))
    flops, exps = 16 * queries * keys * width, 2 * queries * keys * width // 128
    return called(
        functools.partial(attend_kernel, save), "attend", out_shape, (q, kv, mark_q, mark_k), flops, exps
    )


def attend_back_kernel(q_ref, kv_ref, do_ref, out_ref, lse_ref, mark_q_ref, mark_k_ref, dq_ref, dkv_ref):
    scaling = jnp.asarray(HEAD_DIM ** (-0.5), BF)
    mark_k = mark_k_ref[...]
    mark_q = jnp.concatenate([mark_q_ref[...]] * 2)
    for pair in range(q_ref.shape[1] // 128):
        columns = slice(128 * pair, 128 * pair + 128)
        q = by_head(q_ref[:, columns] * scaling)
        do = by_head(do_ref[:, columns])
        out = by_head(out_ref[:, columns])
        k = kv_ref[:, 256 * pair : 256 * pair + 128]
        v = kv_ref[:, 256 * pair + 128 : 256 * pair + 256]
        lse = jnp.concatenate([lse_ref[:, 2 * pair : 2 * pair + 1], lse_ref[:, 2 * pair + 1 : 2 * pair + 2]])
        delta = jnp.sum(do.astype(F32) * out.astype(F32), axis=1, keepdims=True)
        q_marked = jnp.concatenate([q, mark_q], axis=1)
        k_marked = jnp.concatenate([k, mark_k], axis=1)
        probs = jnp.exp(mxu(q_marked, k_marked, NT) - lse)
        grad_scores = (probs * (mxu(do, v, NT) - delta)).astype(BF)
        dq_ref[:, columns] = (of_heads(mxu(grad_scores, k)) * HEAD_DIM ** (-0.5)).astype(BF)
        dkv_ref[:, 256 * pair : 256 * pair + 128] = mxu(q.T, grad_scores).T.astype(BF)
        dkv_ref[:, 256 * pair + 128 : 256 * pair + 256] = mxu(do.T, probs.astype(BF)).T.astype(BF)


def attend_back(q, kv, do, out, lse, mark_q, mark_k):
    queries, width = q.shape
    keys = kv.shape[0]
    out_shape = [jax.ShapeDtypeStruct(q.shape, BF), jax.ShapeDtypeStruct(kv.shape, BF)]
    flops, exps = 40 * queries * keys * width, 2 * queries * keys * width // 128
    operands = (q, kv, do, out, lse, mark_q, mark_k)
    return called(attend_back_kernel, "attend_back", out_shape, operands, flops, exps)


def gelu_and_slope(values):
    phi = 0.5 * (1.0 + lax.erf(values * 0.7071067811865476))
    slope = phi + values * (0.3989422804014327 * jnp.exp(-0.5 * values * values))
    return values * phi, slope


BLOCK = 256


def feed_kernel(save, x_ref, up, down, out_ref, act_ref, *kept):
    x = x_ref[...]
    for at in range(0, up.shape[1], BLOCK):
        columns = slice(at, at + BLOCK)
        act, slope = gelu_and_slope(mxu(x, up[:, columns]))
        act_ref[:, columns] = act.astype(BF)
        if save:
            kept[0][:, columns] = slope.astype(BF)
    for at in range(0, out_ref.shape[1], BLOCK):
        columns = slice(at, at + BLOCK)
        out_ref[:, columns] = mxu(act_ref[...], down[:, columns])


def feed(x, up, down, save):
    rows, width = x.shape
    units = up.shape[1]
    kept = jax.ShapeDtypeStruct((rows, units), BF)
    out_shape = [jax.ShapeDtypeStruct((rows, width), F32), kept] + ([kept] if save else [])
    flops, exps = 4 * rows * width * units, 2 * rows * units
    return called(functools.partial(feed_kernel, save), "feed", out_shape, (x, up, down), flops, exps)


def feed_back_kernel(g_ref, slope_ref, up, down, out_ref, grad_ref):
    g = g_ref[...]
    for at in range(0, down.shape[0], BLOCK):
        rows = slice(at, at + BLOCK)
        grad = mxu(g, down[rows, :], NT) * slope_ref[:, rows].astype(F32)
        grad_ref[:, rows] = grad.astype(BF)
    for at in range(0, out_ref.shape[1], BLOCK):
        rows = slice(at, at + BLOCK)
        out_ref[:, rows] = mxu(grad_ref[...], up[rows, :], NT)


def feed_back(g, slope, up, down):
    rows, width = g.shape
    units = up.shape[1]
    out_shape = [jax.ShapeDtypeStruct((rows, width), F32), jax.ShapeDtypeStruct((rows, units), BF)]
    return called(feed_back_kernel, "feed_back", out_shape, (g, slope, up, down), 4 * rows * width * units, 0)


def dot(left, right, dims=NN):
    return lax.dot_general(left, right, dims, preferred_element_type=F32)


def from_other(part):
    half = part.shape[0] // 2
    other = swapped(part.astype(BF)).astype(F32)
    return jnp.concatenate([other[half:], other[:half]])


class Forward:
    def __init__(self, start, ring, marks, norms, received=None):
        self.ring, self.marks, self.norms = ring, marks, norms
        self.start, self.received = start, received
        self.rows = start.shape[0]

    def norm(self, earlier=None):
        hidden_low = self.start
        if self.received is not None:
            received = after(self.received, earlier)
            hidden_low = jnp.where(lax.axis_index("section") == 0, self.start, received)
        self.hidden = hidden_low.astype(F32)
        self.hidden_other = swapped(hidden_low)
        normed = layer_norm(self.hidden, self.norms[0], self.norms[1]).astype(BF)
        self.normed = normed
        self.fetched = [fetched(normed, self.ring, d) for d in (1, 2, 3)]

    def collect(self, earlier=None):
        normed = self.normed
        ring_rows = jnp.concatenate(after([normed] + self.fetched, earlier))
        other_rows = swapped(ring_rows)
        self.normed_all = jnp.concatenate([ring_rows, other_rows])
        self.normed_chip = jnp.concatenate([normed, other_rows[: self.rows]])

    def attention(self, weights, save, earlier):
        normed_all, normed_chip = after((self.normed_all, self.normed_chip), earlier)
        self.kv = dot(normed_all, weights["kv"]).astype(BF)
        self.q = dot(normed_chip, weights["q"]).astype(BF)
        self.attended, *self.lse = attend(self.q, self.kv, *self.marks, save)

    def feed_forward(self, weights, save, arrivals):
        rows = self.rows
        part = dot(self.attended, weights["out"])
        hidden = jnp.concatenate([self.hidden, self.hidden_other.astype(F32)])
        self.middle = hidden + part + from_other(part)
        normed_ffn = layer_norm(self.middle, self.norms[2], self.norms[3]).astype(BF)
        self.normed_ffn = after(normed_ffn, arrivals)
        fed, self.act, *self.slope = feed(self.normed_ffn, *weights["feed"], save)
        self.fed = fed
        self.result = (self.middle[:rows] + fed[:rows] + swapped(fed[rows:].astype(BF)).astype(F32)).astype(BF)


class Backward:
    def __init__(self, grad_low, forward):
        self.grad_low, self.forward = grad_low, forward
        self.rows = grad_low.shape[0]
        self.grad_chip = jnp.concatenate([grad_low, swapped(grad_low)])

    def feed_forward(self, weights, earlier, arrivals):
        rows, forward = self.rows, self.forward
        grad_chip = after(self.grad_chip, earlier)
        back, self.grad_up = feed_back(grad_chip, *forward.slope, *weights["feed"])
        back = after(back, arrivals)
        grad_normed = back + from_other(back)
        gain = forward.norms[2]
        part, unit = layer_norm_back(forward.middle, gain, grad_normed)
        self.grad_gain_ffn = jnp.sum(grad_normed[:rows] * unit[:rows], axis=0)
        self.grad_bias_ffn = jnp.sum(grad_normed[:rows], axis=0)
        grad_middle = grad_chip.astype(F32) + part
        self.grad_middle = grad_middle[:rows]
        self.grad_middle_low = grad_middle.astype(BF)
        self.grad_heads = dot(self.grad_middle_low, weights["out"], NT).astype(BF)

    def attention(self, weights, earlier):
        forward = self.forward
        grad_heads = after(self.grad_heads, earlier)
        self.dq, self.dkv = attend_back(
            forward.q, forward.kv, grad_heads, forward.attended, *forward.lse, *forward.marks
        )

    def project(self, weights, earlier=None):
        rows = self.rows
        self.dq, self.dkv = after((self.dq, self.dkv), earlier)
        grad_all = dot(self.dkv, weights["kv"], NT)
        grad_chip = dot(self.dq, weights["q"], NT)
        half = grad_all.shape[0] // 2
        own = jnp.concatenate([grad_all[:rows] + grad_chip[:rows], grad_all[rows:half]])
        away = jnp.concatenate([grad_all[half : half + rows] + grad_chip[rows:], grad_all[half + rows :]])
        self.ring_grads = own + swapped(away.astype(BF)).astype(F32)

    def spread(self):
        rows = self.rows
        self.pieces = [
            moved(self.ring_grads[d * rows : (d + 1) * rows].astype(BF), self.forward.ring, d)
            for d in (1, 2, 3)
        ]

    def reduce(self, earlier=None):
        forward = self.forward
        grad_normed = self.ring_grads[: self.rows]
        for piece in after(self.pieces, earlier):
            grad_normed = grad_normed + piece.astype(F32)
        part, unit = layer_norm_back(forward.hidden, forward.norms[0], grad_normed)
        self.grad_gain_attn = jnp.sum(grad_normed * unit, axis=0)
        self.grad_bias_attn = jnp.sum(grad_normed, axis=0)
        self.grad_hidden_low = (self.grad_middle + part).astype(BF)

    def vectors(self):
        return jnp.stack([self.grad_gain_attn, self.grad_bias_attn, self.grad_gain_ffn, self.grad_bias_ffn])


def marks_of(lengths, place, rows, core):
    index = lax.iota(jnp.int32, 8 * rows)
    core_at = jnp.where(index < 4 * rows, core, 1 - core)
    chip_at = lax.rem(place + lax.rem(index // rows, 4), 4)
    positions = chip_at * (2 * rows) + core_at * rows + lax.rem(index, rows)
    cells = lengths.shape[0]
    bounds = jnp.cumsum(lengths)
    segments = jnp.sum((positions[:, None] >= bounds[None, :]).astype(jnp.int32), axis=1, keepdims=True)
    places = lax.broadcasted_iota(jnp.int32, (1, 128), 1)
    own = segments == places
    mark_q = jnp.where(own | (places >= cells), 0.0, MASKED).astype(BF)
    mark_k = own.astype(BF)
    return jnp.concatenate([mark_q[:rows], mark_q[4 * rows : 5 * rows]]), mark_k


def attention_shards(w_qkv, w_out, core_zero):
    width = w_out.shape[1]
    half = width // 2

    def arranged(core):
        pieces = []
        for pair in range(half // 128):
            at = half * core + 128 * pair
            pieces.append(w_qkv[:, width + at : width + at + 128])
            pieces.append(w_qkv[:, 2 * width + at : 2 * width + at + 128])
        pieces.append(w_qkv[:, half * core : half * core + half])
        pieces.append(w_out[:, half * core : half * core + half])
        return jnp.concatenate(pieces, axis=1)

    both = exchanged_in(arranged(0), arranged(1), core_zero)
    return both[:, :width], both[:, width:]


def exchanged_in(zero, one, core_zero):
    mine = picked(core_zero, zero, one)
    other = swapped(picked(core_zero, one, zero))
    return jnp.concatenate([picked(core_zero, mine, other), picked(core_zero, other, mine)])


def up_shard(w_up, core_zero):
    rows = w_up.shape[0]
    units = w_up.reshape(rows, 16, 2, w_up.shape[1] // 32)
    return exchanged_in(units[:, :, 0].reshape(rows, -1), units[:, :, 1].reshape(rows, -1), core_zero)


def out_rows(out_half, core_zero):
    half = out_half.shape[1]
    zero, one = out_half[:half], out_half[half:]
    mine = picked(core_zero, zero, one)
    other = swapped(picked(core_zero, one, zero))
    return jnp.concatenate([picked(core_zero, mine, other), picked(core_zero, other, mine)], axis=1)


TN = (((0,), (0,)), ((), ()))


def summed(lefts, rights):
    return dot(jnp.concatenate(lefts), jnp.concatenate(rights), TN)


def feed_grads(backs):
    forwards = [back.forward for back in backs]
    down = summed([f.act for f in forwards], [back.grad_chip for back in backs])
    up = summed([f.normed_ffn for f in forwards], [back.grad_up for back in backs])
    return up.astype(BF), down.astype(BF)


def out_grads(backs, core_zero):
    grads = summed([back.forward.attended for back in backs], [back.grad_middle_low for back in backs])
    grads = grads.astype(BF)
    half = grads.shape[0]
    zero, one = grads[:, :half], grads[:, half:]
    mine = picked(core_zero, zero, one)
    other = swapped(picked(core_zero, one, zero))
    return jnp.concatenate([picked(core_zero, mine, other), picked(core_zero, other, mine)])


def query_grads(backs):
    return summed([back.forward.normed_chip for back in backs], [back.dq for back in backs]).astype(BF)


def key_value_grads(backs):
    return summed([back.forward.normed_all for back in backs], [back.dkv for back in backs]).astype(BF)


def vector_grads(backs):
    vectors = sum(back.vectors() for back in backs)
    vectors = jnp.pad(vectors, ((0, 128 - vectors.shape[0]), (0, 0))).astype(BF)
    vectors = vectors.astype(F32) + swapped(vectors).astype(F32)
    return vectors.astype(BF).T


def exchanged_out(shard, core_zero):
    rows = shard.shape[0] // 2
    zero, one = shard[:rows], shard[rows:]
    mine = picked(core_zero, zero, one)
    other = swapped(picked(core_zero, one, zero).astype(BF)).astype(F32)
    return picked(core_zero, mine, other), picked(core_zero, other, mine)


def whole_features(shard, section, target):
    both = jnp.stack([shard[0], transposed(shard[1])])
    pieces = []
    for z in range(4):
        pieces.append(both if z == target else lax.ppermute(both, "section", [(z, target)]))
    return jnp.concatenate(pieces, axis=2)


def spread_features(both, section, source):
    width = both.shape[2] // 4
    total = None
    for z in range(4):
        piece = both[:, :, z * width : (z + 1) * width]
        if z == source:
            piece = jnp.where(section == source, piece, jnp.zeros_like(piece))
        else:
            piece = lax.ppermute(piece, "section", [(source, z)])
        total = piece if total is None else total + piece
    return jnp.stack([total[0], transposed(total[1])])


def local(
    block_input,
    cotangent,
    cell_lengths,
    norm_attn_gain,
    norm_attn_bias,
    w_qkv,
    w_out,
    norm_ffn_gain,
    norm_ffn_bias,
    w_up,
    w_down,
):
    section = lax.axis_index("section")
    at_x = lax.axis_index("dp")
    at_y = lax.axis_index("y")
    core = lax.axis_index("core")
    core_zero = core == 0
    sections = lax.axis_size("section")
    rows = block_input.shape[1]
    rings = ("y", "dp")
    width = w_out.shape[2]
    half = width // 2

    w_down_whole = lax.all_gather(w_down[0], ("dp", "y"), axis=0, tiled=True)
    w_up_whole = lax.all_gather(up_shard(w_up[0], core_zero), ("dp", "y"), axis=0, tiled=True)
    kv_shard, rest_shard = attention_shards(w_qkv[0], w_out[0], core_zero)
    kv, rest = Gather([kv_shard], "dp", "y"), Gather([rest_shard], "y", "dp")
    near = kv.neighbours() + rest.neighbours()
    vectors = jnp.concatenate([norm_attn_gain, norm_attn_bias, norm_ffn_gain, norm_ffn_bias])
    norms = gathered_vectors(after(vectors, near))
    norms = tuple(norms[i : i + 1] for i in range(4))
    start = whole_features(after(block_input, near), section, 0)
    kv.along_first()
    rest.along_first()
    kv.along_second()
    rest.along_second()
    passes = [Forward(start[m], rings[m], None, norms) for m in range(2)]
    for now in passes:
        now.norm()
    marks = (
        marks_of(cell_lengths[2 * at_x], at_y, rows, core),
        marks_of(cell_lengths[2 * at_y + 1], at_x, rows, core),
    )
    for m, now in enumerate(passes):
        now.marks = marks[m]
        now.collect()
    (w_kv,) = kv.placed()
    (rest_whole,) = rest.placed()
    weights = {"kv": w_kv, "q": rest_whole[:, :half], "out": out_rows(rest_whole[:, half:], core_zero)}
    weights["feed"] = (w_up_whole, w_down_whole)

    forward_pairs = [(s, s + 1) for s in range(sections - 1)]
    result = None
    for step in range(sections):
        final = step == sections - 1
        for m in range(2):
            now, other = passes[m], passes[1 - m]
            waiting = step + m > 0 and not (final and m == 1)
            now.attention(weights, final, result)
            if waiting:
                other.norm(now.attended)
            now.feed_forward(weights, final, other.fetched[::2] if waiting else None)
            if waiting:
                other.collect(now.fed)
            result = now.result
            if not final:
                received = lax.ppermute(result, "section", forward_pairs)
                passes[m] = Forward(start[m], rings[m], marks[m], norms, received)
    block_output = spread_features(jnp.stack([now.result for now in passes]), section, sections - 1)

    last_grad = whole_features(cotangent, section, sections - 1)
    backs = [Backward(last_grad[m], passes[m]) for m in range(2)]
    backward_pairs = [(s + 1, s) for s in range(sections - 1)]
    earlier = result
    for step in range(sections):
        final = step == sections - 1
        for m in range(2):
            now, other = backs[m], backs[1 - m]
            waiting = step + m > 0
            now.feed_forward(weights, earlier, other.pieces[::2] if waiting else None)
            if waiting:
                other.reduce(now.grad_heads)
            if final and m == 1:
                break
            now.attention(weights, other.grad_hidden_low if waiting else None)
            if waiting:
                received = lax.ppermute(other.grad_hidden_low, "section", backward_pairs)
                received = after(received, now.dkv)
                grad_low = jnp.where(section == sections - 1, last_grad[1 - m], received)
                now.project(weights, grad_low)
                backs[1 - m] = Backward(grad_low, passes[1 - m])
            else:
                now.project(weights)
            now.spread()
            earlier = now.ring_grads

    arrived = backs[0].pieces
    up_grad, down_grad = feed_grads(backs)
    up_grads = lax.psum_scatter(up_grad, ("dp", "y"), scatter_dimension=0, tiled=True)
    sum_zero = Scatter([after(down_grad[:, :half], arrived)], "y", "dp")
    sum_one = Scatter([after(down_grad[:, half:], arrived)], "dp", "y")
    far = sum_zero.far() + sum_one.far()
    backs[1].attention(weights, (backs[0].grad_hidden_low, far))
    near = sum_zero.near() + sum_one.near()
    backs[1].project(weights, near)
    backs[1].spread()
    mine = sum_zero.bundle(), sum_one.bundle()
    sum_kv = Scatter([key_value_grads(backs)], "y", "dp")
    out_part = out_grads(backs, core_zero)
    query_part = query_grads(backs)
    backs[1].reduce(mine)
    sum_rest = Scatter([query_part, out_part, vector_grads(backs)], "dp", "y")
    sum_kv.far()
    sum_rest.far()
    near = sum_kv.near(mine) + sum_rest.near(mine)
    sum_zero.small_far()
    sum_one.small_far()
    mine = sum_kv.bundle(), sum_rest.bundle()
    down_grads = [sum_zero.total(near), sum_one.total(near)]
    input_grad = spread_features(
        after(jnp.stack([now.grad_hidden_low for now in backs]), near), section, 0
    ).astype(F32)
    sum_kv.small_far()
    sum_rest.small_far()
    kv_grads = sum_kv.total()
    rest_grads = sum_rest.total()

    own_rows = w_out.shape[1]
    units = jnp.stack(exchanged_out(up_grads.astype(F32), core_zero), axis=1)
    units = units.reshape(own_rows, 2, 16, -1).transpose(0, 2, 1, 3)
    grad_up = units.reshape(own_rows, -1)
    grad_down = jnp.concatenate(down_grads, axis=1)
    kv_cores = exchanged_out(kv_grads, core_zero)
    rest_cores = exchanged_out(rest_grads[:, :width], core_zero)
    keys, values = [], []
    for part in kv_cores:
        for pair in range(half // 128):
            keys.append(part[:, 256 * pair : 256 * pair + 128])
            values.append(part[:, 256 * pair + 128 : 256 * pair + 256])
    grad_qkv = jnp.concatenate([rest_cores[0][:, :half], rest_cores[1][:, :half]] + keys + values, axis=1)
    grad_out = jnp.concatenate([rest_cores[0][:, half:width], rest_cores[1][:, half:width]], axis=1)
    columns = rest_grads[:, width:]
    grad_vectors = picked(core_zero, columns[:own_rows], columns[own_rows:]).T[:4]
    return (
        block_output,
        input_grad,
        grad_vectors[0:1],
        grad_vectors[1:2],
        grad_qkv[None],
        grad_out[None],
        grad_vectors[2:3],
        grad_vectors[3:4],
        grad_up[None],
        grad_down[None],
    )


def solution(mesh):
    sizes = mesh.devices.shape
    cores = Mesh(mesh.devices.reshape(sizes[0], sizes[1], sizes[2] // 2, 2), ("section", "dp", "y", "core"))
    seq = ("y", "core")
    plane = ("dp", "y", "core")
    rows = P("dp", seq, "section")
    vector = P("section", plane)
    matrix = P("section", plane, None)
    return jax.shard_map(
        local,
        mesh=cores,
        in_specs=(rows, rows, P(), vector, vector, matrix, matrix, vector, vector, matrix, matrix),
        out_specs=(rows, rows, vector, vector, matrix, matrix, vector, vector, matrix, matrix),
        check_vma=False,
    )
```

time: 2880 us -> 1100 us (0.38)
  other arithmetic: 889 us -> 97.5 us
  waiting for transfers between devices: 936 us -> 300 us
  local copies, waits for them, and re-layouts: 409 us -> 122 us
  blocking collectives: 264 us -> 0 us
  starting transfers between devices: 43.3 us -> 272 us
  matrix products: 294 us -> 111 us
  Pallas kernels: 0 us -> 158 us
    all_gather x24 -> x2, waiting for transfers between devices: 562 us -> 0.01 us  [the longest x1 0.01 us: local(): w_down_whole = lax.all_gather(w_down[0], ('dp', 'y'), axis=0, tiled=True)]
    add x30 -> x21, other arithmetic: 319 us -> 8.74 us  [the longest x8 5.03 us: project(): grad_all[:rows] + grad_chip[:rows]]
    reduce_scatter x6 -> x1, waiting for transfers between devices: 270 us -> 0.01 us  [local(): lax.psum_scatter(up_grad, ('dp', 'y'), scatter_dimension=0, tiled=True)]
    convert_element_type x74 -> x80, other arithmetic: 273 us -> 30.4 us  [the longest x8 5.4 us: feed_forward(): layer_norm(self.middle, self.norms[2], self.norms[3]).astype(BF)]
    unnamed x2 -> x0, blocking collectives: 240 us -> none
    ppermute x10 -> x195, starting transfers between devices: 42 us -> 272 us  [the longest x167 219 us: moved(): lax.ppermute(value, axis, [(i, (i + steps) % count) for i in range(count)])]
    ppermute x10 -> x195, waiting for transfers between devices: 72.4 us -> 299 us  [the longest x167 271 us: moved(): lax.ppermute(value, axis, [(i, (i + steps) % count) for i in range(count)])]
    dot_general x46 -> x53, matrix products: 294 us -> 111 us  [dot(): return lax.dot_general(left, right, dims, preferred_element_type=F32)]
  transfers between devices with their start and end apart: 45 -> 198, of which waited for: 32 -> 89; matrix products, arithmetic and copies ran while one was open for 30% -> 20% of each run, Pallas kernels for 0% -> 14%
where the time goes in v1:
time: 1100 us; the launch traced here: 1080 us
  waiting for transfers between devices  300 us (27%)
  starting transfers between devices  272 us (25%)
  Pallas kernels  158 us (14%)
  local copies, waits for them, and re-layouts  122 us (11%)
  matrix products  111 us (10%)
  other arithmetic  97.5 us (9%)
  between operations  20.3 us (2%)
    ppermute x167, waiting for transfers between devices, moved(): lax.ppermute(value, axis, [(i, (i + steps) % count) for i in range(count)])  271 us
    ppermute x167, starting transfers between devices, moved(): lax.ppermute(value, axis, [(i, (i + steps) % count) for i in range(count)])  219 us
    pallas_call x32, Pallas kernels, called(): pl.pallas_call(kernel, out_shape=out_shape, in_specs=[whole()] * len(oper...  146 us
    dot_general x53, matrix products, dot(): return lax.dot_general(left, right, dims, preferred_element_type=F32)  111 us
    unnamed x666, local copies, waits for them, and re-layouts  66.5 us
  transfers between devices with their start and end apart: 198, of which 89 were waited for; matrix products, arithmetic and copies ran while one was open for 20% of the time, Pallas kernels for 14%

profile of v1, /device:TPU:23, one launch (start us, length us, event | category | flops | bytes accessed | tf_op | source)
XLA Modules:
  0.0 1080.7 jit_solution(14336259999774156034)
XLA Ops:
  30.5 7.2 collective-permute-done.1
  103.7 6.9 collective-permute-done.39
  113.9 9.6 collective-permute-start.20
  144.7 11.4 %collective-permute-done.24.refs_2_ = bf16[2,1,80,1280]{3,2,1,0:T(8,128)(2,1)S(1)} collective-permute-done((bf16[2,1,80,1280]{3,2,1,0:T(8,128)(2,1)S(1)}, bf16[2,1,80,1280]{3,2,1,0:T(8,128)(2,1)S(1)}, u32[]{:S(2)}, u32[]{:S(2)}) %collective-permute-start.24) | collective-permute-done | bytes 409632 | tf_op jit(solution)/shard_map/ppermute | solution.py:21
  172.2 5.6 place_dp.1
  230.0 8.5 collective-permute-done.43
  308.9 9.3 collective-permute-done.61
  386.9 9.6 collective-permute-done.77
  430.4 7.5 collective-permute-done.85
  463.2 6.1 collective-permute-done.97
  500.2 6.9 attend_back.8
  545.7 6.9 attend_back.9
  582.8 5.8 collective-permute-done.114
  590.9 6.9 attend_back.10
  634.0 6.1 collective-permute-done.118
  643.2 6.9 attend_back.11
  687.1 6.1 collective-permute-done.128
  696.2 6.9 attend_back.12
  736.3 5.9 collective-permute-done.132
  744.1 6.9 attend_back.13
  805.3 6.9 attend_back.14
  828.4 6.4 fusion.262
  850.2 6.3 collective-permute-done.146
  861.7 5.6 convolution_convert_fusion
  897.3 6.9 attend_back.15
  916.6 9.2 convolution_convert_fusion.2
  944.8 9.0 collective-permute-done.192
  954.5 6.0 collective-permute-done.188
  974.9 9.9 collective-permute-done.157
  1002.9 5.8 collective-permute-start.185
  1013.1 9.5 collective-permute-start.170
  1049.5 13.5 %collective-permute-start.178 = (bf16[40,1280]{1,0:T(8,128)(2,1)S(1)}, bf16[40,1280]{1,0:T(8,128)(2,1)S(1)}, u32[]{:S(2)}, u32[]{:S(2)}) collective-permute-start(bf16[40,1280]{1,0:T(8,128)(2,1)S(1)} %select_convert_fusion.4), channel_id=1, source_target_pairs={{0,1},{1,0},{2,3},{3,2},{4,5},{5,4},{6,7},{7,6},{8,9},{9,8},{10,11... | collective-permute-start | bytes 307208 | tf_op jit(solution)/shard_map/ppermute | solution.py:21
  (1596 shorter events, 818.5 us)
Async XLA Ops:
  7.2 189.4 %all-gather.6.cloned.1.call-start = ((), (), s32[]{:S(2)}) async-start(), calls=%async_computation.3 | async-start | bytes 6963200 | tf_op jit(solution)/shard_map/all_gather | solution.py:632
  7.9 188.7 %all-gather.4.cloned.1.call-start = ((), (), s32[]{:S(2)}) async-start(), calls=%async_computation.1 | async-start | bytes 6963200 | tf_op jit(solution)/shard_map/all_gather | solution.py:633
  30.4 1036.1 %reduce-scatter.2.cloned.1.call-start = ((), (), s32[]{:S(2)}) async-start(), calls=%async_computation.2 | async-start | bytes 6963200 | tf_op jit(solution)/shard_map/reduce_scatter | solution.py:707
  48.5 37.1 %collective-permute-start.28 = (bf16[1,80,640]{2,1,0:T(8,128)(2,1)}, bf16[1,80,640]{2,1,0:T(8,128)(2,1)S(1)}, u32[]{:S(2)}, u32[]{:S(2)}) collective-permute-start(bf16[1,80,640]{2,1,0:T(8,128)(2,1)} %slice.1532), channel_id=1, source_target_pairs={{0,8},{8,16},{16,24},{24,0},{1,9},{9,17},{17,25},{25,1},{2,10},{10... | collective-permute-start | bytes 307208 | tf_op jit(solution)/shard_map/ppermute | solution.py:21
  63.4 25.6 %collective-permute-start.27 = (bf16[1,80,640]{2,1,0:T(8,128)(2,1)S(1)}, bf16[1,80,640]{2,1,0:T(8,128)(2,1)}, u32[]{:S(2)}, u32[]{:S(2)}) collective-permute-start(bf16[1,80,640]{2,1,0:T(8,128)(2,1)S(1)} %slice.1531), channel_id=1, source_target_pairs={{0,24},{8,0},{16,8},{24,16},{1,25},{9,1},{17,9},{25,17},{2,26},{10... | collective-permute-start | bytes 307208 | tf_op jit(solution)/shard_map/ppermute | solution.py:21
  99.4 35.3 %collective-permute-start.23 = (bf16[4,1,80,1280]{3,2,1,0:T(8,128)(2,1)S(1)}, bf16[4,1,80,1280]{3,2,1,0:T(8,128)(2,1)S(1)}, u32[]{:S(2)}, u32[]{:S(2)}) collective-permute-start(bf16[4,1,80,1280]{3,2,1,0:T(8,128)(2,1)S(1)} %pad_maximum_fusion.19.refs_0_), channel_id=1, source_target_pairs={{0,24},{8,0},{16,8},{24,16},{1,25},{9,1},{17,9},{25,17},{2,26},{10... | collective-permute-start | bytes 2457608 | tf_op jit(solution)/shard_map/ppermute | solution.py:21
  100.1 34.8 %collective-permute-start.25 = (bf16[4,1,80,1280]{3,2,1,0:T(8,128)(2,1)S(1)}, bf16[4,1,80,1280]{3,2,1,0:T(8,128)(2,1)}, u32[]{:S(2)}, u32[]{:S(2)}) collective-permute-start(bf16[4,1,80,1280]{3,2,1,0:T(8,128)(2,1)S(1)} %pad_maximum_fusion.19.refs_0_), channel_id=1, source_target_pairs={{0,8},{8,16},{16,24},{24,0},{1,9},{9,17},{17,25},{25,1},{2,10},{10... | collective-permute-start | bytes 2457608 | tf_op jit(solution)/shard_map/ppermute | solution.py:21
  110.6 28.1 %collective-permute-start.29 = (bf16[4,1,80,1280]{3,2,1,0:T(8,128)(2,1)S(1)}, bf16[4,1,80,1280]{3,2,1,0:T(8,128)(2,1)S(1)}, u32[]{:S(2)}, u32[]{:S(2)}) collective-permute-start(bf16[4,1,80,1280]{3,2,1,0:T(8,128)(2,1)S(1)} %pad_maximum_fusion.20.refs_0_), channel_id=1, source_target_pairs={{0,6},{2,0},{4,2},{6,4},{1,7},{3,1},{5,3},{7,5},{8,14},{10,8},{12,... | collective-permute-start | bytes 2457608 | tf_op jit(solution)/shard_map/ppermute | solution.py:21
  112.5 31.1 %collective-permute-start.31 = (bf16[4,1,80,1280]{3,2,1,0:T(8,128)(2,1)S(1)}, bf16[4,1,80,1280]{3,2,1,0:T(8,128)(2,1)}, u32[]{:S(2)}, u32[]{:S(2)}) collective-permute-start(bf16[4,1,80,1280]{3,2,1,0:T(8,128)(2,1)S(1)} %pad_maximum_fusion.20.refs_0_), channel_id=1, source_target_pairs={{0,2},{2,4},{4,6},{6,0},{1,3},{3,5},{5,7},{7,1},{8,10},{10,12},{12... | collective-permute-start | bytes 2457608 | tf_op jit(solution)/shard_map/ppermute | solution.py:21
  113.9 63.9 %collective-permute-start.20 = (bf16[512,1280]{1,0:T(8,128)(2,1)}, bf16[512,1280]{1,0:T(8,128)(2,1)}, u32[]{:S(2)}, u32[]{:S(2)}) collective-permute-start(bf16[512,1280]{1,0:T(8,128)(2,1)} %pad_maximum_fusion.2), channel_id=1, source_target_pairs={{0,1},{1,0},{2,3},{3,2},{4,5},{5,4},{6,7},{7,6},{8,9},{9,8},{10,11... | collective-permute-start | bytes 3932168 | tf_op jit(solution)/shard_map/ppermute | solution.py:21
  134.8 21.3 %collective-permute-start.24 = (bf16[2,1,80,1280]{3,2,1,0:T(8,128)(2,1)S(1)}, bf16[2,1,80,1280]{3,2,1,0:T(8,128)(2,1)S(1)}, u32[]{:S(2)}, u32[]{:S(2)}) collective-permute-start(bf16[2,1,80,1280]{3,2,1,0:T(8,128)(2,1)S(1)} %slice.1528), channel_id=1, source_target_pairs={{0,24},{8,0},{16,8},{24,16},{1,25},{9,1},{17,9},{25,17},{2,26},{10... | collective-permute-start | bytes 1228808 | tf_op jit(solution)/shard_map/ppermute | solution.py:21
  136.2 22.8 %collective-permute-start.26 = (bf16[2,1,80,1280]{3,2,1,0:T(8,128)(2,1)S(1)}, bf16[2,1,80,1280]{3,2,1,0:T(8,128)(2,1)S(1)}, u32[]{:S(2)}, u32[]{:S(2)}) collective-permute-start(bf16[2,1,80,1280]{3,2,1,0:T(8,128)(2,1)S(1)} %slice.1529), channel_id=1, source_target_pairs={{0,8},{8,16},{16,24},{24,0},{1,9},{9,17},{17,25},{25,1},{2,10},{10... | collective-permute-start | bytes 1228808 | tf_op jit(solution)/shard_map/ppermute | solution.py:21
  138.8 30.9 %collective-permute-start.30 = (bf16[2,1,80,1280]{3,2,1,0:T(8,128)(2,1)S(1)}, bf16[2,1,80,1280]{3,2,1,0:T(8,128)(2,1)S(1)}, u32[]{:S(2)}, u32[]{:S(2)}) collective-permute-start(bf16[2,1,80,1280]{3,2,1,0:T(8,128)(2,1)S(1)} %slice.1533), channel_id=1, source_target_pairs={{0,6},{2,0},{4,2},{6,4},{1,7},{3,1},{5,3},{7,5},{8,14},{10,8},{12,... | collective-permute-start | bytes 1228808 | tf_op jit(solution)/shard_map/ppermute | solution.py:21
  144.6 25.6 %collective-permute-start.32 = (bf16[2,1,80,1280]{3,2,1,0:T(8,128)(2,1)S(1)}, bf16[2,1,80,1280]{3,2,1,0:T(8,128)(2,1)S(1)}, u32[]{:S(2)}, u32[]{:S(2)}) collective-permute-start(bf16[2,1,80,1280]{3,2,1,0:T(8,128)(2,1)S(1)} %slice.1534), channel_id=1, source_target_pairs={{0,2},{2,4},{4,6},{6,0},{1,3},{3,5},{5,7},{7,1},{8,10},{10,12},{12... | collective-permute-start | bytes 1228808 | tf_op jit(solution)/shard_map/ppermute | solution.py:21
  156.1 302.4 %collective-permute-start.96 = (bf16[128,320]{1,0:T(8,128)(2,1)}, bf16[128,320]{1,0:T(8,128)(2,1)}, u32[]{:S(2)}, u32[]{:S(2)}) collective-permute-start(bf16[128,320]{1,0:T(8,128)(2,1)} %bitcast.38), channel_id=1, source_target_pairs={{0,0},{2,8},{4,16},{6,24},{8,2},{10,10},{12,18},{14,26},{16,4},{18... | collective-permute-start | bytes 245768 | tf_op jit(solution)/shard_map/ppermute | solution.py:35
  159.1 33.5 %collective-permute-start.41 = (bf16[512,1280]{1,0:T(8,128)(2,1)S(1)}, bf16[512,1280]{1,0:T(8,128)(2,1)S(1)}, u32[]{:S(2)}, u32[]{:S(2)}) collective-permute-start(bf16[512,1280]{1,0:T(8,128)(2,1)S(1)} %pad_maximum_fusion.3), channel_id=1, source_target_pairs={{0,1},{1,0},{2,3},{3,2},{4,5},{5,4},{6,7},{7,6},{8,9},{9,8},{10,11... | collective-permute-start | bytes 3932168 | tf_op jit(solution)/shard_map/ppermute | solution.py:21
  224.8 20.9 %collective-permute-start.44 = (bf16[128,1280]{1,0:T(8,128)(2,1)S(1)}, bf16[128,1280]{1,0:T(8,128)(2,1)S(1)}, u32[]{:S(2)}, u32[]{:S(2)}) collective-permute-start(bf16[128,1280]{1,0:T(8,128)(2,1)S(1)} %add_convert_fusion.17), channel_id=1, source_target_pairs={{0,4},{2,6},{4,0},{6,2},{1,5},{3,7},{5,1},{7,3},{8,12},{10,14},{12... | collective-permute-start | bytes 983048 | tf_op jit(solution)/shard_map/ppermute | solution.py:21
  298.5 23.5 %collective-permute-start.60 = (bf16[128,1280]{1,0:T(8,128)(2,1)S(1)}, bf16[128,1280]{1,0:T(8,128)(2,1)S(1)}, u32[]{:S(2)}, u32[]{:S(2)}) collective-permute-start(bf16[128,1280]{1,0:T(8,128)(2,1)S(1)} %add_convert_fusion.15), channel_id=1, source_target_pairs={{0,4},{2,6},{4,0},{6,2},{1,5},{3,7},{5,1},{7,3},{8,12},{10,14},{12... | collective-permute-start | bytes 983048 | tf_op jit(solution)/shard_map/ppermute | solution.py:21
  378.1 22.2 %collective-permute-start.76 = (bf16[128,1280]{1,0:T(8,128)(2,1)S(1)}, bf16[128,1280]{1,0:T(8,128)(2,1)S(1)}, u32[]{:S(2)}, u32[]{:S(2)}) collective-permute-start(bf16[128,1280]{1,0:T(8,128)(2,1)S(1)} %add_convert_fusion.13), channel_id=1, source_target_pairs={{0,4},{2,6},{4,0},{6,2},{1,5},{3,7},{5,1},{7,3},{8,12},{10,14},{12... | collective-permute-start | bytes 983048 | tf_op jit(solution)/shard_map/ppermute | solution.py:21
  418.9 22.8 %collective-permute-start.88 = (bf16[128,1280]{1,0:T(8,128)(2,1)S(1)}, bf16[128,1280]{1,0:T(8,128)(2,1)S(1)}, u32[]{:S(2)}, u32[]{:S(2)}) collective-permute-start(bf16[128,1280]{1,0:T(8,128)(2,1)S(1)} %add_convert_fusion.12), channel_id=1, source_target_pairs={{0,16},{8,24},{16,0},{24,8},{1,17},{9,25},{17,1},{25,9},{2,18},{10... | collective-permute-start | bytes 983048 | tf_op jit(solution)/shard_map/ppermute | solution.py:21
  868.7 21.7 %collective-permute-start.149 = (bf16[256,1280]{1,0:T(8,128)(2,1)S(1)}, bf16[256,1280]{1,0:T(8,128)(2,1)S(1)}, u32[]{:S(2)}, u32[]{:S(2)}) collective-permute-start(bf16[256,1280]{1,0:T(8,128)(2,1)S(1)} %convert_element_type.1020), channel_id=1, source_target_pairs={{0,1},{1,0},{2,3},{3,2},{4,5},{5,4},{6,7},{7,6},{8,9},{9,8},{10,11... | collective-permute-start | bytes 1966088 | tf_op jit(solution)/shard_map/ppermute | solution.py:21
  876.0 60.4 %collective-permute-start.159 = (bf16[4,160,640]{2,1,0:T(8,128)(2,1)S(1)}, bf16[4,160,640]{2,1,0:T(8,128)(2,1)S(1)}, u32[]{:S(2)}, u32[]{:S(2)}) collective-permute-start(bf16[4,160,640]{2,1,0:T(8,128)(2,1)S(1)} %pad_maximum_fusion.22), channel_id=1, source_target_pairs={{0,6},{2,0},{4,2},{6,4},{1,7},{3,1},{5,3},{7,5},{8,14},{10,8},{12,... | collective-permute-start | bytes 2457608 | tf_op jit(solution)/shard_map/ppermute | solution.py:21
  877.2 59.2 %collective-permute-start.158 = (bf16[4,160,640]{2,1,0:T(8,128)(2,1)}, bf16[4,160,640]{2,1,0:T(8,128)(2,1)}, u32[]{:S(2)}, u32[]{:S(2)}) collective-permute-start(bf16[4,160,640]{2,1,0:T(8,128)(2,1)} %pad_maximum_fusion.21), channel_id=1, source_target_pairs={{0,2},{2,4},{4,6},{6,0},{1,3},{3,5},{5,7},{7,1},{8,10},{10,12},{12... | collective-permute-start | bytes 2457608 | tf_op jit(solution)/shard_map/ppermute | solution.py:21
  886.7 41.2 %collective-permute-start.161 = (bf16[4,160,640]{2,1,0:T(8,128)(2,1)}, bf16[4,160,640]{2,1,0:T(8,128)(2,1)}, u32[]{:S(2)}, u32[]{:S(2)}) collective-permute-start(bf16[4,160,640]{2,1,0:T(8,128)(2,1)} %pad_maximum_fusion.24), channel_id=1, source_target_pairs={{0,24},{8,0},{16,8},{24,16},{1,25},{9,1},{17,9},{25,17},{2,26},{10... | collective-permute-start | bytes 2457608 | tf_op jit(solution)/shard_map/ppermute | solution.py:21
  887.7 41.9 %collective-permute-start.160 = (bf16[4,160,640]{2,1,0:T(8,128)(2,1)}, bf16[4,160,640]{2,1,0:T(8,128)(2,1)}, u32[]{:S(2)}, u32[]{:S(2)}) collective-permute-start(bf16[4,160,640]{2,1,0:T(8,128)(2,1)} %pad_maximum_fusion.23), channel_id=1, source_target_pairs={{0,8},{8,16},{16,24},{24,0},{1,9},{9,17},{17,25},{25,1},{2,10},{10... | collective-permute-start | bytes 2457608 | tf_op jit(solution)/shard_map/ppermute | solution.py:21
  914.3 49.4 %collective-permute-start.154 = (bf16[512,1280]{1,0:T(8,128)(2,1)S(1)}, bf16[512,1280]{1,0:T(8,128)(2,1)S(1)}, u32[]{:S(2)}, u32[]{:S(2)}) collective-permute-start(bf16[512,1280]{1,0:T(8,128)(2,1)S(1)} %pad_maximum_fusion.17), channel_id=1, source_target_pairs={{0,1},{1,0},{2,3},{3,2},{4,5},{5,4},{6,7},{7,6},{8,9},{9,8},{10,11... | collective-permute-start | bytes 3932168 | tf_op jit(solution)/shard_map/ppermute | solution.py:21
  928.0 33.3 %collective-permute-start.164 = (bf16[640,640]{1,0:T(8,128)(2,1)S(1)}, bf16[640,640]{1,0:T(8,128)(2,1)S(1)}, u32[]{:S(2)}, u32[]{:S(2)}) collective-permute-start(bf16[640,640]{1,0:T(8,128)(2,1)S(1)} %broadcast_select_fusion.2), channel_id=1, source_target_pairs={{0,1},{1,0},{2,3},{3,2},{4,5},{5,4},{6,7},{7,6},{8,9},{9,8},{10,11... | collective-permute-start | bytes 2457608 | tf_op jit(solution)/shard_map/ppermute | solution.py:21
  937.9 25.5 %collective-permute-start.163 = (bf16[2,80,1280]{2,1,0:T(8,128)(2,1)S(1)}, bf16[2,80,1280]{2,1,0:T(8,128)(2,1)S(1)}, u32[]{:S(2)}, u32[]{:S(2)}) collective-permute-start(bf16[2,80,1280]{2,1,0:T(8,128)(2,1)S(1)} %get-tuple-element.342), channel_id=1, source_target_pairs={{0,6},{2,0},{4,2},{6,4},{1,7},{3,1},{5,3},{7,5},{8,14},{10,8},{12,... | collective-permute-start | bytes 1228808 | tf_op jit(solution)/shard_map/ppermute | solution.py:21
  938.0 25.4 %collective-permute-start.162 = (bf16[2,80,1280]{2,1,0:T(8,128)(2,1)S(1)}, bf16[2,80,1280]{2,1,0:T(8,128)(2,1)S(1)}, u32[]{:S(2)}, u32[]{:S(2)}) collective-permute-start(bf16[2,80,1280]{2,1,0:T(8,128)(2,1)S(1)} %get-tuple-element.341), channel_id=1, source_target_pairs={{0,2},{2,4},{4,6},{6,0},{1,3},{3,5},{5,7},{7,1},{8,10},{10,12},{12... | collective-permute-start | bytes 1228808 | tf_op jit(solution)/shard_map/ppermute | solution.py:21
  1002.9 21.0 %collective-permute-start.185 = (bf16[40,1280]{1,0:T(8,128)(2,1)S(1)}, bf16[40,1280]{1,0:T(8,128)(2,1)S(1)}, u32[]{:S(2)}, u32[]{:S(2)}) collective-permute-start(bf16[40,1280]{1,0:T(8,128)(2,1)S(1)} %select_convert_fusion.3), channel_id=1, source_target_pairs={{0,1},{1,0},{2,3},{3,2},{4,5},{5,4},{6,7},{7,6},{8,9},{9,8},{10,11... | collective-permute-start | bytes 307208 | tf_op jit(solution)/shard_map/ppermute | solution.py:21
  1009.0 28.8 %collective-permute-start.173 = (bf16[4,80,1408]{2,1,0:T(8,128)(2,1)S(1)}, bf16[4,80,1408]{2,1,0:T(8,128)(2,1)S(1)}, u32[]{:S(2)}, u32[]{:S(2)}) collective-permute-start(bf16[4,80,1408]{2,1,0:T(8,128)(2,1)S(1)} %pad_maximum_fusion.18), channel_id=1, source_target_pairs={{0,24},{8,0},{16,8},{24,16},{1,25},{9,1},{17,9},{25,17},{2,26},{10... | collective-permute-start | bytes 2703368 | tf_op jit(solution)/shard_map/ppermute | solution.py:21
  1010.4 27.5 %collective-permute-start.172 = (bf16[4,80,1408]{2,1,0:T(8,128)(2,1)S(1)}, bf16[4,80,1408]{2,1,0:T(8,128)(2,1)S(1)}, u32[]{:S(2)}, u32[]{:S(2)}) collective-permute-start(bf16[4,80,1408]{2,1,0:T(8,128)(2,1)S(1)} %maximum_maximum_fusion), channel_id=1, source_target_pairs={{0,8},{8,16},{16,24},{24,0},{1,9},{9,17},{17,25},{25,1},{2,10},{10... | collective-permute-start | bytes 2703368 | tf_op jit(solution)/shard_map/ppermute | solution.py:21
  (468 other events, 3669.5 us)
Sparse Core Ops, SparseCore 0:
  10.2 71.4 all-gather.5
  84.5 87.6 all-gather.3
  867.5 93.2 reduce-scatter.1

commit v2 on v1

--- a/solution.py
+++ b/solution.py
@@ -13,6 +13,7 @@
 MASKED = -1e30
 BF = jnp.bfloat16
 F32 = jnp.float32
+BLOCK = 256
 VMEM_LIMIT = 20 * 1024 * 1024
 
 
@@ -113,19 +114,6 @@
         return [whole.reshape(16 * rows, columns) for whole in wholes]
 
 
-def gathered_vectors(vectors):
-    count, width = vectors.shape
-    own = jnp.pad(vectors, ((0, 8 - count), (0, 128 - width)))
-    other = swapped(own)
-    core_zero = lax.axis_index("core") == 0
-    block = jnp.stack([picked(core_zero, own, other), picked(core_zero, other, own)])
-    rows = jnp.stack([block] + [fetched(block, "y", d) for d in (1, 2, 3)])
-    plane = jnp.stack([rows] + [fetched(rows, "dp", d) for d in (1, 2, 3)])
-    plane = jnp.roll(plane, (lax.axis_index("dp"), lax.axis_index("y")), (0, 1))
-    plane = plane[:, :, :, :count, :width].transpose(3, 0, 1, 2, 4)
-    return plane.reshape(count, -1).astype(F32)
-
-
 class Scatter:
     def __init__(self, wholes, big, small):
         self.big, self.small = big, small
@@ -315,6 +303,26 @@
         dkv_ref[:, 256 * pair + 128 : 256 * pair + 256] = mxu(do.T, probs.astype(BF)).T.astype(BF)
 
 
+def project_back_kernel(dq_ref, dkv_ref, w_q_ref, w_kv_ref, own_ref, away_ref):
+    rows = dq_ref.shape[0] // 2
+    half = dkv_ref.shape[0] // 2
+    for at in range(0, own_ref.shape[1], BLOCK):
+        columns = slice(at, at + BLOCK)
+        by_kv = mxu(dkv_ref[...], w_kv_ref[columns, :], NT)
+        by_q = mxu(dq_ref[...], w_q_ref[columns, :], NT)
+        own_ref[:rows, columns] = by_kv[:rows] + by_q[:rows]
+        own_ref[rows:, columns] = by_kv[rows:half]
+        away_ref[:rows, columns] = (by_kv[half : half + rows] + by_q[rows:]).astype(BF)
+        away_ref[rows:, columns] = by_kv[half + rows :].astype(BF)
+
+
+def project_back(dq, dkv, w_q, w_kv):
+    keys, width = dkv.shape
+    out_shape = [jax.ShapeDtypeStruct((keys // 2, width), kind) for kind in (F32, BF)]
+    flops = 2 * keys * width * width
+    return called(project_back_kernel, "project_back", out_shape, (dq, dkv, w_q, w_kv), flops, 0)
+
+
 def attend_back(q, kv, do, out, lse, mark_q, mark_k):
     queries, width = q.shape
     keys = kv.shape[0]
@@ -328,9 +336,6 @@
     phi = 0.5 * (1.0 + lax.erf(values * 0.7071067811865476))
     slope = phi + values * (0.3989422804014327 * jnp.exp(-0.5 * values * values))
     return values * phi, slope
-
-
-BLOCK = 256
 
 
 def feed_kernel(save, x_ref, up, down, out_ref, act_ref, *kept):
@@ -398,22 +403,53 @@
         self.hidden_other = swapped(hidden_low)
         normed = layer_norm(self.hidden, self.norms[0], self.norms[1]).astype(BF)
         self.normed = normed
-        self.fetched = [fetched(normed, self.ring, d) for d in (1, 2, 3)]
+        self.near = fetched(normed, self.ring, 1), fetched(normed, self.ring, 3)
+
+    def fetch_raw(self, earlier):
+        self.hidden_low = after(self.start, earlier)
+        self.hidden_other = swapped(self.hidden_low)
+        self.near = fetched(self.hidden_low, self.ring, 1), fetched(self.hidden_low, self.ring, 3)
+        self.fetch_far()
+
+    def collect_raw(self):
+        self.hidden = self.hidden_low.astype(F32)
+        plus, minus = self.near
+        ring_rows = jnp.concatenate([self.hidden_low, plus, *self.far, minus])
+        rows = jnp.concatenate([ring_rows, swapped(ring_rows)]).astype(F32)
+        self.normed_all = layer_norm(rows, self.norms[0], self.norms[1]).astype(BF)
+        half = 4 * self.rows
+        self.normed_chip = jnp.concatenate(
+            [self.normed_all[: self.rows], self.normed_all[half : half + self.rows]]
+        )
+
+    def swap_near(self):
+        plus, minus = self.near
+        self.other_near = swapped(jnp.concatenate([self.normed, plus, minus]))
+
+    def fetch_far(self):
+        plus, minus = self.near
+        half = self.rows // 2
+        self.far = fetched(plus[:half], self.ring, 1), fetched(minus[half:], self.ring, 3)
 
     def collect(self, earlier=None):
-        normed = self.normed
-        ring_rows = jnp.concatenate(after([normed] + self.fetched, earlier))
-        other_rows = swapped(ring_rows)
-        self.normed_all = jnp.concatenate([ring_rows, other_rows])
-        self.normed_chip = jnp.concatenate([normed, other_rows[: self.rows]])
-
-    def attention(self, weights, save, earlier):
+        rows, normed = self.rows, self.normed
+        plus, minus = self.near
+        two = jnp.concatenate(after(self.far, earlier))
+        other_near, other_two = self.other_near, swapped(two)
+        self.normed_all = jnp.concatenate(
+            [normed, plus, two, minus, other_near[: 2 * rows], other_two, other_near[2 * rows :]]
+        )
+        self.normed_chip = jnp.concatenate([normed, other_near[:rows]])
+
+    def project(self, weights, earlier):
         normed_all, normed_chip = after((self.normed_all, self.normed_chip), earlier)
         self.kv = dot(normed_all, weights["kv"]).astype(BF)
         self.q = dot(normed_chip, weights["q"]).astype(BF)
+
+    def attention(self, save):
         self.attended, *self.lse = attend(self.q, self.kv, *self.marks, save)
 
-    def feed_forward(self, weights, save, arrivals):
+    def feed_forward(self, weights, save, arrivals, between):
         rows = self.rows
         part = dot(self.attended, weights["out"])
         hidden = jnp.concatenate([self.hidden, self.hidden_other.astype(F32)])
@@ -421,7 +457,7 @@
         normed_ffn = layer_norm(self.middle, self.norms[2], self.norms[3]).astype(BF)
         self.normed_ffn = after(normed_ffn, arrivals)
         fed, self.act, *self.slope = feed(self.normed_ffn, *weights["feed"], save)
-        self.fed = fed
+        self.fed = fed = after(fed, between)
         self.result = (self.middle[:rows] + fed[:rows] + swapped(fed[rows:].astype(BF)).astype(F32)).astype(BF)
 
 
@@ -446,7 +482,7 @@
         self.grad_middle_low = grad_middle.astype(BF)
         self.grad_heads = dot(self.grad_middle_low, weights["out"], NT).astype(BF)
 
-    def attention(self, weights, earlier):
+    def attention(self, earlier):
         forward = self.forward
         grad_heads = after(self.grad_heads, earlier)
         self.dq, self.dkv = attend_back(
@@ -454,27 +490,41 @@
         )
 
     def project(self, weights, earlier=None):
+        dq, dkv = after((self.dq, self.dkv), earlier)
+        self.own, self.away = project_back(dq, dkv, weights["q"], weights["kv"])
+
+    def sum_cores(self, earlier=None):
         rows = self.rows
-        self.dq, self.dkv = after((self.dq, self.dkv), earlier)
-        grad_all = dot(self.dkv, weights["kv"], NT)
-        grad_chip = dot(self.dq, weights["q"], NT)
-        half = grad_all.shape[0] // 2
-        own = jnp.concatenate([grad_all[:rows] + grad_chip[:rows], grad_all[rows:half]])
-        away = jnp.concatenate([grad_all[half : half + rows] + grad_chip[rows:], grad_all[half + rows :]])
-        self.ring_grads = own + swapped(away.astype(BF)).astype(F32)
-
-    def spread(self):
-        rows = self.rows
-        self.pieces = [
-            moved(self.ring_grads[d * rows : (d + 1) * rows].astype(BF), self.forward.ring, d)
-            for d in (1, 2, 3)
+        own, away = after((self.own, self.away), earlier)
+        far = swapped(away[2 * rows : 3 * rows])
+        near = swapped(jnp.concatenate([away[: 2 * rows], away[3 * rows :]]))
+        self.ring_grads = [
+            own[d * rows : (d + 1) * rows] + part.astype(F32)
+            for d, part in enumerate((near[:rows], near[rows : 2 * rows], far, near[2 * rows :]))
         ]
+
+    def piece(self, steps, lower=0, upper=None):
+        return self.ring_grads[steps][lower : self.rows if upper is None else upper]
+
+    def spread_far(self):
+        half, ring = self.rows // 2, self.forward.ring
+        self.far = (
+            moved(self.piece(2, 0, half).astype(BF), ring, 1),
+            moved(self.piece(2, half).astype(BF), ring, -1),
+        )
+
+    def spread_near(self, earlier=None):
+        half, ring = self.rows // 2, self.forward.ring
+        from_left, from_right = after(self.far, earlier)
+        right = jnp.concatenate([self.piece(1, 0, half) + from_left.astype(F32), self.piece(1, half)])
+        left = jnp.concatenate([self.piece(3, 0, half), self.piece(3, half) + from_right.astype(F32)])
+        self.near = moved(right.astype(BF), ring, 1), moved(left.astype(BF), ring, -1)
 
     def reduce(self, earlier=None):
         forward = self.forward
-        grad_normed = self.ring_grads[: self.rows]
-        for piece in after(self.pieces, earlier):
-            grad_normed = grad_normed + piece.astype(F32)
+        grad_normed = self.piece(0)
+        for part in after(self.near, earlier):
+            grad_normed = grad_normed + part.astype(F32)
         part, unit = layer_norm_back(forward.hidden, forward.norms[0], grad_normed)
         self.grad_gain_attn = jnp.sum(grad_normed * unit, axis=0)
         self.grad_bias_attn = jnp.sum(grad_normed, axis=0)
@@ -499,7 +549,7 @@
     return jnp.concatenate([mark_q[:rows], mark_q[4 * rows : 5 * rows]]), mark_k
 
 
-def attention_shards(w_qkv, w_out, core_zero):
+def attention_shards(w_qkv, w_out, vectors, core_zero):
     width = w_out.shape[1]
     half = width // 2
 
@@ -511,6 +561,7 @@
             pieces.append(w_qkv[:, 2 * width + at : 2 * width + at + 128])
         pieces.append(w_qkv[:, half * core : half * core + half])
         pieces.append(w_out[:, half * core : half * core + half])
+        pieces.append(jnp.pad(vectors.T, ((0, 0), (0, 128 - vectors.shape[0]))))
         return jnp.concatenate(pieces, axis=1)
 
     both = exchanged_in(arranged(0), arranged(1), core_zero)
@@ -546,9 +597,10 @@
 
 def feed_grads(backs):
     forwards = [back.forward for back in backs]
-    down = summed([f.act for f in forwards], [back.grad_chip for back in backs])
-    up = summed([f.normed_ffn for f in forwards], [back.grad_up for back in backs])
-    return up.astype(BF), down.astype(BF)
+    down = summed([f.act for f in forwards], [back.grad_chip for back in backs]).astype(BF)
+    up = summed([f.normed_ffn for f in forwards], [back.grad_up for back in backs]).astype(BF)
+    down = down.reshape(16, 2, -1, down.shape[1]).transpose(1, 0, 2, 3).reshape(2, -1, down.shape[1])
+    return jnp.concatenate([up, down[0], down[1]], axis=1)
 
 
 def out_grads(backs, core_zero):
@@ -565,15 +617,15 @@
     return summed([back.forward.normed_chip for back in backs], [back.dq for back in backs]).astype(BF)
 
 
-def key_value_grads(backs):
-    return summed([back.forward.normed_all for back in backs], [back.dkv for back in backs]).astype(BF)
+def key_value_grads(backs, earlier):
+    dkv = after([back.dkv for back in backs], earlier)
+    return summed([back.forward.normed_all for back in backs], dkv).astype(BF)
 
 
 def vector_grads(backs):
     vectors = sum(back.vectors() for back in backs)
     vectors = jnp.pad(vectors, ((0, 128 - vectors.shape[0]), (0, 0))).astype(BF)
-    vectors = vectors.astype(F32) + swapped(vectors).astype(F32)
-    return vectors.astype(BF).T
+    return added(vectors, swapped(vectors)).T
 
 
 def exchanged_out(shard, core_zero):
@@ -631,30 +683,31 @@
 
     w_down_whole = lax.all_gather(w_down[0], ("dp", "y"), axis=0, tiled=True)
     w_up_whole = lax.all_gather(up_shard(w_up[0], core_zero), ("dp", "y"), axis=0, tiled=True)
-    kv_shard, rest_shard = attention_shards(w_qkv[0], w_out[0], core_zero)
+    vectors = jnp.concatenate([norm_attn_gain, norm_attn_bias, norm_ffn_gain, norm_ffn_bias])
+    kv_shard, rest_shard = attention_shards(w_qkv[0], w_out[0], vectors, core_zero)
     kv, rest = Gather([kv_shard], "dp", "y"), Gather([rest_shard], "y", "dp")
+    start = whole_features(block_input, section, 0)
+    passes = [Forward(start[m], rings[m], None, None) for m in range(2)]
     near = kv.neighbours() + rest.neighbours()
-    vectors = jnp.concatenate([norm_attn_gain, norm_attn_bias, norm_ffn_gain, norm_ffn_bias])
-    norms = gathered_vectors(after(vectors, near))
-    norms = tuple(norms[i : i + 1] for i in range(4))
-    start = whole_features(after(block_input, near), section, 0)
+    for now in passes:
+        now.fetch_raw(near)
     kv.along_first()
     rest.along_first()
     kv.along_second()
     rest.along_second()
-    passes = [Forward(start[m], rings[m], None, norms) for m in range(2)]
-    for now in passes:
-        now.norm()
     marks = (
         marks_of(cell_lengths[2 * at_x], at_y, rows, core),
         marks_of(cell_lengths[2 * at_y + 1], at_x, rows, core),
     )
-    for m, now in enumerate(passes):
-        now.marks = marks[m]
-        now.collect()
     (w_kv,) = kv.placed()
     (rest_whole,) = rest.placed()
-    weights = {"kv": w_kv, "q": rest_whole[:, :half], "out": out_rows(rest_whole[:, half:], core_zero)}
+    weights = {"kv": w_kv, "q": rest_whole[:, :half], "out": out_rows(rest_whole[:, half:width], core_zero)}
+    norms = rest_whole[:, width:].T[:4].astype(F32)
+    norms = tuple(norms[i : i + 1] for i in range(4))
+    last_grad = whole_features(after(cotangent, (w_kv, rest_whole)), section, sections - 1)
+    for m, now in enumerate(passes):
+        now.marks, now.norms = marks[m], norms
+        now.collect_raw()
     weights["feed"] = (w_up_whole, w_down_whole)
 
     forward_pairs = [(s, s + 1) for s in range(sections - 1)]
@@ -664,10 +717,16 @@
         for m in range(2):
             now, other = passes[m], passes[1 - m]
             waiting = step + m > 0 and not (final and m == 1)
-            now.attention(weights, final, result)
+            now.project(weights, result)
+            now.attention(final)
             if waiting:
                 other.norm(now.attended)
-            now.feed_forward(weights, final, other.fetched[::2] if waiting else None)
+                now.attended = after(now.attended, other.normed)
+                other.swap_near()
+                other.fetch_far()
+            now.feed_forward(
+                weights, final, other.near if waiting else last_grad, other.other_near if waiting else None
+            )
             if waiting:
                 other.collect(now.fed)
             result = now.result
@@ -676,7 +735,6 @@
                 passes[m] = Forward(start[m], rings[m], marks[m], norms, received)
     block_output = spread_features(jnp.stack([now.result for now in passes]), section, sections - 1)
 
-    last_grad = whole_features(cotangent, section, sections - 1)
     backs = [Backward(last_grad[m], passes[m]) for m in range(2)]
     backward_pairs = [(s + 1, s) for s in range(sections - 1)]
     earlier = result
@@ -685,59 +743,62 @@
         for m in range(2):
             now, other = backs[m], backs[1 - m]
             waiting = step + m > 0
-            now.feed_forward(weights, earlier, other.pieces[::2] if waiting else None)
+            if step == 1 and m == 0:
+                earlier = (earlier, block_output)
+            now.feed_forward(weights, earlier, other.far if waiting else None)
             if waiting:
-                other.reduce(now.grad_heads)
+                other.spread_near()
             if final and m == 1:
                 break
-            now.attention(weights, other.grad_hidden_low if waiting else None)
+            now.attention(None)
             if waiting:
+                other.reduce(now.dkv)
+                now.project(weights, other.grad_hidden_low)
                 received = lax.ppermute(other.grad_hidden_low, "section", backward_pairs)
-                received = after(received, now.dkv)
+                received = after(received, now.own)
                 grad_low = jnp.where(section == sections - 1, last_grad[1 - m], received)
-                now.project(weights, grad_low)
                 backs[1 - m] = Backward(grad_low, passes[1 - m])
+                now.sum_cores(grad_low)
             else:
                 now.project(weights)
-            now.spread()
+                now.sum_cores()
+            now.spread_far()
             earlier = now.ring_grads
 
-    arrived = backs[0].pieces
-    up_grad, down_grad = feed_grads(backs)
-    up_grads = lax.psum_scatter(up_grad, ("dp", "y"), scatter_dimension=0, tiled=True)
-    sum_zero = Scatter([after(down_grad[:, :half], arrived)], "y", "dp")
-    sum_one = Scatter([after(down_grad[:, half:], arrived)], "dp", "y")
-    far = sum_zero.far() + sum_one.far()
-    backs[1].attention(weights, (backs[0].grad_hidden_low, far))
-    near = sum_zero.near() + sum_one.near()
-    backs[1].project(weights, near)
-    backs[1].spread()
-    mine = sum_zero.bundle(), sum_one.bundle()
-    sum_kv = Scatter([key_value_grads(backs)], "y", "dp")
+    joint = feed_grads(backs)
+    backs[0].reduce()
+    backs[1].attention((backs[0].grad_hidden_low, joint))
+    joint = lax.psum_scatter(joint, ("dp", "y"), scatter_dimension=0, tiled=True).astype(F32)
+    backs[1].project(weights)
+    backs[1].sum_cores()
+    backs[1].spread_far()
+    backs[1].spread_near()
+    kv_part = key_value_grads(backs, backs[1].far)
     out_part = out_grads(backs, core_zero)
     query_part = query_grads(backs)
-    backs[1].reduce(mine)
+    backs[1].reduce((kv_part, query_part))
+    sum_kv = Scatter([after(kv_part, backs[1].near)], "y", "dp")
     sum_rest = Scatter([query_part, out_part, vector_grads(backs)], "dp", "y")
     sum_kv.far()
     sum_rest.far()
-    near = sum_kv.near(mine) + sum_rest.near(mine)
-    sum_zero.small_far()
-    sum_one.small_far()
-    mine = sum_kv.bundle(), sum_rest.bundle()
-    down_grads = [sum_zero.total(near), sum_one.total(near)]
+    sum_kv.near()
+    sum_rest.near()
+    mine = sum_kv.bundle()
+    sum_rest.bundle()
     input_grad = spread_features(
-        after(jnp.stack([now.grad_hidden_low for now in backs]), near), section, 0
+        after(jnp.stack([now.grad_hidden_low for now in backs]), mine), section, 0
     ).astype(F32)
     sum_kv.small_far()
     sum_rest.small_far()
     kv_grads = sum_kv.total()
     rest_grads = sum_rest.total()
+    up_grads = joint[:, : 2 * width]
+    grad_down = jnp.concatenate([joint[:, 2 * width : 3 * width], joint[:, 3 * width :]])
 
     own_rows = w_out.shape[1]
-    units = jnp.stack(exchanged_out(up_grads.astype(F32), core_zero), axis=1)
+    units = jnp.stack(exchanged_out(up_grads, core_zero), axis=1)
     units = units.reshape(own_rows, 2, 16, -1).transpose(0, 2, 1, 3)
     grad_up = units.reshape(own_rows, -1)
-    grad_down = jnp.concatenate(down_grads, axis=1)
     kv_cores = exchanged_out(kv_grads, core_zero)
     rest_cores = exchanged_out(rest_grads[:, :width], core_zero)
     keys, values = [], []

time: 1100 us -> 976 us (0.89)
  waiting for transfers between devices: 300 us -> 223 us
  matrix products: 111 us -> 66.1 us
  Pallas kernels: 158 us -> 191 us
  local copies, waits for them, and re-layouts: 122 us -> 108 us
    ppermute x167 -> x174, waiting for transfers between devices: 271 us -> 182 us  [moved(): lax.ppermute(value, axis, [(i, (i + steps) % count) for i in range(count)])]
    dot_general x53 -> x37, matrix products: 111 us -> 66.1 us  [dot(): return lax.dot_general(left, right, dims, preferred_element_type=F32)]
    pallas_call x32 -> x40, Pallas kernels: 146 us -> 182 us  [called(): pl.pallas_call(kernel, out_shape=out_shape, in_specs=[whole()] * len(oper...]
    ppermute x6, waiting for transfers between devices: 9.98 us -> 26.1 us  [local(): received = lax.ppermute(other.grad_hidden_low, 'section', backward_pairs)]
    ppermute x167 -> x174, starting transfers between devices: 219 us -> 206 us  [moved(): lax.ppermute(value, axis, [(i, (i + steps) % count) for i in range(count)])]
    unnamed x666 -> x483, local copies, waits for them, and re-layouts: 66.5 us -> 57.6 us
  transfers between devices with their start and end apart: 198 -> 205, of which waited for: 89 -> 74; matrix products, arithmetic and copies ran while one was open for 20% -> 21% of each run, Pallas kernels for 14% -> 19%
where the time goes in v2:
time: 976 us; the launch traced here: 963 us
  starting transfers between devices  266 us (27%)
  waiting for transfers between devices  223 us (23%)
  Pallas kernels  191 us (20%)
  local copies, waits for them, and re-layouts  108 us (11%)
  other arithmetic  88.8 us (9%)
  matrix products  66.1 us (7%)
  between operations  20.2 us (2%)
    ppermute x174, starting transfers between devices, moved(): lax.ppermute(value, axis, [(i, (i + steps) % count) for i in range(count)])  206 us
    ppermute x174, waiting for transfers between devices, moved(): lax.ppermute(value, axis, [(i, (i + steps) % count) for i in range(count)])  182 us
    pallas_call x40, Pallas kernels, called(): pl.pallas_call(kernel, out_shape=out_shape, in_specs=[whole()] * len(oper...  182 us
    dot_general x37, matrix products, dot(): return lax.dot_general(left, right, dims, preferred_element_type=F32)  66.1 us
    unnamed x483, local copies, waits for them, and re-layouts  57.6 us
    ppermute x6, waiting for transfers between devices, local(): received = lax.ppermute(other.grad_hidden_low, 'section', backward_pairs)  26.1 us
  transfers between devices with their start and end apart: 205, of which 74 were waited for; matrix products, arithmetic and copies ran while one was open for 21% of the time, Pallas kernels for 19%

profile of v2, /device:TPU:23, one launch (start us, length us, event | category | flops | bytes accessed | tf_op | source)
XLA Modules:
  0.0 963.1 jit_solution(2192047598168298406)
XLA Ops:
  56.6 17.8 %collective-permute-done.15 = bf16[1,80,640]{2,1,0:T(8,128)(2,1)S(1)} collective-permute-done((bf16[1,80,640]{2,1,0:T(8,128)(2,1)S(1)}, bf16[1,80,640]{2,1,0:T(8,128)(2,1)S(1)}, u32[]{:S(2)}, u32[]{:S(2)}) %collective-permute-start.15) | collective-permute-done | bytes 102432 | tf_op jit(solution)/shard_map/ppermute | solution.py:22
  83.0 13.8 %collective-permute-start.37 = (bf16[64,1280]{1,0:T(8,128)(2,1)S(1)}, bf16[64,1280]{1,0:T(8,128)(2,1)S(1)}, u32[]{:S(2)}, u32[]{:S(2)}) collective-permute-start(bf16[64,1280]{1,0:T(8,128)(2,1)S(1)} %slice.1744), channel_id=1, source_target_pairs={{0,24},{8,0},{16,8},{24,16},{1,25},{9,1},{17,9},{25,17},{2,26},{10... | collective-permute-start | bytes 491528 | tf_op jit(solution)/shard_map/ppermute | solution.py:22
  98.4 7.0 collective-permute-done.37
  112.0 6.1 collective-permute-done.11
  118.8 7.6 collective-permute-start.40
  132.4 8.4 collective-permute-done.24.refs_2_
  245.6 5.3 collective-permute-done.44
  284.1 5.5 collective-permute-done.53
  300.8 6.5 collective-permute-start.57
  356.3 5.2 collective-permute-done.73
  426.4 5.2 collective-permute-done.93
  486.2 7.1 attend_back.8
  518.0 7.1 attend_back.9
  557.5 7.1 attend_back.10
  570.8 5.4 collective-permute-done.126
  592.9 7.1 attend_back.11
  606.1 5.4 collective-permute-done.135
  631.9 7.1 attend_back.12
  645.1 5.3 collective-permute-done.144
  667.6 7.1 attend_back.13
  680.8 5.4 collective-permute-done.153
  707.9 7.1 attend_back.14
  744.5 5.3 fusion.209
  764.6 6.8 pad_maximum_fusion
  779.3 6.9 attend_back.15
  800.8 5.7 collective-permute-done.173
  811.6 7.5 convolution_convert_fusion.2
  823.8 4.8 collective-permute-done.176
  849.2 4.9 collective-permute-done.179
  865.2 10.0 %collective-permute-done.180 = bf16[4,80,1280]{2,1,0:T(8,128)(2,1)S(1)} collective-permute-done((bf16[4,80,1280]{2,1,0:T(8,128)(2,1)S(1)}, bf16[4,80,1280]{2,1,0:T(8,128)(2,1)S(1)}, u32[]{:S(2)}, u32[]{:S(2)}) %collective-permute-start.180) | collective-permute-done | bytes 819232 | tf_op jit(solution)/shard_map/ppermute | solution.py:22
  883.3 14.9 %collective-permute-done.198 = bf16[80,640]{1,0:T(8,128)(2,1)S(1)} collective-permute-done((bf16[80,640]{1,0:T(8,128)(2,1)S(1)}, bf16[80,640]{1,0:T(8,128)(2,1)S(1)}, u32[]{:S(2)}, u32[]{:S(2)}) %collective-permute-start.198) | collective-permute-done | bytes 102432 | tf_op jit(solution)/shard_map/ppermute | solution.py:22
  935.9 7.5 collective-permute-done.194
  (1441 shorter events, 709.1 us)
Async XLA Ops:
  7.2 207.3 %all-gather.6.cloned.1.call-start = ((), (), s32[]{:S(2)}) async-start(), calls=%async_computation.3 | async-start | bytes 6963200 | tf_op jit(solution)/shard_map/all_gather | solution.py:684
  7.9 206.5 %all-gather.4.cloned.1.call-start = ((), (), s32[]{:S(2)}) async-start(), calls=%async_computation.1 | async-start | bytes 6963200 | tf_op jit(solution)/shard_map/all_gather | solution.py:685
  33.7 914.8 %reduce-scatter.2.cloned.1.call-start = ((), (), s32[]{:S(2)}) async-start(), calls=%async_computation.2 | async-start | bytes 13926400 | tf_op jit(solution)/shard_map/reduce_scatter | solution.py:771
  49.9 27.3 %collective-permute-start.36 = (bf16[128,1280]{1,0:T(8,128)(2,1)S(1)}, bf16[128,1280]{1,0:T(8,128)(2,1)S(1)}, u32[]{:S(2)}, u32[]{:S(2)}) collective-permute-start(bf16[128,1280]{1,0:T(8,128)(2,1)S(1)} %get-tuple-element.191), channel_id=1, source_target_pairs={{0,24},{8,0},{16,8},{24,16},{1,25},{9,1},{17,9},{25,17},{2,26},{10... | collective-permute-start | bytes 983048 | tf_op jit(solution)/shard_map/ppermute | solution.py:22
  49.9 28.9 %collective-permute-start.38 = (bf16[128,1280]{1,0:T(8,128)(2,1)S(1)}, bf16[128,1280]{1,0:T(8,128)(2,1)S(1)}, u32[]{:S(2)}, u32[]{:S(2)}) collective-permute-start(bf16[128,1280]{1,0:T(8,128)(2,1)S(1)} %get-tuple-element.191), channel_id=1, source_target_pairs={{0,8},{8,16},{16,24},{24,0},{1,9},{9,17},{17,25},{25,1},{2,10},{10... | collective-permute-start | bytes 983048 | tf_op jit(solution)/shard_map/ppermute | solution.py:22
  53.3 25.5 %collective-permute-start.10 = (bf16[128,1280]{1,0:T(8,128)(2,1)S(1)}, bf16[128,1280]{1,0:T(8,128)(2,1)S(1)}, u32[]{:S(2)}, u32[]{:S(2)}) collective-permute-start(bf16[128,1280]{1,0:T(8,128)(2,1)S(1)} %get-tuple-element.187), channel_id=1, source_target_pairs={{0,6},{2,0},{4,2},{6,4},{1,7},{3,1},{5,3},{7,5},{8,14},{10,8},{12,... | collective-permute-start | bytes 983048 | tf_op jit(solution)/shard_map/ppermute | solution.py:22
  54.6 22.4 %collective-permute-start.16 = (bf16[1,80,768]{2,1,0:T(8,128)(2,1)S(1)}, bf16[1,80,768]{2,1,0:T(8,128)(2,1)S(1)}, u32[]{:S(2)}, u32[]{:S(2)}) collective-permute-start(bf16[1,80,768]{2,1,0:T(8,128)(2,1)S(1)} %slice.1715), channel_id=1, source_target_pairs={{0,2},{2,4},{4,6},{6,0},{1,3},{3,5},{5,7},{7,1},{8,10},{10,12},{12... | collective-permute-start | bytes 368648 | tf_op jit(solution)/shard_map/ppermute | solution.py:22
  77.0 41.8 %collective-permute-start.23 = (bf16[4,1,80,1280]{3,2,1,0:T(8,128)(2,1)S(1)}, bf16[4,1,80,1280]{3,2,1,0:T(8,128)(2,1)S(1)}, u32[]{:S(2)}, u32[]{:S(2)}) collective-permute-start(bf16[4,1,80,1280]{3,2,1,0:T(8,128)(2,1)S(1)} %pad_maximum_fusion.19.refs_0_), channel_id=1, source_target_pairs={{0,6},{2,0},{4,2},{6,4},{1,7},{3,1},{5,3},{7,5},{8,14},{10,8},{12,... | collective-permute-start | bytes 2457608 | tf_op jit(solution)/shard_map/ppermute | solution.py:22
  77.2 49.3 %collective-permute-start.25 = (bf16[4,1,80,1280]{3,2,1,0:T(8,128)(2,1)S(1)}, bf16[4,1,80,1280]{3,2,1,0:T(8,128)(2,1)S(1)}, u32[]{:S(2)}, u32[]{:S(2)}) collective-permute-start(bf16[4,1,80,1280]{3,2,1,0:T(8,128)(2,1)S(1)} %pad_maximum_fusion.19.refs_0_), channel_id=1, source_target_pairs={{0,2},{2,4},{4,6},{6,0},{1,3},{3,5},{5,7},{7,1},{8,10},{10,12},{12... | collective-permute-start | bytes 2457608 | tf_op jit(solution)/shard_map/ppermute | solution.py:22
  78.7 47.9 %collective-permute-start.17 = (bf16[4,1,80,1408]{3,2,1,0:T(8,128)(2,1)S(1)}, bf16[4,1,80,1408]{3,2,1,0:T(8,128)(2,1)S(1)}, u32[]{:S(2)}, u32[]{:S(2)}) collective-permute-start(bf16[4,1,80,1408]{3,2,1,0:T(8,128)(2,1)S(1)} %pad_maximum_fusion.17.refs_0_), channel_id=1, source_target_pairs={{0,24},{8,0},{16,8},{24,16},{1,25},{9,1},{17,9},{25,17},{2,26},{10... | collective-permute-start | bytes 2703368 | tf_op jit(solution)/shard_map/ppermute | solution.py:22
  78.8 49.3 %collective-permute-start.19 = (bf16[4,1,80,1408]{3,2,1,0:T(8,128)(2,1)S(1)}, bf16[4,1,80,1408]{3,2,1,0:T(8,128)(2,1)S(1)}, u32[]{:S(2)}, u32[]{:S(2)}) collective-permute-start(bf16[4,1,80,1408]{3,2,1,0:T(8,128)(2,1)S(1)} %pad_maximum_fusion.17.refs_0_), channel_id=1, source_target_pairs={{0,8},{8,16},{16,24},{24,0},{1,9},{9,17},{17,25},{25,1},{2,10},{10... | collective-permute-start | bytes 2703368 | tf_op jit(solution)/shard_map/ppermute | solution.py:22
  83.0 22.3 %collective-permute-start.37 = (bf16[64,1280]{1,0:T(8,128)(2,1)S(1)}, bf16[64,1280]{1,0:T(8,128)(2,1)S(1)}, u32[]{:S(2)}, u32[]{:S(2)}) collective-permute-start(bf16[64,1280]{1,0:T(8,128)(2,1)S(1)} %slice.1744), channel_id=1, source_target_pairs={{0,24},{8,0},{16,8},{24,16},{1,25},{9,1},{17,9},{25,17},{2,26},{10... | collective-permute-start | bytes 491528 | tf_op jit(solution)/shard_map/ppermute | solution.py:22
  118.8 42.8 %collective-permute-start.40 = (bf16[512,1280]{1,0:T(8,128)(2,1)}, bf16[512,1280]{1,0:T(8,128)(2,1)}, u32[]{:S(2)}, u32[]{:S(2)}) collective-permute-start(bf16[512,1280]{1,0:T(8,128)(2,1)} %get-tuple-element.710), channel_id=1, source_target_pairs={{0,1},{1,0},{2,3},{3,2},{4,5},{5,4},{6,7},{7,6},{8,9},{9,8},{10,11... | collective-permute-start | bytes 3932168 | tf_op jit(solution)/shard_map/ppermute | solution.py:22
  128.1 19.8 %collective-permute-start.18 = (bf16[2,1,80,1408]{3,2,1,0:T(8,128)(2,1)S(1)}, bf16[2,1,80,1408]{3,2,1,0:T(8,128)(2,1)S(1)}, u32[]{:S(2)}, u32[]{:S(2)}) collective-permute-start(bf16[2,1,80,1408]{3,2,1,0:T(8,128)(2,1)S(1)} %slice.1716), channel_id=1, source_target_pairs={{0,24},{8,0},{16,8},{24,16},{1,25},{9,1},{17,9},{25,17},{2,26},{10... | collective-permute-start | bytes 1351688 | tf_op jit(solution)/shard_map/ppermute | solution.py:22
  140.9 26.7 %collective-permute-start.14 = (bf16[512,1280]{1,0:T(8,128)(2,1)}, bf16[512,1280]{1,0:T(8,128)(2,1)}, u32[]{:S(2)}, u32[]{:S(2)}) collective-permute-start(bf16[512,1280]{1,0:T(8,128)(2,1)} %get-tuple-element.716), channel_id=1, source_target_pairs={{0,1},{1,0},{2,3},{3,2},{4,5},{5,4},{6,7},{7,6},{8,9},{9,8},{10,11... | collective-permute-start | bytes 3932168 | tf_op jit(solution)/shard_map/ppermute | solution.py:22
  156.5 26.1 %collective-permute-start.27 = (bf16[640,640]{1,0:T(8,128)(2,1)}, bf16[640,640]{1,0:T(8,128)(2,1)}, u32[]{:S(2)}, u32[]{:S(2)}) collective-permute-start(bf16[640,640]{1,0:T(8,128)(2,1)} %broadcast_select_fusion.6), channel_id=1, source_target_pairs={{0,1},{1,0},{2,3},{3,2},{4,5},{5,4},{6,7},{7,6},{8,9},{9,8},{10,11... | collective-permute-start | bytes 2457608 | tf_op jit(solution)/shard_map/ppermute | solution.py:22
  186.1 23.2 %collective-permute-start.28 = (bf16[256,1280]{1,0:T(8,128)(2,1)}, bf16[256,1280]{1,0:T(8,128)(2,1)}, u32[]{:S(2)}, u32[]{:S(2)}) collective-permute-start(bf16[256,1280]{1,0:T(8,128)(2,1)} %get-tuple-element.792), channel_id=1, source_target_pairs={{0,1},{1,0},{2,3},{3,2},{4,5},{5,4},{6,7},{7,6},{8,9},{9,8},{10,11... | collective-permute-start | bytes 1966088 | tf_op jit(solution)/shard_map/ppermute | solution.py:22
  245.2 38.7 %collective-permute-start.41 = (bf16[128,1280]{1,0:T(8,128)(2,1)S(1)}, bf16[128,1280]{1,0:T(8,128)(2,1)S(1)}, u32[]{:S(2)}, u32[]{:S(2)}) collective-permute-start(bf16[128,1280]{1,0:T(8,128)(2,1)S(1)} %get-tuple-element.514), channel_id=1, source_target_pairs={{0,1},{1,0},{2,3},{3,2},{4,5},{5,4},{6,7},{7,6},{8,9},{9,8},{10,11... | collective-permute-start | bytes 983048 | tf_op jit(solution)/shard_map/ppermute | solution.py:22
  284.0 37.2 %collective-permute-start.66 = (bf16[128,1280]{1,0:T(8,128)(2,1)S(1)}, bf16[128,1280]{1,0:T(8,128)(2,1)S(1)}, u32[]{:S(2)}, u32[]{:S(2)}) collective-permute-start(bf16[128,1280]{1,0:T(8,128)(2,1)S(1)} %get-tuple-element.510), channel_id=1, source_target_pairs={{0,1},{1,0},{2,3},{3,2},{4,5},{5,4},{6,7},{7,6},{8,9},{9,8},{10,11... | collective-permute-start | bytes 983048 | tf_op jit(solution)/shard_map/ppermute | solution.py:22
  321.3 35.0 %collective-permute-start.61 = (bf16[128,1280]{1,0:T(8,128)(2,1)S(1)}, bf16[128,1280]{1,0:T(8,128)(2,1)S(1)}, u32[]{:S(2)}, u32[]{:S(2)}) collective-permute-start(bf16[128,1280]{1,0:T(8,128)(2,1)S(1)} %get-tuple-element.502), channel_id=1, source_target_pairs={{0,1},{1,0},{2,3},{3,2},{4,5},{5,4},{6,7},{7,6},{8,9},{9,8},{10,11... | collective-permute-start | bytes 983048 | tf_op jit(solution)/shard_map/ppermute | solution.py:22
  478.0 20.4 %collective-permute-start.105 = (bf16[2,128,320]{2,1,0:T(8,128)(2,1)S(1)}, bf16[2,128,320]{2,1,0:T(8,128)(2,1)S(1)}, u32[]{:S(2)}, u32[]{:S(2)}) collective-permute-start(bf16[2,128,320]{2,1,0:T(8,128)(2,1)S(1)} %get-tuple-element.643), channel_id=1, source_target_pairs={{96,64},{97,65},{98,66},{99,67},{100,68},{101,69},{102,70},{103,71... | collective-permute-start | bytes 491528 | tf_op jit(solution)/shard_map/ppermute | solution.py:655
  478.8 19.6 %collective-permute-start.103 = (bf16[2,128,320]{2,1,0:T(8,128)(2,1)S(1)}, bf16[2,128,320]{2,1,0:T(8,128)(2,1)S(1)}, u32[]{:S(2)}, u32[]{:S(2)}) collective-permute-start(bf16[2,128,320]{2,1,0:T(8,128)(2,1)S(1)} %get-tuple-element.642), channel_id=1, source_target_pairs={{96,0},{97,1},{98,2},{99,3},{100,4},{101,5},{102,6},{103,7},{104,8... | collective-permute-start | bytes 491528 | tf_op jit(solution)/shard_map/ppermute | solution.py:655
  694.5 20.6 %collective-permute-start.160 = (bf16[128,1280]{1,0:T(8,128)(2,1)S(1)}, bf16[128,1280]{1,0:T(8,128)(2,1)S(1)}, u32[]{:S(2)}, u32[]{:S(2)}) collective-permute-start(bf16[128,1280]{1,0:T(8,128)(2,1)S(1)} %pad_maximum_fusion.57), channel_id=1, source_target_pairs={{0,8},{8,16},{16,24},{24,0},{1,9},{9,17},{17,25},{25,1},{2,10},{10... | collective-permute-start | bytes 983048 | tf_op jit(solution)/shard_map/ppermute | solution.py:22
  829.8 19.3 %collective-permute-start.177 = (bf16[2,80,1280]{2,1,0:T(8,128)(2,1)}, bf16[2,80,1280]{2,1,0:T(8,128)(2,1)}, u32[]{:S(2)}, u32[]{:S(2)}) collective-permute-start(bf16[2,80,1280]{2,1,0:T(8,128)(2,1)} %get-tuple-element.551), channel_id=1, source_target_pairs={{0,2},{2,4},{4,6},{6,0},{1,3},{3,5},{5,7},{7,1},{8,10},{10,12},{12... | collective-permute-start | bytes 1228808 | tf_op jit(solution)/shard_map/ppermute | solution.py:22
  831.9 22.1 %collective-permute-start.179 = (bf16[2,80,1280]{2,1,0:T(8,128)(2,1)}, bf16[2,80,1280]{2,1,0:T(8,128)(2,1)}, u32[]{:S(2)}, u32[]{:S(2)}) collective-permute-start(bf16[2,80,1280]{2,1,0:T(8,128)(2,1)} %get-tuple-element.553), channel_id=1, source_target_pairs={{0,6},{2,0},{4,2},{6,4},{1,7},{3,1},{5,3},{7,5},{8,14},{10,8},{12,... | collective-permute-start | bytes 1228808 | tf_op jit(solution)/shard_map/ppermute | solution.py:22
  855.5 19.6 %collective-permute-start.180 = (bf16[4,80,1280]{2,1,0:T(8,128)(2,1)S(1)}, bf16[4,80,1280]{2,1,0:T(8,128)(2,1)S(1)}, u32[]{:S(2)}, u32[]{:S(2)}) collective-permute-start(bf16[4,80,1280]{2,1,0:T(8,128)(2,1)S(1)} %pad_maximum_fusion.21), channel_id=1, source_target_pairs={{0,6},{2,0},{4,2},{6,4},{1,7},{3,1},{5,3},{7,5},{8,14},{10,8},{12,... | collective-permute-start | bytes 2457608 | tf_op jit(solution)/shard_map/ppermute | solution.py:22
  855.7 19.4 %collective-permute-start.178 = (bf16[4,80,1280]{2,1,0:T(8,128)(2,1)S(1)}, bf16[4,80,1280]{2,1,0:T(8,128)(2,1)S(1)}, u32[]{:S(2)}, u32[]{:S(2)}) collective-permute-start(bf16[4,80,1280]{2,1,0:T(8,128)(2,1)S(1)} %pad_maximum_fusion.20), channel_id=1, source_target_pairs={{0,2},{2,4},{4,6},{6,0},{1,3},{3,5},{5,7},{7,1},{8,10},{10,12},{12... | collective-permute-start | bytes 2457608 | tf_op jit(solution)/shard_map/ppermute | solution.py:22
  861.4 57.4 %collective-permute-start.190 = (bf16[4,80,1408]{2,1,0:T(8,128)(2,1)}, bf16[4,80,1408]{2,1,0:T(8,128)(2,1)S(1)}, u32[]{:S(2)}, u32[]{:S(2)}) collective-permute-start(bf16[4,80,1408]{2,1,0:T(8,128)(2,1)} %pad_maximum_fusion.18), channel_id=1, source_target_pairs={{0,24},{8,0},{16,8},{24,16},{1,25},{9,1},{17,9},{25,17},{2,26},{10... | collective-permute-start | bytes 2703368 | tf_op jit(solution)/shard_map/ppermute | solution.py:22
  862.5 56.3 %collective-permute-start.188 = (bf16[4,80,1408]{2,1,0:T(8,128)(2,1)}, bf16[4,80,1408]{2,1,0:T(8,128)(2,1)}, u32[]{:S(2)}, u32[]{:S(2)}) collective-permute-start(bf16[4,80,1408]{2,1,0:T(8,128)(2,1)} %maximum_maximum_fusion), channel_id=1, source_target_pairs={{0,8},{8,16},{16,24},{24,0},{1,9},{9,17},{17,25},{25,1},{2,10},{10... | collective-permute-start | bytes 2703368 | tf_op jit(solution)/shard_map/ppermute | solution.py:22
  876.7 21.5 %collective-permute-start.198 = (bf16[80,640]{1,0:T(8,128)(2,1)S(1)}, bf16[80,640]{1,0:T(8,128)(2,1)S(1)}, u32[]{:S(2)}, u32[]{:S(2)}) collective-permute-start(bf16[80,640]{1,0:T(8,128)(2,1)S(1)} %get-tuple-element.753), channel_id=1, source_target_pairs={{0,24},{8,0},{16,8},{24,16},{1,25},{9,1},{17,9},{25,17},{2,26},{10... | collective-permute-start | bytes 307208 | tf_op jit(solution)/shard_map/ppermute | solution.py:22
  877.9 29.9 %collective-permute-start.183 = (bf16[2,128,320]{2,1,0:T(8,128)(2,1)S(1)}, bf16[2,128,320]{2,1,0:T(8,128)(2,1)S(1)}, u32[]{:S(2)}, u32[]{:S(2)}) collective-permute-start(bf16[2,128,320]{2,1,0:T(8,128)(2,1)S(1)} %get-tuple-element.621), channel_id=1, source_target_pairs={{0,96},{1,97},{2,98},{3,99},{4,100},{5,101},{6,102},{7,103},{8,104... | collective-permute-start | bytes 491528 | tf_op jit(solution)/shard_map/ppermute | solution.py:655
  879.4 28.4 %collective-permute-start.182 = (bf16[2,128,320]{2,1,0:T(8,128)(2,1)S(1)}, bf16[2,128,320]{2,1,0:T(8,128)(2,1)S(1)}, u32[]{:S(2)}, u32[]{:S(2)}) collective-permute-start(bf16[2,128,320]{2,1,0:T(8,128)(2,1)S(1)} %get-tuple-element.622), channel_id=1, source_target_pairs={{0,64},{1,65},{2,66},{3,67},{4,68},{5,69},{6,70},{7,71},{8,72},{9,... | collective-permute-start | bytes 491528 | tf_op jit(solution)/shard_map/ppermute | solution.py:655
  (372 other events, 3115.1 us)
Sparse Core Ops, SparseCore 0:
  10.2 80.0 all-gather.5
  93.0 75.4 all-gather.3
  771.5 128.0 reduce-scatter.1

commit v3 on v2

--- a/solution.py
+++ b/solution.py
@@ -338,44 +338,50 @@
     return values * phi, slope
 
 
-def feed_kernel(save, x_ref, up, down, out_ref, act_ref, *kept):
+def feed_kernel(save, x_ref, joint, out_ref, act_ref, *kept):
     x = x_ref[...]
-    for at in range(0, up.shape[1], BLOCK):
+    width = out_ref.shape[1]
+    for at in range(0, 2 * width, BLOCK):
         columns = slice(at, at + BLOCK)
-        act, slope = gelu_and_slope(mxu(x, up[:, columns]))
+        act, slope = gelu_and_slope(mxu(x, joint[:, columns]))
         act_ref[:, columns] = act.astype(BF)
         if save:
             kept[0][:, columns] = slope.astype(BF)
-    for at in range(0, out_ref.shape[1], BLOCK):
-        columns = slice(at, at + BLOCK)
-        out_ref[:, columns] = mxu(act_ref[...], down[:, columns])
-
-
-def feed(x, up, down, save):
+    for at in range(0, width, BLOCK):
+        first, second = 2 * width + at, 3 * width + at
+        out_ref[:, at : at + BLOCK] = mxu(act_ref[:, :width], joint[:, first : first + BLOCK]) + mxu(
+            act_ref[:, width:], joint[:, second : second + BLOCK]
+        )
+
+
+def feed(x, joint, save):
     rows, width = x.shape
-    units = up.shape[1]
+    units = 2 * width
     kept = jax.ShapeDtypeStruct((rows, units), BF)
     out_shape = [jax.ShapeDtypeStruct((rows, width), F32), kept] + ([kept] if save else [])
     flops, exps = 4 * rows * width * units, 2 * rows * units
-    return called(functools.partial(feed_kernel, save), "feed", out_shape, (x, up, down), flops, exps)
-
-
-def feed_back_kernel(g_ref, slope_ref, up, down, out_ref, grad_ref):
+    return called(functools.partial(feed_kernel, save), "feed", out_shape, (x, joint), flops, exps)
+
+
+def feed_back_kernel(g_ref, slope_ref, joint, out_ref, grad_ref):
     g = g_ref[...]
-    for at in range(0, down.shape[0], BLOCK):
+    width = out_ref.shape[1]
+    for half in range(2):
+        for at in range(0, width, BLOCK):
+            down = joint[at : at + BLOCK, (2 + half) * width : (3 + half) * width]
+            units = slice(half * width + at, half * width + at + BLOCK)
+            grad = mxu(g, down, NT) * slope_ref[:, units].astype(F32)
+            grad_ref[:, units] = grad.astype(BF)
+    for at in range(0, width, BLOCK):
         rows = slice(at, at + BLOCK)
-        grad = mxu(g, down[rows, :], NT) * slope_ref[:, rows].astype(F32)
-        grad_ref[:, rows] = grad.astype(BF)
-    for at in range(0, out_ref.shape[1], BLOCK):
-        rows = slice(at, at + BLOCK)
-        out_ref[:, rows] = mxu(grad_ref[...], up[rows, :], NT)
-
-
-def feed_back(g, slope, up, down):
+        out_ref[:, rows] = mxu(grad_ref[...], joint[rows, : 2 * width], NT)
+
+
+def feed_back(g, slope, joint):
     rows, width = g.shape
-    units = up.shape[1]
+    units = 2 * width
     out_shape = [jax.ShapeDtypeStruct((rows, width), F32), jax.ShapeDtypeStruct((rows, units), BF)]
-    return called(feed_back_kernel, "feed_back", out_shape, (g, slope, up, down), 4 * rows * width * units, 0)
+    return called(feed_back_kernel, "feed_back", out_shape, (g, slope, joint), 4 * rows * width * units, 0)
 
 
 def dot(left, right, dims=NN):
@@ -456,7 +462,7 @@
         self.middle = hidden + part + from_other(part)
         normed_ffn = layer_norm(self.middle, self.norms[2], self.norms[3]).astype(BF)
         self.normed_ffn = after(normed_ffn, arrivals)
-        fed, self.act, *self.slope = feed(self.normed_ffn, *weights["feed"], save)
+        fed, self.act, *self.slope = feed(self.normed_ffn, weights["feed"], save)
         self.fed = fed = after(fed, between)
         self.result = (self.middle[:rows] + fed[:rows] + swapped(fed[rows:].astype(BF)).astype(F32)).astype(BF)
 
@@ -470,7 +476,7 @@
     def feed_forward(self, weights, earlier, arrivals):
         rows, forward = self.rows, self.forward
         grad_chip = after(self.grad_chip, earlier)
-        back, self.grad_up = feed_back(grad_chip, *forward.slope, *weights["feed"])
+        back, self.grad_up = feed_back(grad_chip, *forward.slope, weights["feed"])
         back = after(back, arrivals)
         grad_normed = back + from_other(back)
         gain = forward.norms[2]
@@ -549,22 +555,31 @@
     return jnp.concatenate([mark_q[:rows], mark_q[4 * rows : 5 * rows]]), mark_k
 
 
+def arrange_kernel(qkv_ref, out_ref, vectors_ref, mine_ref, other_ref):
+    width = out_ref.shape[1]
+    half = width // 2
+    core = lax.axis_index("core")
+    for at_core, target in ((core, mine_ref), (1 - core, other_ref)):
+        start = at_core * half
+
+        def columns(base, size):
+            return pl.ds(pl.multiple_of(start + base, 128), size)
+
+        for pair in range(half // 128):
+            target[:, 256 * pair : 256 * pair + 128] = qkv_ref[:, columns(width + 128 * pair, 128)]
+            target[:, 256 * pair + 128 : 256 * pair + 256] = qkv_ref[:, columns(2 * width + 128 * pair, 128)]
+        target[:, width : width + half] = qkv_ref[:, columns(0, half)]
+        target[:, width + half : 2 * width] = out_ref[:, columns(0, half)]
+        target[:, 2 * width :] = vectors_ref[...]
+
+
 def attention_shards(w_qkv, w_out, vectors, core_zero):
-    width = w_out.shape[1]
-    half = width // 2
-
-    def arranged(core):
-        pieces = []
-        for pair in range(half // 128):
-            at = half * core + 128 * pair
-            pieces.append(w_qkv[:, width + at : width + at + 128])
-            pieces.append(w_qkv[:, 2 * width + at : 2 * width + at + 128])
-        pieces.append(w_qkv[:, half * core : half * core + half])
-        pieces.append(w_out[:, half * core : half * core + half])
-        pieces.append(jnp.pad(vectors.T, ((0, 0), (0, 128 - vectors.shape[0]))))
-        return jnp.concatenate(pieces, axis=1)
-
-    both = exchanged_in(arranged(0), arranged(1), core_zero)
+    rows, width = w_out.shape
+    columns = jnp.pad(vectors.T, ((0, 0), (0, 128 - vectors.shape[0])))
+    out_shape = [jax.ShapeDtypeStruct((rows, 2 * width + 128), BF)] * 2
+    mine, other = called(arrange_kernel, "arrange", out_shape, (w_qkv, w_out, columns), 0, 0)
+    other = swapped(other)
+    both = jnp.concatenate([picked(core_zero, mine, other), picked(core_zero, other, mine)])
     return both[:, :width], both[:, width:]
 
 
@@ -574,10 +589,12 @@
     return jnp.concatenate([picked(core_zero, mine, other), picked(core_zero, other, mine)])
 
 
-def up_shard(w_up, core_zero):
+def feed_shard(w_up, w_down, core_zero):
     rows = w_up.shape[0]
-    units = w_up.reshape(rows, 16, 2, w_up.shape[1] // 32)
-    return exchanged_in(units[:, :, 0].reshape(rows, -1), units[:, :, 1].reshape(rows, -1), core_zero)
+    units = w_up.reshape(rows, 16, 2, 2, -1).transpose(2, 0, 3, 1, 4).reshape(2, rows, -1)
+    up = exchanged_in(units[0], units[1], core_zero)
+    half = w_down.shape[0] // 2
+    return jnp.concatenate([up, w_down[:half], w_down[half:]], axis=1)
 
 
 def out_rows(out_half, core_zero):
@@ -597,10 +614,12 @@
 
 def feed_grads(backs):
     forwards = [back.forward for back in backs]
-    down = summed([f.act for f in forwards], [back.grad_chip for back in backs]).astype(BF)
-    up = summed([f.normed_ffn for f in forwards], [back.grad_up for back in backs]).astype(BF)
-    down = down.reshape(16, 2, -1, down.shape[1]).transpose(1, 0, 2, 3).reshape(2, -1, down.shape[1])
-    return jnp.concatenate([up, down[0], down[1]], axis=1)
+    width = backs[0].grad_chip.shape[1]
+    up = summed([f.normed_ffn for f in forwards], [back.grad_up for back in backs])
+    act = jnp.concatenate([f.act for f in forwards])
+    grads = jnp.concatenate([back.grad_chip for back in backs])
+    down = [dot(act[:, h * width : (h + 1) * width], grads, TN) for h in range(2)]
+    return jnp.concatenate([up.astype(BF)] + [part.astype(BF) for part in down], axis=1)
 
 
 def out_grads(backs, core_zero):
@@ -636,25 +655,42 @@
     return picked(core_zero, mine, other), picked(core_zero, other, mine)
 
 
-def whole_features(shard, section, target):
-    both = jnp.stack([shard[0], transposed(shard[1])])
-    pieces = []
-    for z in range(4):
-        pieces.append(both if z == target else lax.ppermute(both, "section", [(z, target)]))
-    return jnp.concatenate(pieces, axis=2)
-
-
-def spread_features(both, section, source):
-    width = both.shape[2] // 4
-    total = None
-    for z in range(4):
-        piece = both[:, :, z * width : (z + 1) * width]
-        if z == source:
-            piece = jnp.where(section == source, piece, jnp.zeros_like(piece))
-        else:
-            piece = lax.ppermute(piece, "section", [(source, z)])
-        total = piece if total is None else total + piece
-    return jnp.stack([total[0], transposed(total[1])])
+SOURCES = ((1, 2), (2, 1), (3, 0))
+
+
+def whole_features(inputs, cotangents, section):
+    turned = transposed(jnp.stack([inputs[1], cotangents[1]]))
+    inputs = jnp.stack([inputs[0], turned[0]])
+    cotangents = jnp.stack([cotangents[0], turned[1]])
+    one, two, three = (
+        lax.ppermute(picked(section == a, inputs, cotangents), "section", [(a, 0), (b, 3)]) for a, b in SOURCES
+    )
+    start = jnp.concatenate([inputs, one, two, three], axis=2)
+    last = jnp.concatenate([three, two, one, cotangents], axis=2)
+    return start, last
+
+
+def spread_features(grads, outputs, section):
+    width = grads.shape[2] // 4
+
+    def piece(value, z):
+        return value[:, :, z * width : (z + 1) * width]
+
+    one, two, three = (
+        lax.ppermute(picked(section == 0, piece(grads, a), piece(outputs, b)), "section", [(0, a), (3, b)])
+        for a, b in SOURCES
+    )
+
+    def by_section(values):
+        result = values[3]
+        for z in range(3):
+            result = jnp.where(section == z, values[z], result)
+        return result
+
+    grads = by_section((piece(grads, 0), one, two, three))
+    outputs = by_section((three, two, one, piece(outputs, 3)))
+    turned = transposed(jnp.stack([grads[1], outputs[1]]))
+    return jnp.stack([grads[0], turned[0]]), jnp.stack([outputs[0], turned[1]])
 
 
 def local(
@@ -681,20 +717,19 @@
     width = w_out.shape[2]
     half = width // 2
 
-    w_down_whole = lax.all_gather(w_down[0], ("dp", "y"), axis=0, tiled=True)
-    w_up_whole = lax.all_gather(up_shard(w_up[0], core_zero), ("dp", "y"), axis=0, tiled=True)
+    feed_whole = lax.all_gather(feed_shard(w_up[0], w_down[0], core_zero), ("dp", "y"), axis=0, tiled=True)
     vectors = jnp.concatenate([norm_attn_gain, norm_attn_bias, norm_ffn_gain, norm_ffn_bias])
     kv_shard, rest_shard = attention_shards(w_qkv[0], w_out[0], vectors, core_zero)
     kv, rest = Gather([kv_shard], "dp", "y"), Gather([rest_shard], "y", "dp")
-    start = whole_features(block_input, section, 0)
+    start, last_grad = whole_features(block_input, cotangent, section)
     passes = [Forward(start[m], rings[m], None, None) for m in range(2)]
-    near = kv.neighbours() + rest.neighbours()
+    kv.neighbours((start, last_grad))
+    rest.neighbours((start, last_grad))
+    kv.along_first()
+    rest.along_first()
+    near = kv.along_second() + rest.along_second()
     for now in passes:
         now.fetch_raw(near)
-    kv.along_first()
-    rest.along_first()
-    kv.along_second()
-    rest.along_second()
     marks = (
         marks_of(cell_lengths[2 * at_x], at_y, rows, core),
         marks_of(cell_lengths[2 * at_y + 1], at_x, rows, core),
@@ -704,11 +739,10 @@
     weights = {"kv": w_kv, "q": rest_whole[:, :half], "out": out_rows(rest_whole[:, half:width], core_zero)}
     norms = rest_whole[:, width:].T[:4].astype(F32)
     norms = tuple(norms[i : i + 1] for i in range(4))
-    last_grad = whole_features(after(cotangent, (w_kv, rest_whole)), section, sections - 1)
     for m, now in enumerate(passes):
         now.marks, now.norms = marks[m], norms
         now.collect_raw()
-    weights["feed"] = (w_up_whole, w_down_whole)
+    weights["feed"] = feed_whole
 
     forward_pairs = [(s, s + 1) for s in range(sections - 1)]
     result = None
@@ -725,7 +759,7 @@
                 other.swap_near()
                 other.fetch_far()
             now.feed_forward(
-                weights, final, other.near if waiting else last_grad, other.other_near if waiting else None
+                weights, final, other.near if waiting else None, other.other_near if waiting else None
             )
             if waiting:
                 other.collect(now.fed)
@@ -733,7 +767,7 @@
             if not final:
                 received = lax.ppermute(result, "section", forward_pairs)
                 passes[m] = Forward(start[m], rings[m], marks[m], norms, received)
-    block_output = spread_features(jnp.stack([now.result for now in passes]), section, sections - 1)
+    block_output = jnp.stack([now.result for now in passes])
 
     backs = [Backward(last_grad[m], passes[m]) for m in range(2)]
     backward_pairs = [(s + 1, s) for s in range(sections - 1)]
@@ -743,8 +777,6 @@
         for m in range(2):
             now, other = backs[m], backs[1 - m]
             waiting = step + m > 0
-            if step == 1 and m == 0:
-                earlier = (earlier, block_output)
             now.feed_forward(weights, earlier, other.far if waiting else None)
             if waiting:
                 other.spread_near()
@@ -783,22 +815,20 @@
     sum_rest.far()
     sum_kv.near()
     sum_rest.near()
-    mine = sum_kv.bundle()
-    sum_rest.bundle()
-    input_grad = spread_features(
-        after(jnp.stack([now.grad_hidden_low for now in backs]), mine), section, 0
-    ).astype(F32)
-    sum_kv.small_far()
-    sum_rest.small_far()
-    kv_grads = sum_kv.total()
-    rest_grads = sum_rest.total()
+    mine = sum_kv.bundle(), sum_rest.bundle()
+    sum_kv.mine, sum_rest.mine = after(mine, mine[::-1])
+    small = sum_kv.small_far() + sum_rest.small_far()
+    own_rows = w_out.shape[1]
     up_grads = joint[:, : 2 * width]
     grad_down = jnp.concatenate([joint[:, 2 * width : 3 * width], joint[:, 3 * width :]])
-
-    own_rows = w_out.shape[1]
     units = jnp.stack(exchanged_out(up_grads, core_zero), axis=1)
-    units = units.reshape(own_rows, 2, 16, -1).transpose(0, 2, 1, 3)
+    units = units.reshape(own_rows, 2, 2, 16, -1).transpose(0, 3, 1, 2, 4)
     grad_up = units.reshape(own_rows, -1)
+    input_grad = after(jnp.stack([now.grad_hidden_low for now in backs]), small)
+    input_grad, block_output = spread_features(input_grad, block_output, section)
+    kv_grads = after(sum_kv.total(), grad_up)
+    rest_grads = sum_rest.total()
+
     kv_cores = exchanged_out(kv_grads, core_zero)
     rest_cores = exchanged_out(rest_grads[:, :width], core_zero)
     keys, values = [], []
@@ -812,7 +842,7 @@
     grad_vectors = picked(core_zero, columns[:own_rows], columns[own_rows:]).T[:4]
     return (
         block_output,
-        input_grad,
+        input_grad.astype(F32),
         grad_vectors[0:1],
         grad_vectors[1:2],
         grad_qkv[None],

time: 976 us -> 933 us (0.956)
  local copies, waits for them, and re-layouts: 108 us -> 84 us
  other arithmetic: 88.8 us -> 67 us
  starting transfers between devices: 266 us -> 247 us
  waiting for transfers between devices: 223 us -> 237 us
    ppermute x174, waiting for transfers between devices: 182 us -> 196 us  [moved(): lax.ppermute(value, axis, [(i, (i + steps) % count) for i in range(count)])]
    ppermute x12 -> x6, starting transfers between devices: 22.8 us -> 16.9 us  [the longest x3 8.69 us: spread_features(): lax.ppermute(picked(section == 0, piece(grads, a), piece(outputs, b)), 's...]
    pallas_call x40 -> x41, Pallas kernels: 182 us -> 187 us  [called(): pl.pallas_call(kernel, out_shape=out_shape, in_specs=[whole()] * len(oper...]
    dot_general x37 -> x38, matrix products: 66.1 us -> 70.7 us  [dot(): return lax.dot_general(left, right, dims, preferred_element_type=F32)]
    unnamed x483 -> x445, local copies, waits for them, and re-layouts: 57.6 us -> 55 us
  transfers between devices with their start and end apart: 205 -> 196, of which waited for: 74 -> 77; matrix products, arithmetic and copies ran while one was open for 21% -> 17% of each run, Pallas kernels for 19% -> 19%
where the time goes in v3:
time: 933 us; the launch traced here: 922 us
  starting transfers between devices  247 us (26%)
  waiting for transfers between devices  237 us (25%)
  Pallas kernels  196 us (21%)
  local copies, waits for them, and re-layouts  84 us (9%)
  matrix products  70.7 us (8%)
  other arithmetic  67 us (7%)
  between operations  20 us (2%)
    ppermute x174, starting transfers between devices, moved(): lax.ppermute(value, axis, [(i, (i + steps) % count) for i in range(count)])  199 us
    ppermute x174, waiting for transfers between devices, moved(): lax.ppermute(value, axis, [(i, (i + steps) % count) for i in range(count)])  196 us
    pallas_call x41, Pallas kernels, called(): pl.pallas_call(kernel, out_shape=out_shape, in_specs=[whole()] * len(oper...  187 us
    dot_general x38, matrix products, dot(): return lax.dot_general(left, right, dims, preferred_element_type=F32)  70.7 us
    unnamed x445, local copies, waits for them, and re-layouts  55 us
    ppermute x6, waiting for transfers between devices, local(): received = lax.ppermute(other.grad_hidden_low, 'section', backward_pairs)  26.5 us
  transfers between devices with their start and end apart: 196, of which 77 were waited for; matrix products, arithmetic and copies ran while one was open for 17% of the time, Pallas kernels for 19%

profile of v3, /device:TPU:23, one launch (start us, length us, event | category | flops | bytes accessed | tf_op | source)
XLA Modules:
  0.0 922.4 jit_solution(3302769246435294136)
XLA Ops:
  18.4 6.2 collective-permute-done
  27.4 5.7 collective-permute-start.1
  33.2 5.2 collective-permute-done.2
  45.4 5.5 collective-permute-start.14
  63.8 5.8 collective-permute-done.13
  74.3 31.6 %collective-permute-done.10.refs_1_ = bf16[4,1,80,1280]{3,2,1,0:T(8,128)(2,1)S(1)} collective-permute-done((bf16[4,1,80,1280]{3,2,1,0:T(8,128)(2,1)S(1)}, bf16[4,1,80,1280]{3,2,1,0:T(8,128)(2,1)S(1)}, u32[]{:S(2)}, u32[]{:S(2)}) %collective-permute-start.10) | collective-permute-done | bytes 819232 | tf_op jit(solution)/shard_map/ppermute | solution.py:22
  113.4 12.1 %collective-permute-done.32.refs_2_ = bf16[2,1,80,1280]{3,2,1,0:T(8,128)(2,1)S(1)} collective-permute-done((bf16[2,1,80,1280]{3,2,1,0:T(8,128)(2,1)S(1)}, bf16[2,1,80,1280]{3,2,1,0:T(8,128)(2,1)S(1)}, u32[]{:S(2)}, u32[]{:S(2)}) %collective-permute-start.32) | collective-permute-done | bytes 409632 | tf_op jit(solution)/shard_map/ppermute | solution.py:22
  213.6 5.5 collective-permute-done.41
  250.6 5.7 collective-permute-done.49
  323.3 5.2 collective-permute-done.69
  358.1 5.5 collective-permute-done.80
  397.8 5.7 collective-permute-done.89
  424.1 5.4 convolution_convert_fusion.4.kv_ref
  455.2 6.9 attend_back.8
  483.5 6.9 attend_back.9
  497.4 5.5 collective-permute-done.109
  522.9 6.9 attend_back.10
  536.8 5.3 collective-permute-done.118
  558.0 6.9 attend_back.11
  571.9 5.5 collective-permute-done.127
  598.6 6.9 attend_back.12
  612.5 5.4 collective-permute-done.136
  634.8 6.9 attend_back.13
  678.9 6.9 attend_back.14
  729.1 6.6 pad_maximum_fusion
  745.6 6.9 attend_back.15
  765.7 6.1 collective-permute-done.165
  776.1 7.5 convolution_convert_fusion.3
  829.0 10.0 %collective-permute-done.172 = bf16[4,80,1280]{2,1,0:T(8,128)(2,1)S(1)} collective-permute-done((bf16[4,80,1280]{2,1,0:T(8,128)(2,1)S(1)}, bf16[4,80,1280]{2,1,0:T(8,128)(2,1)S(1)}, u32[]{:S(2)}, u32[]{:S(2)}) %collective-permute-start.172) | collective-permute-done | bytes 819232 | tf_op jit(solution)/shard_map/ppermute | solution.py:22
  840.0 17.1 %collective-permute-done.178 = bf16[4,80,1408]{2,1,0:T(8,128)(2,1)S(1)} collective-permute-done((bf16[4,80,1408]{2,1,0:T(8,128)(2,1)S(1)}, bf16[4,80,1408]{2,1,0:T(8,128)(2,1)S(1)}, u32[]{:S(2)}, u32[]{:S(2)}) %collective-permute-start.178) | collective-permute-done | bytes 901152 | tf_op jit(solution)/shard_map/ppermute | solution.py:22
  888.2 5.4 collective-permute-start.192
  894.9 8.8 collective-permute-start.189
  (1380 shorter events, 659.1 us)
Async XLA Ops:
  7.2 179.1 %all-gather.2.cloned.1.call-start = ((), (), s32[]{:S(2)}) async-start(), calls=%async_computation.1 | async-start | bytes 13926400 | tf_op jit(solution)/shard_map/all_gather | solution.py:720
  12.5 895.4 %reduce-scatter.2.cloned.1.call-start = ((), (), s32[]{:S(2)}) async-start(), calls=%async_computation.2 | async-start | bytes 13926400 | tf_op jit(solution)/shard_map/reduce_scatter | solution.py:803
  12.8 20.3 %collective-permute-start.5 = (bf16[40,2688]{1,0:T(8,128)(2,1)S(1)}, bf16[40,2688]{1,0:T(8,128)(2,1)S(1)}, u32[]{:S(2)}, u32[]{:S(2)}) collective-permute-start(bf16[40,2688]{1,0:T(8,128)(2,1)S(1)} %get-tuple-element.191), channel_id=1, source_target_pairs={{0,1},{1,0},{2,3},{3,2},{4,5},{5,4},{6,7},{7,6},{8,9},{9,8},{10,11... | collective-permute-start | bytes 645128 | tf_op jit(solution)/shard_map/ppermute | solution.py:22
  63.7 42.2 %collective-permute-start.10 = (bf16[4,1,80,1280]{3,2,1,0:T(8,128)(2,1)S(1)}, bf16[4,1,80,1280]{3,2,1,0:T(8,128)(2,1)S(1)}, u32[]{:S(2)}, u32[]{:S(2)}) collective-permute-start(bf16[4,1,80,1280]{3,2,1,0:T(8,128)(2,1)S(1)} %pad_maximum_fusion.20.refs_0_), channel_id=1, source_target_pairs={{0,6},{2,0},{4,2},{6,4},{1,7},{3,1},{5,3},{7,5},{8,14},{10,8},{12,... | collective-permute-start | bytes 2457608 | tf_op jit(solution)/shard_map/ppermute | solution.py:22
  69.8 40.8 %collective-permute-start.16 = (bf16[4,1,80,1408]{3,2,1,0:T(8,128)(2,1)S(1)}, bf16[4,1,80,1408]{3,2,1,0:T(8,128)(2,1)S(1)}, u32[]{:S(2)}, u32[]{:S(2)}) collective-permute-start(bf16[4,1,80,1408]{3,2,1,0:T(8,128)(2,1)S(1)} %pad_maximum_fusion.18.refs_0_), channel_id=1, source_target_pairs={{0,24},{8,0},{16,8},{24,16},{1,25},{9,1},{17,9},{25,17},{2,26},{10... | collective-permute-start | bytes 2703368 | tf_op jit(solution)/shard_map/ppermute | solution.py:22
  69.9 40.7 %collective-permute-start.17 = (bf16[4,1,80,1408]{3,2,1,0:T(8,128)(2,1)S(1)}, bf16[4,1,80,1408]{3,2,1,0:T(8,128)(2,1)S(1)}, u32[]{:S(2)}, u32[]{:S(2)}) collective-permute-start(bf16[4,1,80,1408]{3,2,1,0:T(8,128)(2,1)S(1)} %pad_maximum_fusion.18.refs_0_), channel_id=1, source_target_pairs={{0,8},{8,16},{16,24},{24,0},{1,9},{9,17},{17,25},{25,1},{2,10},{10... | collective-permute-start | bytes 2703368 | tf_op jit(solution)/shard_map/ppermute | solution.py:22
  72.6 35.8 %collective-permute-start.11 = (bf16[4,1,80,1280]{3,2,1,0:T(8,128)(2,1)S(1)}, bf16[4,1,80,1280]{3,2,1,0:T(8,128)(2,1)S(1)}, u32[]{:S(2)}, u32[]{:S(2)}) collective-permute-start(bf16[4,1,80,1280]{3,2,1,0:T(8,128)(2,1)S(1)} %pad_maximum_fusion.20.refs_0_), channel_id=1, source_target_pairs={{0,2},{2,4},{4,6},{6,0},{1,3},{3,5},{5,7},{7,1},{8,10},{10,12},{12... | collective-permute-start | bytes 2457608 | tf_op jit(solution)/shard_map/ppermute | solution.py:22
  106.0 19.5 %collective-permute-start.32 = (bf16[2,1,80,1280]{3,2,1,0:T(8,128)(2,1)S(1)}, bf16[2,1,80,1280]{3,2,1,0:T(8,128)(2,1)S(1)}, u32[]{:S(2)}, u32[]{:S(2)}) collective-permute-start(bf16[2,1,80,1280]{3,2,1,0:T(8,128)(2,1)S(1)} %slice.1647), channel_id=1, source_target_pairs={{0,6},{2,0},{4,2},{6,4},{1,7},{3,1},{5,3},{7,5},{8,14},{10,8},{12,... | collective-permute-start | bytes 1228808 | tf_op jit(solution)/shard_map/ppermute | solution.py:22
  108.5 20.0 %collective-permute-start.33 = (bf16[2,1,80,1280]{3,2,1,0:T(8,128)(2,1)S(1)}, bf16[2,1,80,1280]{3,2,1,0:T(8,128)(2,1)S(1)}, u32[]{:S(2)}, u32[]{:S(2)}) collective-permute-start(bf16[2,1,80,1280]{3,2,1,0:T(8,128)(2,1)S(1)} %slice.1648), channel_id=1, source_target_pairs={{0,2},{2,4},{4,6},{6,0},{1,3},{3,5},{5,7},{7,1},{8,10},{10,12},{12... | collective-permute-start | bytes 1228808 | tf_op jit(solution)/shard_map/ppermute | solution.py:22
  110.6 22.8 %collective-permute-start.19 = (bf16[128,1280]{1,0:T(8,128)(2,1)S(1)}, bf16[128,1280]{1,0:T(8,128)(2,1)S(1)}, u32[]{:S(2)}, u32[]{:S(2)}) collective-permute-start(bf16[128,1280]{1,0:T(8,128)(2,1)S(1)} %get-tuple-element.194), channel_id=1, source_target_pairs={{0,24},{8,0},{16,8},{24,16},{1,25},{9,1},{17,9},{25,17},{2,26},{10... | collective-permute-start | bytes 983048 | tf_op jit(solution)/shard_map/ppermute | solution.py:22
  111.3 24.7 %collective-permute-start.21 = (bf16[128,1280]{1,0:T(8,128)(2,1)S(1)}, bf16[128,1280]{1,0:T(8,128)(2,1)S(1)}, u32[]{:S(2)}, u32[]{:S(2)}) collective-permute-start(bf16[128,1280]{1,0:T(8,128)(2,1)S(1)} %get-tuple-element.194), channel_id=1, source_target_pairs={{0,8},{8,16},{16,24},{24,0},{1,9},{9,17},{17,25},{25,1},{2,10},{10... | collective-permute-start | bytes 983048 | tf_op jit(solution)/shard_map/ppermute | solution.py:22
  113.3 26.2 %collective-permute-start.27 = (bf16[128,1280]{1,0:T(8,128)(2,1)S(1)}, bf16[128,1280]{1,0:T(8,128)(2,1)S(1)}, u32[]{:S(2)}, u32[]{:S(2)}) collective-permute-start(bf16[128,1280]{1,0:T(8,128)(2,1)S(1)} %get-tuple-element.195), channel_id=1, source_target_pairs={{0,6},{2,0},{4,2},{6,4},{1,7},{3,1},{5,3},{7,5},{8,14},{10,8},{12,... | collective-permute-start | bytes 983048 | tf_op jit(solution)/shard_map/ppermute | solution.py:22
  125.5 17.1 %collective-permute-start.29 = (bf16[128,1280]{1,0:T(8,128)(2,1)S(1)}, bf16[128,1280]{1,0:T(8,128)(2,1)S(1)}, u32[]{:S(2)}, u32[]{:S(2)}) collective-permute-start(bf16[128,1280]{1,0:T(8,128)(2,1)S(1)} %get-tuple-element.195), channel_id=1, source_target_pairs={{0,2},{2,4},{4,6},{6,0},{1,3},{3,5},{5,7},{7,1},{8,10},{10,12},{12... | collective-permute-start | bytes 983048 | tf_op jit(solution)/shard_map/ppermute | solution.py:22
  213.2 37.3 %collective-permute-start.53 = (bf16[128,1280]{1,0:T(8,128)(2,1)S(1)}, bf16[128,1280]{1,0:T(8,128)(2,1)S(1)}, u32[]{:S(2)}, u32[]{:S(2)}) collective-permute-start(bf16[128,1280]{1,0:T(8,128)(2,1)S(1)} %get-tuple-element.522), channel_id=1, source_target_pairs={{0,1},{1,0},{2,3},{3,2},{4,5},{5,4},{6,7},{7,6},{8,9},{9,8},{10,11... | collective-permute-start | bytes 983048 | tf_op jit(solution)/shard_map/ppermute | solution.py:22
  250.5 36.9 %collective-permute-start.48 = (bf16[128,1280]{1,0:T(8,128)(2,1)S(1)}, bf16[128,1280]{1,0:T(8,128)(2,1)S(1)}, u32[]{:S(2)}, u32[]{:S(2)}) collective-permute-start(bf16[128,1280]{1,0:T(8,128)(2,1)S(1)} %get-tuple-element.514), channel_id=1, source_target_pairs={{0,1},{1,0},{2,3},{3,2},{4,5},{5,4},{6,7},{7,6},{8,9},{9,8},{10,11... | collective-permute-start | bytes 983048 | tf_op jit(solution)/shard_map/ppermute | solution.py:22
  287.5 35.8 %collective-permute-start.73 = (bf16[128,1280]{1,0:T(8,128)(2,1)S(1)}, bf16[128,1280]{1,0:T(8,128)(2,1)S(1)}, u32[]{:S(2)}, u32[]{:S(2)}) collective-permute-start(bf16[128,1280]{1,0:T(8,128)(2,1)S(1)} %get-tuple-element.510), channel_id=1, source_target_pairs={{0,1},{1,0},{2,3},{3,2},{4,5},{5,4},{6,7},{7,6},{8,9},{9,8},{10,11... | collective-permute-start | bytes 983048 | tf_op jit(solution)/shard_map/ppermute | solution.py:22
  450.5 16.5 %collective-permute-start.107 = (bf16[128,1280]{1,0:T(8,128)(2,1)S(1)}, bf16[128,1280]{1,0:T(8,128)(2,1)S(1)}, u32[]{:S(2)}, u32[]{:S(2)}) collective-permute-start(bf16[128,1280]{1,0:T(8,128)(2,1)S(1)} %get-tuple-element.642), channel_id=1, source_target_pairs={{0,1},{1,0},{2,3},{3,2},{4,5},{5,4},{6,7},{7,6},{8,9},{9,8},{10,11... | collective-permute-start | bytes 983048 | tf_op jit(solution)/shard_map/ppermute | solution.py:22
  511.1 18.7 %collective-permute-start.116 = (bf16[128,1280]{1,0:T(8,128)(2,1)S(1)}, bf16[128,1280]{1,0:T(8,128)(2,1)S(1)}, u32[]{:S(2)}, u32[]{:S(2)}) collective-permute-start(bf16[128,1280]{1,0:T(8,128)(2,1)S(1)} %pad_maximum_fusion.50), channel_id=1, source_target_pairs={{0,8},{8,16},{16,24},{24,0},{1,9},{9,17},{17,25},{25,1},{2,10},{10... | collective-permute-start | bytes 983048 | tf_op jit(solution)/shard_map/ppermute | solution.py:22
  585.6 19.8 %collective-permute-start.134 = (bf16[128,1280]{1,0:T(8,128)(2,1)S(1)}, bf16[128,1280]{1,0:T(8,128)(2,1)S(1)}, u32[]{:S(2)}, u32[]{:S(2)}) collective-permute-start(bf16[128,1280]{1,0:T(8,128)(2,1)S(1)} %pad_maximum_fusion.54), channel_id=1, source_target_pairs={{0,8},{8,16},{16,24},{24,0},{1,9},{9,17},{17,25},{25,1},{2,10},{10... | collective-permute-start | bytes 983048 | tf_op jit(solution)/shard_map/ppermute | solution.py:22
  664.6 21.2 %collective-permute-start.152 = (bf16[128,1280]{1,0:T(8,128)(2,1)S(1)}, bf16[128,1280]{1,0:T(8,128)(2,1)S(1)}, u32[]{:S(2)}, u32[]{:S(2)}) collective-permute-start(bf16[128,1280]{1,0:T(8,128)(2,1)S(1)} %pad_maximum_fusion.58), channel_id=1, source_target_pairs={{0,8},{8,16},{16,24},{24,0},{1,9},{9,17},{17,25},{25,1},{2,10},{10... | collective-permute-start | bytes 983048 | tf_op jit(solution)/shard_map/ppermute | solution.py:22
  771.9 16.5 %collective-permute-start.166 = (bf16[128,1280]{1,0:T(8,128)(2,1)S(1)}, bf16[128,1280]{1,0:T(8,128)(2,1)S(1)}, u32[]{:S(2)}, u32[]{:S(2)}) collective-permute-start(bf16[128,1280]{1,0:T(8,128)(2,1)S(1)} %pad_maximum_fusion.62), channel_id=1, source_target_pairs={{0,8},{8,16},{16,24},{24,0},{1,9},{9,17},{17,25},{25,1},{2,10},{10... | collective-permute-start | bytes 983048 | tf_op jit(solution)/shard_map/ppermute | solution.py:22
  776.0 17.6 %collective-permute-start.168 = (bf16[128,1280]{1,0:T(8,128)(2,1)S(1)}, bf16[128,1280]{1,0:T(8,128)(2,1)S(1)}, u32[]{:S(2)}, u32[]{:S(2)}) collective-permute-start(bf16[128,1280]{1,0:T(8,128)(2,1)S(1)} %pad_maximum_fusion.63), channel_id=1, source_target_pairs={{0,24},{8,0},{16,8},{24,16},{1,25},{9,1},{17,9},{25,17},{2,26},{10... | collective-permute-start | bytes 983048 | tf_op jit(solution)/shard_map/ppermute | solution.py:22
  794.8 20.2 %collective-permute-start.169 = (bf16[2,80,1280]{2,1,0:T(8,128)(2,1)}, bf16[2,80,1280]{2,1,0:T(8,128)(2,1)}, u32[]{:S(2)}, u32[]{:S(2)}) collective-permute-start(bf16[2,80,1280]{2,1,0:T(8,128)(2,1)} %get-tuple-element.555), channel_id=1, source_target_pairs={{0,2},{2,4},{4,6},{6,0},{1,3},{3,5},{5,7},{7,1},{8,10},{10,12},{12... | collective-permute-start | bytes 1228808 | tf_op jit(solution)/shard_map/ppermute | solution.py:22
  797.7 20.4 %collective-permute-start.171 = (bf16[2,80,1280]{2,1,0:T(8,128)(2,1)}, bf16[2,80,1280]{2,1,0:T(8,128)(2,1)}, u32[]{:S(2)}, u32[]{:S(2)}) collective-permute-start(bf16[2,80,1280]{2,1,0:T(8,128)(2,1)} %get-tuple-element.557), channel_id=1, source_target_pairs={{0,6},{2,0},{4,2},{6,4},{1,7},{3,1},{5,3},{7,5},{8,14},{10,8},{12,... | collective-permute-start | bytes 1228808 | tf_op jit(solution)/shard_map/ppermute | solution.py:22
  806.7 18.0 %collective-permute-start.177 = (bf16[2,80,1408]{2,1,0:T(8,128)(2,1)S(1)}, bf16[2,80,1408]{2,1,0:T(8,128)(2,1)S(1)}, u32[]{:S(2)}, u32[]{:S(2)}) collective-permute-start(bf16[2,80,1408]{2,1,0:T(8,128)(2,1)S(1)} %pad_maximum_fusion.41), channel_id=1, source_target_pairs={{0,24},{8,0},{16,8},{24,16},{1,25},{9,1},{17,9},{25,17},{2,26},{10... | collective-permute-start | bytes 1351688 | tf_op jit(solution)/shard_map/ppermute | solution.py:22
  807.9 17.2 %collective-permute-start.175 = (bf16[2,80,1408]{2,1,0:T(8,128)(2,1)S(1)}, bf16[2,80,1408]{2,1,0:T(8,128)(2,1)S(1)}, u32[]{:S(2)}, u32[]{:S(2)}) collective-permute-start(bf16[2,80,1408]{2,1,0:T(8,128)(2,1)S(1)} %pad_maximum_fusion.40), channel_id=1, source_target_pairs={{0,8},{8,16},{16,24},{24,0},{1,9},{9,17},{17,25},{25,1},{2,10},{10... | collective-permute-start | bytes 1351688 | tf_op jit(solution)/shard_map/ppermute | solution.py:22
  819.6 19.4 %collective-permute-start.172 = (bf16[4,80,1280]{2,1,0:T(8,128)(2,1)S(1)}, bf16[4,80,1280]{2,1,0:T(8,128)(2,1)S(1)}, u32[]{:S(2)}, u32[]{:S(2)}) collective-permute-start(bf16[4,80,1280]{2,1,0:T(8,128)(2,1)S(1)} %pad_maximum_fusion.23), channel_id=1, source_target_pairs={{0,6},{2,0},{4,2},{6,4},{1,7},{3,1},{5,3},{7,5},{8,14},{10,8},{12,... | collective-permute-start | bytes 2457608 | tf_op jit(solution)/shard_map/ppermute | solution.py:22
  819.8 19.9 %collective-permute-start.170 = (bf16[4,80,1280]{2,1,0:T(8,128)(2,1)S(1)}, bf16[4,80,1280]{2,1,0:T(8,128)(2,1)S(1)}, u32[]{:S(2)}, u32[]{:S(2)}) collective-permute-start(bf16[4,80,1280]{2,1,0:T(8,128)(2,1)S(1)} %pad_maximum_fusion.22), channel_id=1, source_target_pairs={{0,2},{2,4},{4,6},{6,0},{1,3},{3,5},{5,7},{7,1},{8,10},{10,12},{12... | collective-permute-start | bytes 2457608 | tf_op jit(solution)/shard_map/ppermute | solution.py:22
  825.0 32.1 %collective-permute-start.178 = (bf16[4,80,1408]{2,1,0:T(8,128)(2,1)S(1)}, bf16[4,80,1408]{2,1,0:T(8,128)(2,1)S(1)}, u32[]{:S(2)}, u32[]{:S(2)}) collective-permute-start(bf16[4,80,1408]{2,1,0:T(8,128)(2,1)S(1)} %pad_maximum_fusion.19), channel_id=1, source_target_pairs={{0,24},{8,0},{16,8},{24,16},{1,25},{9,1},{17,9},{25,17},{2,26},{10... | collective-permute-start | bytes 2703368 | tf_op jit(solution)/shard_map/ppermute | solution.py:22
  825.9 31.3 %collective-permute-start.176 = (bf16[4,80,1408]{2,1,0:T(8,128)(2,1)S(1)}, bf16[4,80,1408]{2,1,0:T(8,128)(2,1)S(1)}, u32[]{:S(2)}, u32[]{:S(2)}) collective-permute-start(bf16[4,80,1408]{2,1,0:T(8,128)(2,1)S(1)} %maximum_maximum_fusion), channel_id=1, source_target_pairs={{0,8},{8,16},{16,24},{24,0},{1,9},{9,17},{17,25},{25,1},{2,10},{10... | collective-permute-start | bytes 2703368 | tf_op jit(solution)/shard_map/ppermute | solution.py:22
  885.0 21.0 %collective-permute-start.186 = (bf16[2,128,320]{2,1,0:T(8,128)(2,1)S(1)}, bf16[2,128,320]{2,1,0:T(8,128)(2,1)S(1)}, u32[]{:S(2)}, u32[]{:S(2)}) collective-permute-start(bf16[2,128,320]{2,1,0:T(8,128)(2,1)S(1)} %pad_maximum_fusion.76), channel_id=1, source_target_pairs={{0,0},{2,8},{4,16},{6,24},{8,2},{10,10},{12,18},{14,26},{16,4},{18... | collective-permute-start | bytes 491528 | tf_op jit(solution)/shard_map/ppermute | solution.py:36
  888.2 16.8 %collective-permute-start.192 = (bf16[40,1280]{1,0:T(8,128)(2,1)S(1)}, bf16[40,1280]{1,0:T(8,128)(2,1)S(1)}, u32[]{:S(2)}, u32[]{:S(2)}) collective-permute-start(bf16[40,1280]{1,0:T(8,128)(2,1)S(1)} %select_convert_fusion.3), channel_id=1, source_target_pairs={{0,1},{1,0},{2,3},{3,2},{4,5},{5,4},{6,7},{7,6},{8,9},{9,8},{10,11... | collective-permute-start | bytes 307208 | tf_op jit(solution)/shard_map/ppermute | solution.py:22
  (348 other events, 5587.1 us)
Sparse Core Ops, SparseCore 0:
  12.6 134.7 all-gather.1
  735.8 126.9 reduce-scatter.1

commit v4 on v3

--- a/solution.py
+++ b/solution.py
@@ -798,7 +798,7 @@
             earlier = now.ring_grads
 
     joint = feed_grads(backs)
-    backs[0].reduce()
+    backs[0].reduce(backs[1].grad_up)
     backs[1].attention((backs[0].grad_hidden_low, joint))
     joint = lax.psum_scatter(joint, ("dp", "y"), scatter_dimension=0, tiled=True).astype(F32)
     backs[1].project(weights)

time: 933 us -> 926 us (level)
    unnamed x445 -> x443, local copies, waits for them, and re-layouts: 55 us -> 55 us
  transfers between devices with their start and end apart: 196 -> 196, of which waited for: 77 -> 76; matrix products, arithmetic and copies ran while one was open for 17% -> 17% of each run, Pallas kernels for 19% -> 20%
where the time goes in v4:
time: 926 us; the launch traced here: 916 us
  starting transfers between devices  245 us (26%)
  waiting for transfers between devices  232 us (25%)
  Pallas kernels  196 us (21%)
  local copies, waits for them, and re-layouts  83.4 us (9%)
  matrix products  70.7 us (8%)
  other arithmetic  67.9 us (7%)
  between operations  20.1 us (2%)
    ppermute x174, starting transfers between devices, moved(): lax.ppermute(value, axis, [(i, (i + steps) % count) for i in range(count)])  197 us
    ppermute x174, waiting for transfers between devices, moved(): lax.ppermute(value, axis, [(i, (i + steps) % count) for i in range(count)])  191 us
    pallas_call x41, Pallas kernels, called(): pl.pallas_call(kernel, out_shape=out_shape, in_specs=[whole()] * len(oper...  187 us
    dot_general x38, matrix products, dot(): return lax.dot_general(left, right, dims, preferred_element_type=F32)  70.7 us
    unnamed x443, local copies, waits for them, and re-layouts  55 us
    ppermute x6, waiting for transfers between devices, local(): received = lax.ppermute(other.grad_hidden_low, 'section', backward_pairs)  26.6 us
  transfers between devices with their start and end apart: 196, of which 76 were waited for; matrix products, arithmetic and copies ran while one was open for 17% of the time, Pallas kernels for 20%

profile of v4, /device:TPU:23, one launch (start us, length us, event | category | flops | bytes accessed | tf_op | source)
XLA Modules:
  0.0 915.8 jit_solution(1004882783247415865)
XLA Ops:
  18.4 6.2 collective-permute-done
  27.4 5.7 collective-permute-start.1
  33.2 5.2 collective-permute-done.2
  45.3 5.5 collective-permute-start.14
  63.8 5.8 collective-permute-done.13
  74.3 31.6 %collective-permute-done.10.refs_1_ = bf16[4,1,80,1280]{3,2,1,0:T(8,128)(2,1)S(1)} collective-permute-done((bf16[4,1,80,1280]{3,2,1,0:T(8,128)(2,1)S(1)}, bf16[4,1,80,1280]{3,2,1,0:T(8,128)(2,1)S(1)}, u32[]{:S(2)}, u32[]{:S(2)}) %collective-permute-start.10) | collective-permute-done | bytes 819232 | tf_op jit(solution)/shard_map/ppermute | solution.py:22
  113.4 12.1 %collective-permute-done.32.refs_2_ = bf16[2,1,80,1280]{3,2,1,0:T(8,128)(2,1)S(1)} collective-permute-done((bf16[2,1,80,1280]{3,2,1,0:T(8,128)(2,1)S(1)}, bf16[2,1,80,1280]{3,2,1,0:T(8,128)(2,1)S(1)}, u32[]{:S(2)}, u32[]{:S(2)}) %collective-permute-start.32) | collective-permute-done | bytes 409632 | tf_op jit(solution)/shard_map/ppermute | solution.py:22
  213.8 5.3 collective-permute-done.41
  250.4 5.7 collective-permute-done.49
  358.1 5.3 collective-permute-done.80
  397.6 5.8 collective-permute-done.89
  423.7 5.4 convolution_convert_fusion.4.kv_ref
  454.7 6.9 attend_back.8
  483.0 6.9 attend_back.9
  496.9 5.5 collective-permute-done.109
  522.4 6.9 attend_back.10
  536.3 5.4 collective-permute-done.118
  557.5 6.9 attend_back.11
  571.4 5.5 collective-permute-done.127
  597.8 6.9 attend_back.12
  611.7 5.4 collective-permute-done.136
  634.1 6.9 attend_back.13
  677.9 6.9 attend_back.14
  722.6 6.6 pad_maximum_fusion
  739.6 6.9 attend_back.15
  760.1 6.2 collective-permute-done.165
  770.4 7.5 convolution_convert_fusion.3
  823.1 10.3 %collective-permute-done.172 = bf16[4,80,1280]{2,1,0:T(8,128)(2,1)S(1)} collective-permute-done((bf16[4,80,1280]{2,1,0:T(8,128)(2,1)S(1)}, bf16[4,80,1280]{2,1,0:T(8,128)(2,1)S(1)}, u32[]{:S(2)}, u32[]{:S(2)}) %collective-permute-start.172) | collective-permute-done | bytes 819232 | tf_op jit(solution)/shard_map/ppermute | solution.py:22
  834.4 17.7 %collective-permute-done.178 = bf16[4,80,1408]{2,1,0:T(8,128)(2,1)S(1)} collective-permute-done((bf16[4,80,1408]{2,1,0:T(8,128)(2,1)S(1)}, bf16[4,80,1408]{2,1,0:T(8,128)(2,1)S(1)}, u32[]{:S(2)}, u32[]{:S(2)}) %collective-permute-start.178) | collective-permute-done | bytes 901152 | tf_op jit(solution)/shard_map/ppermute | solution.py:22
  862.9 5.8 collective-permute-start.184
  881.6 5.2 collective-permute-start.192
  888.2 8.9 collective-permute-start.189
  (1378 shorter events, 651.2 us)
Async XLA Ops:
  7.2 179.2 %all-gather.2.cloned.1.call-start = ((), (), s32[]{:S(2)}) async-start(), calls=%async_computation.1 | async-start | bytes 13926400 | tf_op jit(solution)/shard_map/all_gather | solution.py:720
  12.5 888.7 %reduce-scatter.2.cloned.1.call-start = ((), (), s32[]{:S(2)}) async-start(), calls=%async_computation.2 | async-start | bytes 13926400 | tf_op jit(solution)/shard_map/reduce_scatter | solution.py:803
  12.8 20.3 %collective-permute-start.5 = (bf16[40,2688]{1,0:T(8,128)(2,1)S(1)}, bf16[40,2688]{1,0:T(8,128)(2,1)S(1)}, u32[]{:S(2)}, u32[]{:S(2)}) collective-permute-start(bf16[40,2688]{1,0:T(8,128)(2,1)S(1)} %get-tuple-element.193), channel_id=1, source_target_pairs={{0,1},{1,0},{2,3},{3,2},{4,5},{5,4},{6,7},{7,6},{8,9},{9,8},{10,11... | collective-permute-start | bytes 645128 | tf_op jit(solution)/shard_map/ppermute | solution.py:22
  63.7 42.2 %collective-permute-start.10 = (bf16[4,1,80,1280]{3,2,1,0:T(8,128)(2,1)S(1)}, bf16[4,1,80,1280]{3,2,1,0:T(8,128)(2,1)S(1)}, u32[]{:S(2)}, u32[]{:S(2)}) collective-permute-start(bf16[4,1,80,1280]{3,2,1,0:T(8,128)(2,1)S(1)} %pad_maximum_fusion.20.refs_0_), channel_id=1, source_target_pairs={{0,6},{2,0},{4,2},{6,4},{1,7},{3,1},{5,3},{7,5},{8,14},{10,8},{12,... | collective-permute-start | bytes 2457608 | tf_op jit(solution)/shard_map/ppermute | solution.py:22
  69.8 40.8 %collective-permute-start.16 = (bf16[4,1,80,1408]{3,2,1,0:T(8,128)(2,1)S(1)}, bf16[4,1,80,1408]{3,2,1,0:T(8,128)(2,1)S(1)}, u32[]{:S(2)}, u32[]{:S(2)}) collective-permute-start(bf16[4,1,80,1408]{3,2,1,0:T(8,128)(2,1)S(1)} %pad_maximum_fusion.18.refs_0_), channel_id=1, source_target_pairs={{0,24},{8,0},{16,8},{24,16},{1,25},{9,1},{17,9},{25,17},{2,26},{10... | collective-permute-start | bytes 2703368 | tf_op jit(solution)/shard_map/ppermute | solution.py:22
  69.9 40.7 %collective-permute-start.17 = (bf16[4,1,80,1408]{3,2,1,0:T(8,128)(2,1)S(1)}, bf16[4,1,80,1408]{3,2,1,0:T(8,128)(2,1)S(1)}, u32[]{:S(2)}, u32[]{:S(2)}) collective-permute-start(bf16[4,1,80,1408]{3,2,1,0:T(8,128)(2,1)S(1)} %pad_maximum_fusion.18.refs_0_), channel_id=1, source_target_pairs={{0,8},{8,16},{16,24},{24,0},{1,9},{9,17},{17,25},{25,1},{2,10},{10... | collective-permute-start | bytes 2703368 | tf_op jit(solution)/shard_map/ppermute | solution.py:22
  72.6 35.8 %collective-permute-start.11 = (bf16[4,1,80,1280]{3,2,1,0:T(8,128)(2,1)S(1)}, bf16[4,1,80,1280]{3,2,1,0:T(8,128)(2,1)S(1)}, u32[]{:S(2)}, u32[]{:S(2)}) collective-permute-start(bf16[4,1,80,1280]{3,2,1,0:T(8,128)(2,1)S(1)} %pad_maximum_fusion.20.refs_0_), channel_id=1, source_target_pairs={{0,2},{2,4},{4,6},{6,0},{1,3},{3,5},{5,7},{7,1},{8,10},{10,12},{12... | collective-permute-start | bytes 2457608 | tf_op jit(solution)/shard_map/ppermute | solution.py:22
  106.0 19.5 %collective-permute-start.32 = (bf16[2,1,80,1280]{3,2,1,0:T(8,128)(2,1)S(1)}, bf16[2,1,80,1280]{3,2,1,0:T(8,128)(2,1)S(1)}, u32[]{:S(2)}, u32[]{:S(2)}) collective-permute-start(bf16[2,1,80,1280]{3,2,1,0:T(8,128)(2,1)S(1)} %slice.1647), channel_id=1, source_target_pairs={{0,6},{2,0},{4,2},{6,4},{1,7},{3,1},{5,3},{7,5},{8,14},{10,8},{12,... | collective-permute-start | bytes 1228808 | tf_op jit(solution)/shard_map/ppermute | solution.py:22
  108.5 20.3 %collective-permute-start.33 = (bf16[2,1,80,1280]{3,2,1,0:T(8,128)(2,1)S(1)}, bf16[2,1,80,1280]{3,2,1,0:T(8,128)(2,1)S(1)}, u32[]{:S(2)}, u32[]{:S(2)}) collective-permute-start(bf16[2,1,80,1280]{3,2,1,0:T(8,128)(2,1)S(1)} %slice.1648), channel_id=1, source_target_pairs={{0,2},{2,4},{4,6},{6,0},{1,3},{3,5},{5,7},{7,1},{8,10},{10,12},{12... | collective-permute-start | bytes 1228808 | tf_op jit(solution)/shard_map/ppermute | solution.py:22
  110.6 23.0 %collective-permute-start.19 = (bf16[128,1280]{1,0:T(8,128)(2,1)S(1)}, bf16[128,1280]{1,0:T(8,128)(2,1)S(1)}, u32[]{:S(2)}, u32[]{:S(2)}) collective-permute-start(bf16[128,1280]{1,0:T(8,128)(2,1)S(1)} %get-tuple-element.196), channel_id=1, source_target_pairs={{0,24},{8,0},{16,8},{24,16},{1,25},{9,1},{17,9},{25,17},{2,26},{10... | collective-permute-start | bytes 983048 | tf_op jit(solution)/shard_map/ppermute | solution.py:22
  111.4 24.9 %collective-permute-start.21 = (bf16[128,1280]{1,0:T(8,128)(2,1)S(1)}, bf16[128,1280]{1,0:T(8,128)(2,1)S(1)}, u32[]{:S(2)}, u32[]{:S(2)}) collective-permute-start(bf16[128,1280]{1,0:T(8,128)(2,1)S(1)} %get-tuple-element.196), channel_id=1, source_target_pairs={{0,8},{8,16},{16,24},{24,0},{1,9},{9,17},{17,25},{25,1},{2,10},{10... | collective-permute-start | bytes 983048 | tf_op jit(solution)/shard_map/ppermute | solution.py:22
  113.3 26.2 %collective-permute-start.27 = (bf16[128,1280]{1,0:T(8,128)(2,1)S(1)}, bf16[128,1280]{1,0:T(8,128)(2,1)S(1)}, u32[]{:S(2)}, u32[]{:S(2)}) collective-permute-start(bf16[128,1280]{1,0:T(8,128)(2,1)S(1)} %get-tuple-element.197), channel_id=1, source_target_pairs={{0,6},{2,0},{4,2},{6,4},{1,7},{3,1},{5,3},{7,5},{8,14},{10,8},{12,... | collective-permute-start | bytes 983048 | tf_op jit(solution)/shard_map/ppermute | solution.py:22
  125.5 17.2 %collective-permute-start.29 = (bf16[128,1280]{1,0:T(8,128)(2,1)S(1)}, bf16[128,1280]{1,0:T(8,128)(2,1)S(1)}, u32[]{:S(2)}, u32[]{:S(2)}) collective-permute-start(bf16[128,1280]{1,0:T(8,128)(2,1)S(1)} %get-tuple-element.197), channel_id=1, source_target_pairs={{0,2},{2,4},{4,6},{6,0},{1,3},{3,5},{5,7},{7,1},{8,10},{10,12},{12... | collective-permute-start | bytes 983048 | tf_op jit(solution)/shard_map/ppermute | solution.py:22
  213.4 36.9 %collective-permute-start.53 = (bf16[128,1280]{1,0:T(8,128)(2,1)S(1)}, bf16[128,1280]{1,0:T(8,128)(2,1)S(1)}, u32[]{:S(2)}, u32[]{:S(2)}) collective-permute-start(bf16[128,1280]{1,0:T(8,128)(2,1)S(1)} %get-tuple-element.525), channel_id=1, source_target_pairs={{0,1},{1,0},{2,3},{3,2},{4,5},{5,4},{6,7},{7,6},{8,9},{9,8},{10,11... | collective-permute-start | bytes 983048 | tf_op jit(solution)/shard_map/ppermute | solution.py:22
  250.3 37.1 %collective-permute-start.48 = (bf16[128,1280]{1,0:T(8,128)(2,1)S(1)}, bf16[128,1280]{1,0:T(8,128)(2,1)S(1)}, u32[]{:S(2)}, u32[]{:S(2)}) collective-permute-start(bf16[128,1280]{1,0:T(8,128)(2,1)S(1)} %get-tuple-element.517), channel_id=1, source_target_pairs={{0,1},{1,0},{2,3},{3,2},{4,5},{5,4},{6,7},{7,6},{8,9},{9,8},{10,11... | collective-permute-start | bytes 983048 | tf_op jit(solution)/shard_map/ppermute | solution.py:22
  287.5 35.6 %collective-permute-start.73 = (bf16[128,1280]{1,0:T(8,128)(2,1)S(1)}, bf16[128,1280]{1,0:T(8,128)(2,1)S(1)}, u32[]{:S(2)}, u32[]{:S(2)}) collective-permute-start(bf16[128,1280]{1,0:T(8,128)(2,1)S(1)} %get-tuple-element.513), channel_id=1, source_target_pairs={{0,1},{1,0},{2,3},{3,2},{4,5},{5,4},{6,7},{7,6},{8,9},{9,8},{10,11... | collective-permute-start | bytes 983048 | tf_op jit(solution)/shard_map/ppermute | solution.py:22
  510.6 18.7 %collective-permute-start.116 = (bf16[128,1280]{1,0:T(8,128)(2,1)S(1)}, bf16[128,1280]{1,0:T(8,128)(2,1)S(1)}, u32[]{:S(2)}, u32[]{:S(2)}) collective-permute-start(bf16[128,1280]{1,0:T(8,128)(2,1)S(1)} %pad_maximum_fusion.50), channel_id=1, source_target_pairs={{0,8},{8,16},{16,24},{24,0},{1,9},{9,17},{17,25},{25,1},{2,10},{10... | collective-permute-start | bytes 983048 | tf_op jit(solution)/shard_map/ppermute | solution.py:22
  585.1 19.5 %collective-permute-start.134 = (bf16[128,1280]{1,0:T(8,128)(2,1)S(1)}, bf16[128,1280]{1,0:T(8,128)(2,1)S(1)}, u32[]{:S(2)}, u32[]{:S(2)}) collective-permute-start(bf16[128,1280]{1,0:T(8,128)(2,1)S(1)} %pad_maximum_fusion.54), channel_id=1, source_target_pairs={{0,8},{8,16},{16,24},{24,0},{1,9},{9,17},{17,25},{25,1},{2,10},{10... | collective-permute-start | bytes 983048 | tf_op jit(solution)/shard_map/ppermute | solution.py:22
  663.8 20.9 %collective-permute-start.152 = (bf16[128,1280]{1,0:T(8,128)(2,1)S(1)}, bf16[128,1280]{1,0:T(8,128)(2,1)S(1)}, u32[]{:S(2)}, u32[]{:S(2)}) collective-permute-start(bf16[128,1280]{1,0:T(8,128)(2,1)S(1)} %pad_maximum_fusion.58), channel_id=1, source_target_pairs={{0,8},{8,16},{16,24},{24,0},{1,9},{9,17},{17,25},{25,1},{2,10},{10... | collective-permute-start | bytes 983048 | tf_op jit(solution)/shard_map/ppermute | solution.py:22
  715.2 17.7 %collective-permute-start.162 = (bf16[256,1280]{1,0:T(8,128)(2,1)}, bf16[256,1280]{1,0:T(8,128)(2,1)S(1)}, u32[]{:S(2)}, u32[]{:S(2)}) collective-permute-start(bf16[256,1280]{1,0:T(8,128)(2,1)} %convert_element_type.1004), channel_id=1, source_target_pairs={{0,1},{1,0},{2,3},{3,2},{4,5},{5,4},{6,7},{7,6},{8,9},{9,8},{10,11... | collective-permute-start | bytes 1966088 | tf_op jit(solution)/shard_map/ppermute | solution.py:22
  766.3 16.7 %collective-permute-start.166 = (bf16[128,1280]{1,0:T(8,128)(2,1)S(1)}, bf16[128,1280]{1,0:T(8,128)(2,1)S(1)}, u32[]{:S(2)}, u32[]{:S(2)}) collective-permute-start(bf16[128,1280]{1,0:T(8,128)(2,1)S(1)} %pad_maximum_fusion.62), channel_id=1, source_target_pairs={{0,8},{8,16},{16,24},{24,0},{1,9},{9,17},{17,25},{25,1},{2,10},{10... | collective-permute-start | bytes 983048 | tf_op jit(solution)/shard_map/ppermute | solution.py:22
  770.3 17.0 %collective-permute-start.168 = (bf16[128,1280]{1,0:T(8,128)(2,1)S(1)}, bf16[128,1280]{1,0:T(8,128)(2,1)S(1)}, u32[]{:S(2)}, u32[]{:S(2)}) collective-permute-start(bf16[128,1280]{1,0:T(8,128)(2,1)S(1)} %pad_maximum_fusion.63), channel_id=1, source_target_pairs={{0,24},{8,0},{16,8},{24,16},{1,25},{9,1},{17,9},{25,17},{2,26},{10... | collective-permute-start | bytes 983048 | tf_op jit(solution)/shard_map/ppermute | solution.py:22
  788.5 20.5 %collective-permute-start.169 = (bf16[2,80,1280]{2,1,0:T(8,128)(2,1)}, bf16[2,80,1280]{2,1,0:T(8,128)(2,1)}, u32[]{:S(2)}, u32[]{:S(2)}) collective-permute-start(bf16[2,80,1280]{2,1,0:T(8,128)(2,1)} %get-tuple-element.559), channel_id=1, source_target_pairs={{0,2},{2,4},{4,6},{6,0},{1,3},{3,5},{5,7},{7,1},{8,10},{10,12},{12... | collective-permute-start | bytes 1228808 | tf_op jit(solution)/shard_map/ppermute | solution.py:22
  791.8 20.3 %collective-permute-start.171 = (bf16[2,80,1280]{2,1,0:T(8,128)(2,1)}, bf16[2,80,1280]{2,1,0:T(8,128)(2,1)}, u32[]{:S(2)}, u32[]{:S(2)}) collective-permute-start(bf16[2,80,1280]{2,1,0:T(8,128)(2,1)} %get-tuple-element.561), channel_id=1, source_target_pairs={{0,6},{2,0},{4,2},{6,4},{1,7},{3,1},{5,3},{7,5},{8,14},{10,8},{12,... | collective-permute-start | bytes 1228808 | tf_op jit(solution)/shard_map/ppermute | solution.py:22
  800.7 18.2 %collective-permute-start.177 = (bf16[2,80,1408]{2,1,0:T(8,128)(2,1)S(1)}, bf16[2,80,1408]{2,1,0:T(8,128)(2,1)S(1)}, u32[]{:S(2)}, u32[]{:S(2)}) collective-permute-start(bf16[2,80,1408]{2,1,0:T(8,128)(2,1)S(1)} %pad_maximum_fusion.41), channel_id=1, source_target_pairs={{0,24},{8,0},{16,8},{24,16},{1,25},{9,1},{17,9},{25,17},{2,26},{10... | collective-permute-start | bytes 1351688 | tf_op jit(solution)/shard_map/ppermute | solution.py:22
  801.9 17.3 %collective-permute-start.175 = (bf16[2,80,1408]{2,1,0:T(8,128)(2,1)S(1)}, bf16[2,80,1408]{2,1,0:T(8,128)(2,1)S(1)}, u32[]{:S(2)}, u32[]{:S(2)}) collective-permute-start(bf16[2,80,1408]{2,1,0:T(8,128)(2,1)S(1)} %pad_maximum_fusion.40), channel_id=1, source_target_pairs={{0,8},{8,16},{16,24},{24,0},{1,9},{9,17},{17,25},{25,1},{2,10},{10... | collective-permute-start | bytes 1351688 | tf_op jit(solution)/shard_map/ppermute | solution.py:22
  813.6 19.8 %collective-permute-start.172 = (bf16[4,80,1280]{2,1,0:T(8,128)(2,1)S(1)}, bf16[4,80,1280]{2,1,0:T(8,128)(2,1)S(1)}, u32[]{:S(2)}, u32[]{:S(2)}) collective-permute-start(bf16[4,80,1280]{2,1,0:T(8,128)(2,1)S(1)} %pad_maximum_fusion.23), channel_id=1, source_target_pairs={{0,6},{2,0},{4,2},{6,4},{1,7},{3,1},{5,3},{7,5},{8,14},{10,8},{12,... | collective-permute-start | bytes 2457608 | tf_op jit(solution)/shard_map/ppermute | solution.py:22
  813.8 20.3 %collective-permute-start.170 = (bf16[4,80,1280]{2,1,0:T(8,128)(2,1)S(1)}, bf16[4,80,1280]{2,1,0:T(8,128)(2,1)S(1)}, u32[]{:S(2)}, u32[]{:S(2)}) collective-permute-start(bf16[4,80,1280]{2,1,0:T(8,128)(2,1)S(1)} %pad_maximum_fusion.22), channel_id=1, source_target_pairs={{0,2},{2,4},{4,6},{6,0},{1,3},{3,5},{5,7},{7,1},{8,10},{10,12},{12... | collective-permute-start | bytes 2457608 | tf_op jit(solution)/shard_map/ppermute | solution.py:22
  819.1 33.0 %collective-permute-start.178 = (bf16[4,80,1408]{2,1,0:T(8,128)(2,1)S(1)}, bf16[4,80,1408]{2,1,0:T(8,128)(2,1)S(1)}, u32[]{:S(2)}, u32[]{:S(2)}) collective-permute-start(bf16[4,80,1408]{2,1,0:T(8,128)(2,1)S(1)} %pad_maximum_fusion.19), channel_id=1, source_target_pairs={{0,24},{8,0},{16,8},{24,16},{1,25},{9,1},{17,9},{25,17},{2,26},{10... | collective-permute-start | bytes 2703368 | tf_op jit(solution)/shard_map/ppermute | solution.py:22
  820.0 32.2 %collective-permute-start.176 = (bf16[4,80,1408]{2,1,0:T(8,128)(2,1)S(1)}, bf16[4,80,1408]{2,1,0:T(8,128)(2,1)S(1)}, u32[]{:S(2)}, u32[]{:S(2)}) collective-permute-start(bf16[4,80,1408]{2,1,0:T(8,128)(2,1)S(1)} %maximum_maximum_fusion), channel_id=1, source_target_pairs={{0,8},{8,16},{16,24},{24,0},{1,9},{9,17},{17,25},{25,1},{2,10},{10... | collective-permute-start | bytes 2703368 | tf_op jit(solution)/shard_map/ppermute | solution.py:22
  878.4 20.9 %collective-permute-start.186 = (bf16[2,128,320]{2,1,0:T(8,128)(2,1)S(1)}, bf16[2,128,320]{2,1,0:T(8,128)(2,1)S(1)}, u32[]{:S(2)}, u32[]{:S(2)}) collective-permute-start(bf16[2,128,320]{2,1,0:T(8,128)(2,1)S(1)} %pad_maximum_fusion.76), channel_id=1, source_target_pairs={{0,0},{2,8},{4,16},{6,24},{8,2},{10,10},{12,18},{14,26},{16,4},{18... | collective-permute-start | bytes 491528 | tf_op jit(solution)/shard_map/ppermute | solution.py:36
  881.6 16.7 %collective-permute-start.192 = (bf16[40,1280]{1,0:T(8,128)(2,1)S(1)}, bf16[40,1280]{1,0:T(8,128)(2,1)S(1)}, u32[]{:S(2)}, u32[]{:S(2)}) collective-permute-start(bf16[40,1280]{1,0:T(8,128)(2,1)S(1)} %select_convert_fusion.3), channel_id=1, source_target_pairs={{0,1},{1,0},{2,3},{3,2},{4,5},{5,4},{6,7},{7,6},{8,9},{9,8},{10,11... | collective-permute-start | bytes 307208 | tf_op jit(solution)/shard_map/ppermute | solution.py:22
  (347 other events, 5571.7 us)
Sparse Core Ops, SparseCore 0:
  12.6 134.6 all-gather.1
  729.3 127.1 reduce-scatter.1
